TPU v7x, 32 devices: a whole 2x2x4 slice. The times are simulated.
32 devices in a mesh: rows: 8 (over z, x), cols: 4 (over y, core).
Axes of the slice: x: 2, y: 2, z: 4, core: 2. Of those that a mesh axis runs over, the one named last changes fastest.
Arguments:
- features: bfloat16 [64, 128, 512], P('rows', 'cols'), may hold values from -6 to 6
- kernel: bfloat16 [4608, 512], replicated, may hold values from -0.09375 to 0.09375
- out_grad: bfloat16 [64, 128, 512], P('rows', 'cols'), may hold values from -6 to 6
- projector: bfloat16 [1024, 1024], P('rows', 'cols'), may hold values from -0.375 to 0.375
- mixers: bfloat16 [2, 128, 256], replicated, may hold values from -0.5 to 0.5
Outputs:
- output: bfloat16 [64, 128, 512], P('rows', 'cols')
- grad_features: bfloat16 [64, 128, 512], P('rows', 'cols')
- grad_kernel: float32 [9, 512, 512], P(None, 'rows', 'cols')
- sketch: bfloat16 [128, 4608], P('cols', 'rows')
All inputs are finite; a program needn't handle non-finite values.
Results may differ from a plain program's by a relative error of at most 0.015.
Values may be sent and summed in bfloat16 or wider, within the bound.
No kernel may reach another device: no remote copies, remote signals or barrier semaphores. Data moves between devices by JAX's collectives and lax.ppermute only.
A program may use at most 192 MiB of HBM per device.

v0:
```python
import functools
import jax
import jax.numpy as jnp
from jax import lax
from jax.experimental import pallas as pl
from jax.experimental.pallas import tpu as pltpu
from jax.sharding import PartitionSpec as P

NS_STEPS = 5
GROUP = 8
NT = (((1,), (1,)), ((), ()))
F32, BF16 = jnp.float32, jnp.bfloat16
VMEM = pl.BlockSpec(memory_space=pltpu.VMEM)
SMEM = pl.BlockSpec(memory_space=pltpu.SMEM)
ANY = pl.BlockSpec(memory_space=pl.ANY)


def mm(a, b):
    return jnp.dot(a, b, preferred_element_type=F32)


def spectral(grams):
    size = grams[0].shape[0]
    rows = lax.broadcasted_iota(jnp.int32, (size, size), 0)
    cols = lax.broadcasted_iota(jnp.int32, (size, size), 1)
    diagonal = rows == cols

    def total(x):
        return jnp.sum(jnp.sum(x, axis=1, keepdims=True), axis=0, keepdims=True)

    spreads = []
    for gram in grams:
        trace = total(jnp.where(diagonal, gram, 0.0))
        spread = gram / (trace + 1e-06) - jnp.where(diagonal, 1.0 / size, 0.0)
        spreads.append(spread / (jnp.sqrt(total(spread * spread)) + 1e-06))
    for sweep in range(NS_STEPS):
        low = [y.astype(BF16) for y in spreads]
        squares = [mm(y, y).astype(BF16) for y in low]
        spreads = [1.5 * s - 0.5 * mm(y, z) for s, y, z in zip(spreads, low, squares)]
    return spreads


def combiner(mix, spread):
    return (0.5 * (mix.astype(F32) + mm(mix, spread.astype(BF16)))).astype(BF16)


def gram_terms(parts):
    total = None
    for part in parts:
        term = lax.dot_general(part, part, NT, preferred_element_type=F32)
        total = term if total is None else total + term
    return total


def shifted(block, left, right):
    at = lax.broadcasted_iota(jnp.int32, block.shape, 0)
    wide = block.astype(F32)
    size = block.shape[0]
    low = jnp.where(at == 0, left, pltpu.roll(wide, 1, 0)).astype(BF16)
    high = jnp.where(at == size - 1, right, pltpu.roll(wide, size - 1, 0)).astype(BF16)
    return low, high


def rows_at(src, j, a):
    rows = src.shape[1]
    if a == 1:
        value = src[j]
    elif a == 0:
        value = jnp.concatenate([src[j - 1, rows - 1 : rows], src[j, : rows - 1]], axis=0)
    else:
        value = jnp.concatenate([src[j, 1:rows], src[j + 1, 0:1]], axis=0)
    return value.reshape(-1, src.shape[3])


def row_tree_kernel(step, mix_ref, proj_ref, halo_ref, band_ref, out_ref, raw, lo, hi, sk, sems):
    blocks, rows, cols, chans = raw.shape
    rank = proj_ref.shape[1]
    copies = [
        pltpu.make_async_copy(band_ref.at[j], raw.at[j], sems.at[j]) for j in range(blocks)
    ]
    for copy in copies:
        copy.start()

    def shift(j, h):
        k = j * rows + h
        lo[j, h], hi[j, h] = shifted(raw[j, h], halo_ref[0, k : k + 1], halo_ref[2, k : k + 1])

    copies[0].wait()
    shift(0, rows - 1)
    copies[1].wait()
    for h in range(rows):
        shift(1, h)
    for j in range(1, blocks - 1):
        copies[j + 1].wait()
        for h in range(rows if j + 1 < blocks - 1 else 1):
            shift(j + 1, h)
        half, part = divmod(j - 1, 2)
        for a in range(3):
            for b, src in enumerate((lo, raw, hi)):
                t = 3 * a + b
                sk[half, part * rank : (part + 1) * rank, t * chans : (t + 1) * chans] = mm(
                    proj_ref[j - 1], rows_at(src, j, a)
                ).astype(BF16)
    mix = mix_ref[...]
    count = (blocks - 2) // 2
    width = sk.shape[-1]
    starts = range(0, width, step)
    while count:
        spreads = spectral(
            [gram_terms(sk[i, :, s : s + step] for s in starts) for i in range(count)]
        )
        for i in range(count):
            mixed = combiner(mix, spreads[i])
            for s in starts:
                piece = mm(mixed, sk[i, :, s : s + step]).astype(BF16)
                if count == 1:
                    out_ref[:, s : s + step] = piece
                else:
                    sk[i // 2, (i % 2) * rank : (i % 2 + 1) * rank, s : s + step] = piece
        count //= 2


def row_tree(mix, proj, halo, band):
    blocks, rows, cols, chans = band.shape
    rank = mix.shape[0]
    width = 9 * chans
    return pl.pallas_call(
        functools.partial(row_tree_kernel, 1536),
        out_shape=jax.ShapeDtypeStruct((rank, width), BF16),
        in_specs=[VMEM, VMEM, VMEM, ANY],
        out_specs=VMEM,
        scratch_shapes=[
            pltpu.VMEM((blocks, rows, cols, chans), BF16),
            pltpu.VMEM((blocks, rows, cols, chans), BF16),
            pltpu.VMEM((blocks, rows, cols, chans), BF16),
            pltpu.VMEM(((blocks - 2) // 2, 2 * rank, width), BF16),
            pltpu.SemaphoreType.DMA((blocks,)),
        ],
        compiler_params=pltpu.CompilerParams(vmem_limit_bytes=48 << 20),
        cost_estimate=pl.CostEstimate(flops=2 * 10**10, bytes_accessed=8 << 20, transcendentals=0),
        name="row_tree",
    )(mix, proj, halo, band)


def merge_kernel(step, halves, share, where_ref, mix_ref, *refs):
    rank, width = refs[0].shape
    own = refs[0]
    others = refs[1 : 2 + halves]
    outs = refs[2 + halves :]
    half = width // 2
    core = where_ref[1]

    def spans():
        for s in range(0, width, step):
            if halves:
                which, inner = divmod(s, half)
                place = pl.multiple_of((core + which) % 2 * half + inner, 128)
                other = others[which][:, inner : inner + step]
            else:
                place, other = s, others[0][:, s : s + step]
            yield place, jnp.concatenate([own[:, pl.ds(place, step)], other], axis=0)

    spread = spectral([gram_terms(part for _, part in spans())])[0]
    if share:
        mix = mix_ref[pl.ds(pl.multiple_of(where_ref[2] * share, 16), share), :]
    else:
        mix = mix_ref[...]
    turned = jnp.concatenate([mix[:, rank:], mix[:, :rank]], axis=1)
    mix = jnp.where(where_ref[0] == 0, mix.astype(F32), turned.astype(F32)).astype(BF16)
    mixed = combiner(mix, spread)
    for place, part in spans():
        outs[0][:, pl.ds(place, step)] = mm(mixed, part).astype(BF16)
    if not share:
        outs[1][...] = outs[0][:, pl.ds(pl.multiple_of(core * half, 128), half)]


def merge(where, mix, own, others, share):
    rank, width = own.shape
    shapes = [jax.ShapeDtypeStruct((share or rank, width), BF16)]
    if not share:
        shapes.append(jax.ShapeDtypeStruct((rank, width // 2), BF16))
    return pl.pallas_call(
        functools.partial(merge_kernel, 1152, len(others) == 2, share),
        out_shape=shapes,
        in_specs=[SMEM] + [VMEM] * (2 + len(others)),
        out_specs=[VMEM] * len(shapes),
        compiler_params=pltpu.CompilerParams(vmem_limit_bytes=32 << 20),
        cost_estimate=pl.CostEstimate(flops=4 * 10**9, bytes_accessed=4 << 20, transcendentals=0),
        name="merge",
    )(where, mix, own, *others)


def conv_kernel(where_ref, kernel_ref, halo_ref, feat_ref, grad_ref, out_ref, back_ref, raw, lo, hi, total, sems):
    tap = pl.program_id(0)
    rows, cols, chans = raw.shape[2:]
    row = where_ref[0]
    arrays = (feat_ref, grad_ref)

    @pl.when(tap == 0)
    def start():
        copies = [
            pltpu.make_async_copy(ref.at[pl.ds(row, 3)], raw.at[n], sems.at[n])
            for n, ref in enumerate(arrays)
        ]
        for copy in copies:
            copy.start()
        for n, copy in enumerate(copies):
            copy.wait()
            base = pl.multiple_of(row * rows, rows)
            left = halo_ref[n, pl.ds(base, 3 * rows), :]
            right = halo_ref[2 + n, pl.ds(base, 3 * rows), :]
            for k in range(rows - 1, 2 * rows + 1):
                j, h = divmod(k, rows)
                lo[n, j, h], hi[n, j, h] = shifted(
                    raw[n, j, h], left[k : k + 1], right[k : k + 1]
                )
        total[...] = jnp.zeros_like(total)

    for a in range(3):
        for b in range(3):

            @pl.when(tap == 3 * a + b)
            def add(a=a, b=b):
                weights = kernel_ref[...]
                total[0] += mm(rows_at((lo, raw, hi)[b].at[0], 1, a), weights)
                total[1] += lax.dot_general(
                    rows_at((lo, raw, hi)[2 - b].at[1], 1, 2 - a), weights, NT, preferred_element_type=F32
                )

    @pl.when(tap == 8)
    def finish():
        out_ref[...] = total[0].astype(BF16)
        back_ref[...] = total[1].astype(BF16)


def convolutions(where, kernel, halo, feat_band, grad_band):
    rows, cols, chans = feat_band.shape[1:]
    block = jax.ShapeDtypeStruct((rows * cols, chans), BF16)
    scratch = pltpu.VMEM((2, 3, rows, cols, chans), BF16)
    whole = pl.BlockSpec((rows * cols, chans), lambda t: (0, 0))
    return pl.pallas_call(
        conv_kernel,
        grid=(9,),
        out_shape=[block, block],
        in_specs=[SMEM, pl.BlockSpec((chans, chans), lambda t: (t, 0)), VMEM, ANY, ANY],
        out_specs=[whole, whole],
        scratch_shapes=[
            scratch,
            scratch,
            scratch,
            pltpu.VMEM((2, rows * cols, chans), F32),
            pltpu.SemaphoreType.DMA((2,)),
        ],
        compiler_params=pltpu.CompilerParams(vmem_limit_bytes=32 << 20),
        cost_estimate=pl.CostEstimate(flops=5 * 10**9, bytes_accessed=8 << 20, transcendentals=0),
        name="convolutions",
    )(where, kernel, halo, feat_band, grad_band)


def ring_row(place, count):
    return jnp.where(place < count // 2, 2 * place, 2 * (count - 1 - place) + 1)


def ring_place(row, count):
    return jnp.where(row % 2 == 0, row // 2, count - 1 - row // 2)


def body(features, kernel, out_grad, projector, mixers):
    rows, cols, chans = features.shape
    row_count, col_count = lax.axis_size("rows"), lax.axis_size("cols")
    row, col = lax.axis_index("rows"), lax.axis_index("cols")
    rank = projector.shape[0]
    core = col % 2

    order = list(range(0, row_count, 2)) + list(range(row_count - 1, 0, -2))
    ahead = [(order[i], order[(i + 1) % row_count]) for i in range(row_count)]
    behind = [(j, i) for i, j in ahead]
    east = [(i, i + 1) for i in range(col_count - 1)]
    west = [(j, i) for i, j in east]

    first = jnp.stack([features[:, 0], out_grad[:, 0]])
    last = jnp.stack([features[:, cols - 1], out_grad[:, cols - 1]])
    halo = jnp.concatenate(
        [lax.ppermute(last, "cols", east), lax.ppermute(first, "cols", west)], axis=0
    )

    place = ring_place(row, row_count)
    feat_band = jnp.zeros((row_count + 2, rows, cols, chans), BF16)
    grad_band = jnp.zeros((row_count + 2, rows, cols, chans), BF16)
    halo_band = jnp.zeros((4, (row_count + 2) * rows, chans), F32)
    proj_band = jnp.zeros((row_count,) + projector.shape, BF16)

    def put_map(band, value, at, offset=0):
        return lax.dynamic_update_slice(band, value[None], (at + 1, offset, 0, 0))

    def put_halo(band, value, at):
        return lax.dynamic_update_slice(band, value.astype(F32), (0, (at + 1) * rows, 0))

    def put_proj(band, value, at):
        return lax.dynamic_update_slice(band, value[None], (at, 0, 0))

    feat_band = put_map(feat_band, features, row)
    grad_band = put_map(grad_band, out_grad, row)
    halo_band = put_halo(halo_band, halo, row)
    proj_band = put_proj(proj_band, projector, row)
    up = [features, projector, halo, out_grad]
    down = list(up)
    for step in range(1, row_count // 2):
        up = [lax.ppermute(x, "rows", ahead) for x in up]
        down = [lax.ppermute(x, "rows", behind) for x in down]
        for got, at in ((up, (place - step) % row_count), (down, (place + step) % row_count)):
            at = ring_row(at, row_count)
            feat_band = put_map(feat_band, got[0], at)
            proj_band = put_proj(proj_band, got[1], at)
            halo_band = put_halo(halo_band, got[2], at)
            grad_band = put_map(grad_band, got[3], at)
    at = ring_row((place + row_count // 2) % row_count, row_count)
    mid = rows // 2
    feat_band = put_map(feat_band, lax.ppermute(up[0][:mid], "rows", ahead), at)
    feat_band = put_map(feat_band, lax.ppermute(down[0][mid:], "rows", behind), at, mid)
    proj_band = put_proj(proj_band, lax.ppermute(up[1], "rows", ahead), at)
    halo_band = put_halo(halo_band, lax.ppermute(down[2], "rows", behind), at)
    grad_band = put_map(grad_band, lax.ppermute(up[3][:mid], "rows", ahead), at)
    grad_band = put_map(grad_band, lax.ppermute(down[3][mid:], "rows", behind), at, mid)

    where_rows = jnp.stack([row]).astype(jnp.int32)
    output, grad_features = convolutions(where_rows, kernel, halo_band, feat_band, grad_band)

    share = chans // row_count
    sliced = lax.dynamic_slice_in_dim(feat_band, row * share, share, axis=3)
    sliced = sliced.reshape((row_count + 2) * rows, cols, share)
    ends = lax.dynamic_slice_in_dim(halo_band, row * share, share, axis=2).astype(BF16)
    padded = jnp.concatenate([ends[0][:, None], sliced, ends[2][:, None]], axis=1)
    height = row_count * rows
    patches = jnp.concatenate(
        [
            padded[rows - 1 + a : rows - 1 + a + height, b : b + cols]
            for a in range(3)
            for b in range(3)
        ],
        axis=2,
    ).reshape(height * cols, 9 * share)
    flat_grad = grad_band[1 : row_count + 1].reshape(height * cols, chans)
    terms = lax.dot_general(
        patches, flat_grad, (((0,), (0,)), ((), ())), preferred_element_type=F32
    ).reshape(9, share, col_count, chans // col_count)
    for level in range(col_count.bit_length() - 1):
        bit = col >> level & 1
        pairs = terms.reshape(9, share, -1, 2, chans // col_count)
        keep = lax.dynamic_index_in_dim(pairs, bit, 3, keepdims=False)
        give = lax.dynamic_index_in_dim(pairs, 1 - bit, 3, keepdims=False).astype(BF16)
        perm = [(i, i ^ 1 << level) for i in range(col_count)]
        terms = keep + lax.ppermute(give, "cols", perm).astype(F32)
    grad_kernel = terms.reshape(9, share, chans // col_count)

    groups = []
    for start in range(0, row_count, GROUP):
        groups.append(
            row_tree(
                mixers[0],
                proj_band[start : start + GROUP],
                halo_band[:, start * rows : (start + GROUP + 2) * rows],
                feat_band[start : start + GROUP + 2],
            )
        )
    zero = jnp.zeros((), jnp.int32)
    while len(groups) > 1:
        where = jnp.stack([zero, core, col]).astype(jnp.int32)
        groups = [
            merge(where, mixers[0], groups[i], [groups[i + 1]], 0)[0]
            for i in range(0, len(groups), 2)
        ]
    sketch = groups[0]
    sibling = [(i, i ^ 1) for i in range(col_count)]
    levels = col_count.bit_length() - 1
    for level in range(levels):
        perm = [(i, i ^ 1 << level) for i in range(col_count)]
        where = jnp.stack([col >> level & 1, core, col]).astype(jnp.int32)
        if level:
            mine = lax.ppermute(half, "cols", perm)
            others = [mine, lax.ppermute(mine, "cols", sibling)]
        else:
            others = [lax.ppermute(sketch, "cols", perm)]
        last = level == levels - 1
        result = merge(where, mixers[1], sketch, others, rank // col_count if last else 0)
        if last:
            sketch = result[0]
        else:
            sketch, half = result
    patch_share = sketch.shape[1] // row_count
    own_block = lax.dynamic_slice_in_dim(sketch, row * patch_share, patch_share, axis=1)
    return (
        output.reshape(features.shape),
        grad_features.reshape(features.shape),
        grad_kernel,
        own_block,
    )


def solution(mesh):
    in_specs = (P("rows", "cols", None), P(), P("rows", "cols", None), P("rows", "cols"), P())
    out_specs = (
        P("rows", "cols", None),
        P("rows", "cols", None),
        P(None, "rows", "cols"),
        P("cols", "rows"),
    )
    return jax.shard_map(body, mesh=mesh, in_specs=in_specs, out_specs=out_specs, check_vma=False)
```

profile of v0, /device:TPU:0, one launch (start us, length us, event | category | flops | bytes accessed | tf_op | source)
XLA Modules:
  0.0 190.5 jit_solution(1701649825787634382)
XLA Ops:
  0.6 3.0 %collective-permute-start.28 = (bf16[128,256]{1,0:T(8,128)(2,1)}, bf16[128,256]{1,0:T(8,128)(2,1)S(1)}, u32[]{:S(2)}, u32[]{:S(2)}) collective-permute-start(bf16[128,256]{1,0:T(8,128)(2,1)} %param.8), channel_id=1, source_target_pairs={{8,0},{16,8},{24,16},{28,24},{20,28},{12,20},{4,12},{0,4},{9,1},{1... | collective-permute-start | bytes 196616 | tf_op jit(solution)/shard_map/ppermute | solution.py:310
  15.9 3.9 %collective-permute-done.1 = bf16[2,8,512]{2,1,0:T(8,128)(2,1)S(1)} collective-permute-done((bf16[2,8,512]{2,1,0:T(8,128)(2,1)S(1)}, bf16[2,8,512]{2,1,0:T(8,128)(2,1)S(1)}, u32[]{:S(2)}, u32[]{:S(2)}) %collective-permute-start.1) | collective-permute-done | bytes 16416 | tf_op jit(solution)/shard_map/ppermute | solution.py:284
  21.4 2.2 %collective-permute-done.2 = bf16[4,8,512]{2,1,0:T(8,128)(2,1)S(1)} collective-permute-done((bf16[4,8,512]{2,1,0:T(8,128)(2,1)S(1)}, bf16[4,8,512]{2,1,0:T(8,128)(2,1)S(1)}, u32[]{:S(2)}, u32[]{:S(2)}) %collective-permute-start.2) | collective-permute-done | bytes 32800 | tf_op jit(solution)/shard_map/ppermute | solution.py:309
  25.2 2.4 %collective-permute-done.3 = bf16[4,8,512]{2,1,0:T(8,128)(2,1)S(1)} collective-permute-done((bf16[4,8,512]{2,1,0:T(8,128)(2,1)S(1)}, bf16[4,8,512]{2,1,0:T(8,128)(2,1)S(1)}, u32[]{:S(2)}, u32[]{:S(2)}) %collective-permute-start.3) | collective-permute-done | bytes 32800 | tf_op jit(solution)/shard_map/ppermute | solution.py:310
  33.4 4.9 %collective-permute-done.4 = bf16[4,8,512]{2,1,0:T(8,128)(2,1)S(1)} collective-permute-done((bf16[4,8,512]{2,1,0:T(8,128)(2,1)S(1)}, bf16[4,8,512]{2,1,0:T(8,128)(2,1)S(1)}, u32[]{:S(2)}, u32[]{:S(2)}) %collective-permute-start.4) | collective-permute-done | bytes 32800 | tf_op jit(solution)/shard_map/ppermute | solution.py:309
  39.8 2.3 %collective-permute-done.5 = bf16[4,8,512]{2,1,0:T(8,128)(2,1)S(1)} collective-permute-done((bf16[4,8,512]{2,1,0:T(8,128)(2,1)S(1)}, bf16[4,8,512]{2,1,0:T(8,128)(2,1)S(1)}, u32[]{:S(2)}, u32[]{:S(2)}) %collective-permute-start.5) | collective-permute-done | bytes 32800 | tf_op jit(solution)/shard_map/ppermute | solution.py:310
  42.6 3.4 %collective-permute-done.6 = bf16[4,8,512]{2,1,0:T(8,128)(2,1)S(1)} collective-permute-done((bf16[4,8,512]{2,1,0:T(8,128)(2,1)S(1)}, bf16[4,8,512]{2,1,0:T(8,128)(2,1)S(1)}, u32[]{:S(2)}, u32[]{:S(2)}) %collective-permute-start.6) | collective-permute-done | bytes 32800 | tf_op jit(solution)/shard_map/ppermute | solution.py:309
  47.6 2.3 %collective-permute-done.7 = bf16[4,8,512]{2,1,0:T(8,128)(2,1)S(1)} collective-permute-done((bf16[4,8,512]{2,1,0:T(8,128)(2,1)S(1)}, bf16[4,8,512]{2,1,0:T(8,128)(2,1)S(1)}, u32[]{:S(2)}, u32[]{:S(2)}) %collective-permute-start.7) | collective-permute-done | bytes 32800 | tf_op jit(solution)/shard_map/ppermute | solution.py:310
  50.5 4.0 %collective-permute-done.29 = bf16[128,256]{1,0:T(8,128)(2,1)S(1)} collective-permute-done((bf16[128,256]{1,0:T(8,128)(2,1)}, bf16[128,256]{1,0:T(8,128)(2,1)S(1)}, u32[]{:S(2)}, u32[]{:S(2)}) %collective-permute-start.29) | collective-permute-done | bytes 65568 | tf_op jit(solution)/shard_map/ppermute | solution.py:309
  56.6 2.1 %collective-permute-done.30 = bf16[128,256]{1,0:T(8,128)(2,1)S(1)} collective-permute-done((bf16[128,256]{1,0:T(8,128)(2,1)S(1)}, bf16[128,256]{1,0:T(8,128)(2,1)S(1)}, u32[]{:S(2)}, u32[]{:S(2)}) %collective-permute-start.30) | collective-permute-done | bytes 65568 | tf_op jit(solution)/shard_map/ppermute | solution.py:310
  63.3 4.0 %collective-permute-done.31 = bf16[128,256]{1,0:T(8,128)(2,1)S(1)} collective-permute-done((bf16[128,256]{1,0:T(8,128)(2,1)S(1)}, bf16[128,256]{1,0:T(8,128)(2,1)S(1)}, u32[]{:S(2)}, u32[]{:S(2)}) %collective-permute-start.31) | collective-permute-done | bytes 65568 | tf_op jit(solution)/shard_map/ppermute | solution.py:309
  69.5 2.1 %collective-permute-done.32 = bf16[128,256]{1,0:T(8,128)(2,1)S(1)} collective-permute-done((bf16[128,256]{1,0:T(8,128)(2,1)S(1)}, bf16[128,256]{1,0:T(8,128)(2,1)S(1)}, u32[]{:S(2)}, u32[]{:S(2)}) %collective-permute-start.32) | collective-permute-done | bytes 65568 | tf_op jit(solution)/shard_map/ppermute | solution.py:310
  98.0 23.4 %row_tree.1.refs_0_ = bf16[128,4608]{1,0:T(8,128)(2,1)} custom-call(bf16[128,256]{1,0:T(8,128)(2,1)S(1)} %get-tuple-element.27.mix_ref, bf16[8,128,256]{2,1,0:T(8,128)(2,1)} %bitcast_dynamic-update-slice_fusion.18.proj_ref, f32[4,80,512]{2,1,0:T(8,128)S(1)} %convert_dynamic-update-slice_fusion.halo_ref, ...), custom_call_target="tpu_custom_call" | custom-call | flops 20000000000 | bytes 8388608 | tf_op jit(solution)/shard_map/row_tree/pallas_call | solution.py:127
  123.1 4.0 %copy.16 = bf16[512,2048]{1,0:T(8,128)(2,1)} copy(bf16[512,2048]{0,1:T(8,128)(2,1)} %bitcast.107) | data formatting | bytes 4194304 | tf_op jit(solution)/shard_map/dot_general | solution.py:344
  130.4 3.4 %pad_maximum_fusion = (bf16[64,32,64]{2,1,0:T(8,128)(2,1)}, bf16[64,32,64]{2,1,0:T(8,128)(2,1)}, bf16[64,32,64]{2,1,0:T(8,128)(2,1)}, bf16[64,32,64]{2,1,0:T(8,1...) fusion(bf16[80,1,64]{2,1,0:T(2,128)(2,1)S(1)} %copy.14, ...), kind=kLoop, calls=%fused_computation.14 | loop fusion | flops 3145728 | bytes 3883008 | tf_op jit(solution)/shard_map/concatenate | solution.py:333
  133.8 6.8 %concatenate.48 = bf16[2048,576]{1,0:T(8,128)(2,1)} concatenate(bf16[2048,64]{1,0:T(8,128)(2,1)} %bitcast.113, bf16[2048,64]{1,0:T(8,128)(2,1)} %bitcast.116, bf16[2048,64]{1,0:T(8,128)(2,1)} %bitcast.110, bf16[2048,64]{1,0:T(8,128)(2,1)} %bitcast.112, bf16[2048,64]{1,0:T(8,128)(2,1)} %bitcast.117, bf16[2048,64]{1,0:T(8,128)(2,1)} %bitcast.111, bf16[2048,64]{1,0:T(8,128)(2,1)} %bitcast.114, ...), dimensions={1} | concatenate | bytes 4718592 | tf_op jit(solution)/shard_map/concatenate | solution.py:335
  140.6 4.4 %copy.15 = bf16[576,2048]{1,0:T(8,128)(2,1)} copy(bf16[576,2048]{0,1:T(8,128)(2,1)} %bitcast.105) | data formatting | bytes 4718592 | tf_op jit(solution)/shard_map/dot_general | solution.py:344
  145.0 3.7 %fusion.7 = f32[9,64,2,2,128]{4,1,3,2,0:T(8,128)S(1)} fusion(bf16[9,64,2048,1,1]{2,1,4,3,0:T(8,128)(2,1)} %bitcast.108, bf16[2,2,128,2048,1]{3,2,1,0,4:T(8,128)(2,1)} %bitcast.118), kind=kOutput, calls=%fused_computation.73 | convolution fusion | flops 1207959552 | bytes 5636096 | tf_op jit(solution)/shard_map/dot_general | solution.py:344
  150.0 7.0 %merge.2 = (bf16[128,4608]{1,0:T(8,128)(2,1)S(1)}, bf16[128,2304]{1,0:T(8,128)(2,1)}) custom-call(s32[3]{0:T(128)S(1)} %add_add_fusion.1.where_ref, bf16[128,256]{1,0:T(8,128)(2,1)S(1)} %get-tuple-element.28.mix_ref, bf16[128,4608]{1,0:T(8,128)(2,1)} %row_tree.1.refs_0_, bf16[128,4608]{1,0:T(8,128)(2,1)} %collective-permute-done.34.refs_1_), custom_call_target="tpu_custom_call" | custom-call | flops 4000000000 | bytes 4194304 | tf_op jit(solution)/shard_map/merge/pallas_call | solution.py:182
  159.5 2.1 %collective-permute-start.26 = (bf16[9,64,1,128]{3,1,2,0:T(8,128)(2,1)S(1)}, bf16[9,64,1,128]{3,1,2,0:T(8,128)(2,1)S(1)}, u32[]{:S(2)}, u32[]{:S(2)}) collective-permute-start(bf16[9,64,1,128]{3,1,2,0:T(8,128)(2,1)S(1)} %dynamic-slice_convert_fusion.1), channel_id=1, source_target_pairs={{0,2},{1,3},{2,0},{3,1},{4,6},{5,7},{6,4},{7,5},{8,10},{9,11},{10,... | collective-permute-start | bytes 442376 | tf_op jit(solution)/shard_map/ppermute | solution.py:353
  161.6 13.0 %collective-permute-done.35.refs_1_ = bf16[128,2304]{1,0:T(8,128)(2,1)} collective-permute-done((bf16[128,2304]{1,0:T(8,128)(2,1)}, bf16[128,2304]{1,0:T(8,128)(2,1)}, u32[]{:S(2)}, u32[]{:S(2)}) %collective-permute-start.35) | collective-permute-done | bytes 589856 | tf_op jit(solution)/shard_map/ppermute | solution.py:380
  174.6 2.3 %copy-done = bf16[4608,512]{1,0:T(8,128)(2,1)S(1)} copy-done((bf16[4608,512]{1,0:T(8,128)(2,1)S(1)}, bf16[4608,512]{1,0:T(8,128)(2,1)}, u32[]{:S(2)}) %copy-start) | copy-done | bytes 4718616
  176.9 6.6 %convolutions.1 = (bf16[256,512]{1,0:T(8,128)(2,1)}, bf16[256,512]{1,0:T(8,128)(2,1)}) custom-call(s32[1]{0:T(128)} %bitcast.where_ref, bf16[4608,512]{1,0:T(8,128)(2,1)S(1)} %copy-done, f32[4,80,512]{2,1,0:T(8,128)S(1)} %convert_dynamic-update-slice_fusion.halo_ref, bf16[10,8,32,512]{3,2,1,0:T(8,128)(2,1)} %bitcast_dynamic-update-slice_fusion.16.feat_ref.band_ref, ...), custom_call_target="tpu_custom_call" | custom-call | flops 5000000000 | bytes 8388608 | tf_op jit(solution)/shard_map/convolutions/pallas_call | solution.py:241
  184.3 5.5 %merge.3 = bf16[32,4608]{1,0:T(8,128)(2,1)S(1)} custom-call(s32[3]{0:T(128)S(1)} %add_add_fusion.where_ref, bf16[128,256]{1,0:T(8,128)(2,1)S(1)} %get-tuple-element.28.mix_ref, bf16[128,4608]{1,0:T(8,128)(2,1)S(1)} %copy-done.2, bf16[128,2304]{1,0:T(8,128)(2,1)} %collective-permute-done.35.refs_1_, bf16[128,2304]{1,0:T(8,128)(2,1)S(1)} %collective-permute-done.36.refs_2_), custom_call_target="tpu_custom_call" | custom-call | flops 4000000000 | bytes 4194304 | tf_op jit(solution)/shard_map/merge/pallas_call | solution.py:182
  (138 shorter events, 70.5 us)
Async XLA Ops:
  0.6 30.5 %collective-permute-start.28 = (bf16[128,256]{1,0:T(8,128)(2,1)}, bf16[128,256]{1,0:T(8,128)(2,1)S(1)}, u32[]{:S(2)}, u32[]{:S(2)}) collective-permute-start(bf16[128,256]{1,0:T(8,128)(2,1)} %param.8), channel_id=1, source_target_pairs={{8,0},{16,8},{24,16},{28,24},{20,28},{12,20},{4,12},{0,4},{9,1},{1... | collective-permute-start | bytes 196616 | tf_op jit(solution)/shard_map/ppermute | solution.py:310
  3.6 25.5 %collective-permute-start.27 = (bf16[128,256]{1,0:T(8,128)(2,1)}, bf16[128,256]{1,0:T(8,128)(2,1)}, u32[]{:S(2)}, u32[]{:S(2)}) collective-permute-start(bf16[128,256]{1,0:T(8,128)(2,1)} %param.8), channel_id=1, source_target_pairs={{0,8},{8,16},{16,24},{24,28},{28,20},{20,12},{12,4},{4,0},{1,9},{9... | collective-permute-start | bytes 196616 | tf_op jit(solution)/shard_map/ppermute | solution.py:309
  3.8 69.7 %collective-permute-start.10 = (bf16[8,32,512]{2,1,0:T(8,128)(2,1)}, bf16[8,32,512]{2,1,0:T(8,128)(2,1)}, u32[]{:S(2)}, u32[]{:S(2)}) collective-permute-start(bf16[8,32,512]{2,1,0:T(8,128)(2,1)} %param.5), channel_id=1, source_target_pairs={{8,0},{16,8},{24,16},{28,24},{20,28},{12,20},{4,12},{0,4},{9,1},{1... | collective-permute-start | bytes 786440 | tf_op jit(solution)/shard_map/ppermute | solution.py:310
  5.7 68.6 %collective-permute-start.9 = (bf16[8,32,512]{2,1,0:T(8,128)(2,1)}, bf16[8,32,512]{2,1,0:T(8,128)(2,1)}, u32[]{:S(2)}, u32[]{:S(2)}) collective-permute-start(bf16[8,32,512]{2,1,0:T(8,128)(2,1)} %param.5), channel_id=1, source_target_pairs={{0,8},{8,16},{16,24},{24,28},{28,20},{20,12},{12,4},{4,0},{1,9},{9... | collective-permute-start | bytes 786440 | tf_op jit(solution)/shard_map/ppermute | solution.py:309
  7.7 6.9 %collective-permute-start = (bf16[2,8,512]{2,1,0:T(8,128)(2,1)S(1)}, bf16[2,8,512]{2,1,0:T(8,128)(2,1)S(1)}, u32[]{:S(2)}, u32[]{:S(2)}) collective-permute-start(bf16[2,8,512]{2,1,0:T(8,128)(2,1)S(1)} %pad_maximum_fusion.2), channel_id=1, source_target_pairs={{0,1},{1,2},{2,3},{4,5},{5,6},{6,7},{8,9},{9,10},{10,11},{12,13},{... | collective-permute-start | bytes 49160 | tf_op jit(solution)/shard_map/ppermute | solution.py:284
  27.6 47.9 %collective-permute-start.18 = (bf16[8,32,512]{2,1,0:T(8,128)(2,1)}, bf16[8,32,512]{2,1,0:T(8,128)(2,1)S(1)}, u32[]{:S(2)}, u32[]{:S(2)}) collective-permute-start(bf16[8,32,512]{2,1,0:T(8,128)(2,1)} %param.7), channel_id=1, source_target_pairs={{8,0},{16,8},{24,16},{28,24},{20,28},{12,20},{4,12},{0,4},{9,1},{1... | collective-permute-start | bytes 786440 | tf_op jit(solution)/shard_map/ppermute | solution.py:310
  29.1 47.1 %collective-permute-start.17 = (bf16[8,32,512]{2,1,0:T(8,128)(2,1)}, bf16[8,32,512]{2,1,0:T(8,128)(2,1)S(1)}, u32[]{:S(2)}, u32[]{:S(2)}) collective-permute-start(bf16[8,32,512]{2,1,0:T(8,128)(2,1)} %param.7), channel_id=1, source_target_pairs={{0,8},{8,16},{16,24},{24,28},{28,20},{20,12},{12,4},{4,0},{1,9},{9... | collective-permute-start | bytes 786440 | tf_op jit(solution)/shard_map/ppermute | solution.py:309
  31.2 7.0 %collective-permute-start.4 = (bf16[4,8,512]{2,1,0:T(8,128)(2,1)S(1)}, bf16[4,8,512]{2,1,0:T(8,128)(2,1)S(1)}, u32[]{:S(2)}, u32[]{:S(2)}) collective-permute-start(bf16[4,8,512]{2,1,0:T(8,128)(2,1)S(1)} %collective-permute-done.2), channel_id=1, source_target_pairs={{0,8},{8,16},{16,24},{24,28},{28,20},{20,12},{12,4},{4,0},{1,9},{9... | collective-permute-start | bytes 98312 | tf_op jit(solution)/shard_map/ppermute | solution.py:309
  71.6 9.3 %collective-permute-start.33 = (bf16[128,256]{1,0:T(8,128)(2,1)S(1)}, bf16[128,256]{1,0:T(8,128)(2,1)S(1)}, u32[]{:S(2)}, u32[]{:S(2)}) collective-permute-start(bf16[128,256]{1,0:T(8,128)(2,1)S(1)} %collective-permute-done.31), channel_id=1, source_target_pairs={{0,8},{8,16},{16,24},{24,28},{28,20},{20,12},{12,4},{4,0},{1,9},{9... | collective-permute-start | bytes 196616 | tf_op jit(solution)/shard_map/ppermute | solution.py:321
  73.5 9.5 %collective-permute-start.12 = (bf16[8,32,512]{2,1,0:T(8,128)(2,1)}, bf16[8,32,512]{2,1,0:T(8,128)(2,1)S(1)}, u32[]{:S(2)}, u32[]{:S(2)}) collective-permute-start(bf16[8,32,512]{2,1,0:T(8,128)(2,1)} %collective-permute-done.10), channel_id=1, source_target_pairs={{8,0},{16,8},{24,16},{28,24},{20,28},{12,20},{4,12},{0,4},{9,1},{1... | collective-permute-start | bytes 786440 | tf_op jit(solution)/shard_map/ppermute | solution.py:310
  74.2 9.5 %collective-permute-start.11 = (bf16[8,32,512]{2,1,0:T(8,128)(2,1)}, bf16[8,32,512]{2,1,0:T(8,128)(2,1)S(1)}, u32[]{:S(2)}, u32[]{:S(2)}) collective-permute-start(bf16[8,32,512]{2,1,0:T(8,128)(2,1)} %collective-permute-done.9), channel_id=1, source_target_pairs={{0,8},{8,16},{16,24},{24,28},{28,20},{20,12},{12,4},{4,0},{1,9},{9... | collective-permute-start | bytes 786440 | tf_op jit(solution)/shard_map/ppermute | solution.py:309
  75.5 10.6 %collective-permute-start.20 = (bf16[8,32,512]{2,1,0:T(8,128)(2,1)S(1)}, bf16[8,32,512]{2,1,0:T(8,128)(2,1)S(1)}, u32[]{:S(2)}, u32[]{:S(2)}) collective-permute-start(bf16[8,32,512]{2,1,0:T(8,128)(2,1)S(1)} %collective-permute-done.18), channel_id=1, source_target_pairs={{8,0},{16,8},{24,16},{28,24},{20,28},{12,20},{4,12},{0,4},{9,1},{1... | collective-permute-start | bytes 786440 | tf_op jit(solution)/shard_map/ppermute | solution.py:310
  76.3 11.8 %collective-permute-start.19 = (bf16[8,32,512]{2,1,0:T(8,128)(2,1)S(1)}, bf16[8,32,512]{2,1,0:T(8,128)(2,1)S(1)}, u32[]{:S(2)}, u32[]{:S(2)}) collective-permute-start(bf16[8,32,512]{2,1,0:T(8,128)(2,1)S(1)} %collective-permute-done.17), channel_id=1, source_target_pairs={{0,8},{8,16},{16,24},{24,28},{28,20},{20,12},{12,4},{4,0},{1,9},{9... | collective-permute-start | bytes 786440 | tf_op jit(solution)/shard_map/ppermute | solution.py:309
  82.9 7.2 %collective-permute-start.14 = (bf16[8,32,512]{2,1,0:T(8,128)(2,1)S(1)}, bf16[8,32,512]{2,1,0:T(8,128)(2,1)S(1)}, u32[]{:S(2)}, u32[]{:S(2)}) collective-permute-start(bf16[8,32,512]{2,1,0:T(8,128)(2,1)S(1)} %collective-permute-done.12), channel_id=1, source_target_pairs={{8,0},{16,8},{24,16},{28,24},{20,28},{12,20},{4,12},{0,4},{9,1},{1... | collective-permute-start | bytes 786440 | tf_op jit(solution)/shard_map/ppermute | solution.py:310
  83.7 8.0 %collective-permute-start.13 = (bf16[8,32,512]{2,1,0:T(8,128)(2,1)S(1)}, bf16[8,32,512]{2,1,0:T(8,128)(2,1)S(1)}, u32[]{:S(2)}, u32[]{:S(2)}) collective-permute-start(bf16[8,32,512]{2,1,0:T(8,128)(2,1)S(1)} %collective-permute-done.11), channel_id=1, source_target_pairs={{0,8},{8,16},{16,24},{24,28},{28,20},{20,12},{12,4},{4,0},{1,9},{9... | collective-permute-start | bytes 786440 | tf_op jit(solution)/shard_map/ppermute | solution.py:309
  86.1 6.4 %collective-permute-start.22 = (bf16[8,32,512]{2,1,0:T(8,128)(2,1)S(1)}, bf16[8,32,512]{2,1,0:T(8,128)(2,1)S(1)}, u32[]{:S(2)}, u32[]{:S(2)}) collective-permute-start(bf16[8,32,512]{2,1,0:T(8,128)(2,1)S(1)} %collective-permute-done.20), channel_id=1, source_target_pairs={{8,0},{16,8},{24,16},{28,24},{20,28},{12,20},{4,12},{0,4},{9,1},{1... | collective-permute-start | bytes 786440 | tf_op jit(solution)/shard_map/ppermute | solution.py:310
  90.1 7.2 %collective-permute-start.16 = (bf16[4,32,512]{2,1,0:T(8,128)(2,1)S(1)}, bf16[4,32,512]{2,1,0:T(8,128)(2,1)S(1)}, u32[]{:S(2)}, u32[]{:S(2)}) collective-permute-start(bf16[4,32,512]{2,1,0:T(8,128)(2,1)S(1)} %slice.97), channel_id=1, source_target_pairs={{8,0},{16,8},{24,16},{28,24},{20,28},{12,20},{4,12},{0,4},{9,1},{1... | collective-permute-start | bytes 393224 | tf_op jit(solution)/shard_map/ppermute | solution.py:320
  92.5 29.0 %collective-permute-start.24 = (bf16[4,32,512]{2,1,0:T(8,128)(2,1)S(1)}, bf16[4,32,512]{2,1,0:T(8,128)(2,1)S(1)}, u32[]{:S(2)}, u32[]{:S(2)}) collective-permute-start(bf16[4,32,512]{2,1,0:T(8,128)(2,1)S(1)} %slice.99), channel_id=1, source_target_pairs={{8,0},{16,8},{24,16},{28,24},{20,28},{12,20},{4,12},{0,4},{9,1},{1... | collective-permute-start | bytes 393224 | tf_op jit(solution)/shard_map/ppermute | solution.py:324
  94.4 27.1 %collective-permute-start.23 = (bf16[4,32,512]{2,1,0:T(8,128)(2,1)S(1)}, bf16[4,32,512]{2,1,0:T(8,128)(2,1)S(1)}, u32[]{:S(2)}, u32[]{:S(2)}) collective-permute-start(bf16[4,32,512]{2,1,0:T(8,128)(2,1)S(1)} %slice.98), channel_id=1, source_target_pairs={{0,8},{8,16},{16,24},{24,28},{28,20},{20,12},{12,4},{4,0},{1,9},{9... | collective-permute-start | bytes 393224 | tf_op jit(solution)/shard_map/ppermute | solution.py:323
  121.4 28.6 %collective-permute-start.34 = (bf16[128,4608]{1,0:T(8,128)(2,1)}, bf16[128,4608]{1,0:T(8,128)(2,1)}, u32[]{:S(2)}, u32[]{:S(2)}) collective-permute-start(bf16[128,4608]{1,0:T(8,128)(2,1)} %row_tree.1.refs_0_), channel_id=1, source_target_pairs={{0,1},{1,0},{2,3},{3,2},{4,5},{5,4},{6,7},{7,6},{8,9},{9,8},{10,11... | collective-permute-start | bytes 3538952 | tf_op jit(solution)/shard_map/ppermute | solution.py:383
  149.5 8.6 %collective-permute-start.25 = (bf16[9,64,2,128]{3,1,2,0:T(8,128)(2,1)}, bf16[9,64,2,128]{3,1,2,0:T(8,128)(2,1)}, u32[]{:S(2)}, u32[]{:S(2)}) collective-permute-start(bf16[9,64,2,128]{3,1,2,0:T(8,128)(2,1)} %fusion.4), channel_id=1, source_target_pairs={{0,1},{1,0},{2,3},{3,2},{4,5},{5,4},{6,7},{7,6},{8,9},{9,8},{10,11... | collective-permute-start | bytes 884744 | tf_op jit(solution)/shard_map/ppermute | solution.py:353
  158.1 16.5 %collective-permute-start.35 = (bf16[128,2304]{1,0:T(8,128)(2,1)}, bf16[128,2304]{1,0:T(8,128)(2,1)}, u32[]{:S(2)}, u32[]{:S(2)}) collective-permute-start(bf16[128,2304]{1,0:T(8,128)(2,1)} %get-tuple-element.11), channel_id=1, source_target_pairs={{0,2},{1,3},{2,0},{3,1},{4,6},{5,7},{6,4},{7,5},{8,10},{9,11},{10,... | collective-permute-start | bytes 1769480 | tf_op jit(solution)/shard_map/ppermute | solution.py:380
  159.5 24.1 %collective-permute-start.26 = (bf16[9,64,1,128]{3,1,2,0:T(8,128)(2,1)S(1)}, bf16[9,64,1,128]{3,1,2,0:T(8,128)(2,1)S(1)}, u32[]{:S(2)}, u32[]{:S(2)}) collective-permute-start(bf16[9,64,1,128]{3,1,2,0:T(8,128)(2,1)S(1)} %dynamic-slice_convert_fusion.1), channel_id=1, source_target_pairs={{0,2},{1,3},{2,0},{3,1},{4,6},{5,7},{6,4},{7,5},{8,10},{9,11},{10,... | collective-permute-start | bytes 442376 | tf_op jit(solution)/shard_map/ppermute | solution.py:353
  174.6 9.7 %collective-permute-start.36 = (bf16[128,2304]{1,0:T(8,128)(2,1)}, bf16[128,2304]{1,0:T(8,128)(2,1)S(1)}, u32[]{:S(2)}, u32[]{:S(2)}) collective-permute-start(bf16[128,2304]{1,0:T(8,128)(2,1)} %collective-permute-done.35.refs_1_), channel_id=1, source_target_pairs={{0,1},{1,0},{2,3},{3,2},{4,5},{5,4},{6,7},{7,6},{8,9},{9,8},{10,11... | collective-permute-start | bytes 1769480 | tf_op jit(solution)/shard_map/ppermute | solution.py:381
  (20 other events, 85.8 us)
where the time goes:
time: 192 us; the launch traced here: 191 us
  waiting for transfers between devices  51.9 us (27%)
  local copies, waits for them, and re-layouts  45.2 us (24%)
  Pallas kernels  42.6 us (22%)
  starting transfers between devices  40.3 us (21%)
  other arithmetic  5.56 us (3%)
  matrix products  3.71 us (2%)
    pallas_call x1, Pallas kernels, row_tree(): pl.pallas_call(functools.partial(row_tree_kernel, 1536), out_shape=jax.Sh...  23.4 us
    ppermute x12, waiting for transfers between devices, body(): up = [lax.ppermute(x, 'rows', ahead) for x in up]  19.2 us
    ppermute x12, starting transfers between devices, body(): down = [lax.ppermute(x, 'rows', behind) for x in down]  18 us
    ppermute x12, waiting for transfers between devices, body(): down = [lax.ppermute(x, 'rows', behind) for x in down]  14 us
    ppermute x1, waiting for transfers between devices, body(): mine = lax.ppermute(half, 'cols', perm)  13 us
    pallas_call x2, Pallas kernels, merge(): pl.pallas_call(functools.partial(merge_kernel, 1152, len(others) == 2, sh...  12.6 us
    ppermute x12, starting transfers between devices, body(): up = [lax.ppermute(x, 'rows', ahead) for x in up]  9.86 us
    dynamic_update_slice x18, local copies, waits for them, and re-layouts, put_map(): return lax.dynamic_update_slice(band, value[None], (at + 1, offset, 0, 0))  8.47 us
  transfers between devices with their start and end apart: 37, of which 18 were waited for; matrix products, arithmetic and copies ran while one was open for 26% of the time, Pallas kernels for 19%

commit v1 on v0

v1 whole, which is shorter than its diff:
```python
import functools
import jax
import jax.numpy as jnp
from jax import lax
from jax.experimental import pallas as pl
from jax.experimental.pallas import tpu as pltpu
from jax.sharding import PartitionSpec as P

NS_STEPS = 5
GROUP = 8
NT = (((1,), (1,)), ((), ()))
F32, BF16 = jnp.float32, jnp.bfloat16
VMEM = pl.BlockSpec(memory_space=pltpu.VMEM)
SMEM = pl.BlockSpec(memory_space=pltpu.SMEM)
ANY = pl.BlockSpec(memory_space=pltpu.HBM)


def mm(a, b):
    return jnp.dot(a, b, preferred_element_type=F32)


def spectral(grams):
    size = grams[0].shape[0]
    rows = lax.broadcasted_iota(jnp.int32, (size, size), 0)
    cols = lax.broadcasted_iota(jnp.int32, (size, size), 1)
    diagonal = rows == cols

    def total(x):
        return jnp.sum(jnp.sum(x, axis=1, keepdims=True), axis=0, keepdims=True)

    spreads = []
    for gram in grams:
        trace = total(jnp.where(diagonal, gram, 0.0))
        spread = gram / (trace + 1e-06) - jnp.where(diagonal, 1.0 / size, 0.0)
        spreads.append(spread / (jnp.sqrt(total(spread * spread)) + 1e-06))
    for sweep in range(NS_STEPS):
        low = [y.astype(BF16) for y in spreads]
        squares = [mm(y, y).astype(BF16) for y in low]
        spreads = [1.5 * s - 0.5 * mm(y, z) for s, y, z in zip(spreads, low, squares)]
    return spreads


def combiner(mix, spread):
    return (0.5 * (mix.astype(F32) + mm(mix, spread.astype(BF16)))).astype(BF16)


def gram_terms(parts):
    total = None
    for part in parts:
        term = lax.dot_general(part, part, NT, preferred_element_type=F32)
        total = term if total is None else total + term
    return total


def shifted(block, left, right):
    at = lax.broadcasted_iota(jnp.int32, block.shape, 0)
    wide = block.astype(F32)
    size = block.shape[0]
    low = jnp.where(at == 0, left, pltpu.roll(wide, 1, 0)).astype(BF16)
    high = jnp.where(at == size - 1, right, pltpu.roll(wide, size - 1, 0)).astype(BF16)
    return low, high


def rows_at(src, j, a, cols):
    size = src.shape[1]
    if a == 1:
        return src[j]
    if a == 0:
        return jnp.concatenate([src[j - 1, size - cols : size], src[j, : size - cols]], axis=0)
    return jnp.concatenate([src[j, cols:size], src[j + 1, :cols]], axis=0)


def shift_row(raw, lo, hi, h, cols, side, n=0):
    rows = side.shape[0] // 4
    at = slice(h * cols, (h + 1) * cols)
    left, right = n * rows + h, (2 + n) * rows + h
    lo[at], hi[at] = shifted(raw[at], side[left : left + 1], side[right : right + 1])


def placed(values):
    return [pltpu.with_memory_space_constraint(x, pltpu.HBM) for x in values]


def start_map(refs, i, target, sem, cut=slice(None)):
    size = target.shape[0]
    if i < len(refs) - 2:
        pltpu.make_async_copy(refs[i].at[pl.ds(0, size), cut], target, sem).start()
    else:
        mid = refs[-1].shape[0]
        pltpu.make_async_copy(refs[-2].at[:, cut], target.at[pl.ds(0, mid)], sem).start()
        pltpu.make_async_copy(refs[-1].at[pl.ds(0, size - mid), cut], target.at[pl.ds(mid, size - mid)], sem).start()


def start_rest(refs, i, ends, sem, cut=slice(None), proj=None, proj_sem=None):
    ref = refs[i] if i < len(refs) - 2 else refs[-1]
    size = ends.shape[0]
    below = ref.shape[0] - size
    if proj is None:
        pltpu.make_async_copy(ref.at[pl.ds(below, size), cut], ends, sem).start()
        return
    rank, pixels = proj.shape
    packed = rank * pixels // ref.shape[1]
    below -= packed
    for n in range(rank // packed):
        part = ref.at[pl.ds(below, packed), pl.ds(n * pixels, pixels)]
        pltpu.make_async_copy(part, proj.at[pl.ds(n * packed, packed)], proj_sem).start()


def arrived(target, sem):
    pltpu.make_async_copy(target, target, sem).wait()


def row_tree_kernel(first, step, rows, rows_ref, mix_ref, *refs):
    feats = refs[:-8]
    count = len(feats) - 1
    out_ref, raw, lo, hi, ends, proj, sk, sems = refs[-8:]
    blocks, pixels, chans = raw.shape
    cols = pixels // rows
    rank = proj.shape[1]

    for i in range(count):
        j = rows_ref[i] - first + 1

        @pl.when((j >= 0) & (j < blocks))
        def fetch(i=i, j=j):
            start_map(feats, i, raw.at[j], sems.at[0, j])
            start_rest(feats, i, ends.at[j], sems.at[1, j])

        @pl.when((j >= 1) & (j < blocks - 1))
        def fetch_projector(i=i, j=j):
            start_rest(feats, i, ends.at[j], None, slice(None), proj.at[j], sems.at[2, j])

    def ready(j, wanted):
        if 0 <= first + j - 1 < count:
            arrived(raw.at[j], sems.at[0, j])
            arrived(ends.at[j], sems.at[1, j])
            side = ends[j].astype(F32)
            for h in wanted:
                shift_row(raw.at[j], lo.at[j], hi.at[j], h, cols, side)
        else:
            for h in wanted:
                for ref in (raw, lo, hi):
                    ref[j, h * cols : (h + 1) * cols] = jnp.zeros((cols, chans), BF16)

    ready(0, (rows - 1,))
    ready(1, range(rows))
    for j in range(1, blocks - 1):
        ready(j + 1, range(rows) if j + 1 < blocks - 1 else (0,))
        arrived(proj.at[j], sems.at[2, j])
        half, part = divmod(j - 1, 2)
        for a in range(3):
            for b, src in enumerate((lo, raw, hi)):
                t = 3 * a + b
                sk[half, part * rank : (part + 1) * rank, t * chans : (t + 1) * chans] = mm(
                    proj[j], rows_at(src, j, a, cols)
                ).astype(BF16)
    mix = mix_ref[...]
    left = (blocks - 2) // 2
    width = sk.shape[-1]
    starts = range(0, width, step)
    while left:
        spreads = spectral(
            [gram_terms(sk[i, :, s : s + step] for s in starts) for i in range(left)]
        )
        for i in range(left):
            mixed = combiner(mix, spreads[i])
            for s in starts:
                piece = mm(mixed, sk[i, :, s : s + step]).astype(BF16)
                if left == 1:
                    out_ref[:, s : s + step] = piece
                else:
                    sk[i // 2, (i % 2) * rank : (i % 2 + 1) * rank, s : s + step] = piece
        left //= 2


def row_tree(slots, mix, feats, first, rows, pixels):
    chans = feats[0].shape[1]
    rank = mix.shape[0]
    width = 9 * chans
    blocks = GROUP + 2
    maps = pltpu.VMEM((blocks, pixels, chans), BF16)
    return pl.pallas_call(
        functools.partial(row_tree_kernel, first, 1536, rows),
        out_shape=jax.ShapeDtypeStruct((rank, width), BF16),
        in_specs=[SMEM, VMEM] + [ANY] * len(feats),
        out_specs=VMEM,
        scratch_shapes=[
            maps,
            maps,
            maps,
            pltpu.VMEM((blocks, 4 * rows, chans), BF16),
            pltpu.VMEM((blocks, rank, pixels), BF16),
            pltpu.VMEM((GROUP // 2, 2 * rank, width), BF16),
            pltpu.SemaphoreType.DMA((3, blocks)),
        ],
        compiler_params=pltpu.CompilerParams(vmem_limit_bytes=48 << 20),
        cost_estimate=pl.CostEstimate(flops=2 * 10**10, bytes_accessed=8 << 20, transcendentals=0),
        name="row_tree",
    )(slots, mix, *placed(feats))


def own_columns(where_ref, own, others, mixed, out_ref):
    share = out_ref.shape[1]
    half = own.shape[1] // 2
    window = (share + 2 * 127) // 128 * 128
    start = where_ref[3] * share
    which = start // half
    inner = start - which * half
    base = pl.multiple_of(jnp.minimum(inner // 128 * 128, half - window), 128)
    core = where_ref[1]
    near = others[0][:, pl.ds(base, window)].astype(F32)
    far = others[1][:, pl.ds(base, window)].astype(F32)
    other = jnp.where(core == which, near, far).astype(BF16)
    part = jnp.concatenate([own[:, pl.ds(pl.multiple_of(which * half + base, 128), window)], other], axis=0)
    value = mm(mixed, part)
    value = pltpu.roll(value, (window - (inner - base)) % window, 1)
    out_ref[...] = value[:, :share].astype(BF16)


def merge_kernel(step, halves, share, where_ref, mix_ref, *refs):
    rank, width = refs[0].shape
    own = refs[0]
    others = refs[1 : 2 + halves]
    outs = refs[2 + halves :]
    if not share:
        *outs, merged, sem = outs
    half = width // 2
    core = where_ref[1]

    def spans():
        for s in range(0, width, step):
            if halves:
                which, inner = divmod(s, half)
                place = pl.multiple_of((core + which) % 2 * half + inner, 128)
                other = others[which][:, inner : inner + step]
            else:
                place, other = s, others[0][:, s : s + step]
            yield place, jnp.concatenate([own[:, pl.ds(place, step)], other], axis=0)

    spread = spectral([gram_terms(part for _, part in spans())])[0]
    if share:
        mix = mix_ref[pl.ds(pl.multiple_of(where_ref[2] * share, 16), share), :]
    else:
        mix = mix_ref[...]
    turned = jnp.concatenate([mix[:, rank:], mix[:, :rank]], axis=1)
    mix = jnp.where(where_ref[0] == 0, mix.astype(F32), turned.astype(F32)).astype(BF16)
    mixed = combiner(mix, spread)
    if share:
        own_columns(where_ref, own, others, mixed, outs[0])
        return
    for place, part in spans():
        merged[:, pl.ds(place, step)] = mm(mixed, part).astype(BF16)
    copy = pltpu.make_async_copy(merged, outs[0], sem)
    copy.start()
    outs[1][...] = merged[:, pl.ds(pl.multiple_of(core * half, 128), half)]
    copy.wait()


def merge(where, mix, own, others, share=None):
    rank, width = own.shape
    if share:
        shapes = [jax.ShapeDtypeStruct(share, BF16)]
    else:
        shapes = [pltpu.HBM((rank, width), BF16), jax.ShapeDtypeStruct((rank, width // 2), BF16)]
    return pl.pallas_call(
        functools.partial(merge_kernel, 1152, len(others) == 2, share[0] if share else 0),
        out_shape=shapes,
        in_specs=[SMEM] + [VMEM] * (2 + len(others)),
        out_specs=[VMEM] if share else [ANY, VMEM],
        scratch_shapes=() if share else (pltpu.VMEM((rank, width), BF16), pltpu.SemaphoreType.DMA),
        compiler_params=pltpu.CompilerParams(vmem_limit_bytes=16 << 20),
        cost_estimate=pl.CostEstimate(flops=4 * 10**9, bytes_accessed=4 << 20, transcendentals=0),
        name="merge",
    )(where, mix, own, *others)


def conv_kernel(rows, slots_ref, kernel_ref, *refs):
    count = (len(refs) - 9) // 2 - 1
    feats, grads = refs[: count + 1], refs[count + 1 : 2 * count + 2]
    out_ref, back_ref, raw, lo, hi, ends, weights, total, sems = refs[-9:]
    pixels, chans = raw.shape[2:]
    cols = pixels // rows
    row = slots_ref[0]
    for i in range(count):
        j = slots_ref[i] - row + 1

        @pl.when((j >= 0) & (j < 3))
        def fetch(i=i, j=j):
            start_map(feats, i, raw.at[0, j], sems.at[0, j])
            start_rest(feats, i, ends.at[j], sems.at[2, j])
            start_map(grads, i, raw.at[1, j], sems.at[1, j])

    for t in range(9):
        pltpu.make_async_copy(
            kernel_ref.at[pl.ds(t * chans, chans)], weights.at[t], sems.at[3, t]
        ).start()

    def waits(n, j):
        arrived(raw.at[n, j], sems.at[n, j])
        if n == 0:
            arrived(ends.at[j], sems.at[2, j])

    for n, out in enumerate((out_ref, back_ref)):
        for j, inside in ((0, row > 0), (2, row < count - 1)):

            @pl.when(jnp.logical_not(inside))
            def clear(n=n, j=j):
                raw[n, j] = jnp.zeros((pixels, chans), BF16)
                if n == 0:
                    ends[j] = jnp.zeros(ends.shape[1:], BF16)

            pl.when(inside)(functools.partial(waits, n, j))
        waits(n, 1)
        sides = [ends[j].astype(F32) for j in range(3)]
        for k in range(rows - 1, 2 * rows + 1):
            j, h = divmod(k, rows)
            shift_row(raw.at[n, j], lo.at[n, j], hi.at[n, j], h, cols, sides[j], n)
        for t in range(9):
            a, b = divmod(t, 3)
            if n == 0:
                arrived(weights.at[t], sems.at[3, t])
                term = mm(rows_at((lo, raw, hi)[b].at[n], 1, a, cols), weights[t])
            else:
                term = lax.dot_general(
                    rows_at((lo, raw, hi)[2 - b].at[n], 1, 2 - a, cols),
                    weights[t],
                    NT,
                    preferred_element_type=F32,
                )
            total[...] = total[...] + term if t else term
        out[...] = total[...].astype(BF16)


def convolutions(slots, kernel, feats, grads, rows):
    pixels, chans = grads[0].shape
    block = jax.ShapeDtypeStruct((pixels, chans), BF16)
    scratch = pltpu.VMEM((2, 3, pixels, chans), BF16)
    inputs = [kernel] + feats + grads
    return pl.pallas_call(
        functools.partial(conv_kernel, rows),
        out_shape=[block, block],
        in_specs=[SMEM] + [ANY] * len(inputs),
        out_specs=[VMEM, VMEM],
        scratch_shapes=[
            scratch,
            scratch,
            scratch,
            pltpu.VMEM((3, 4 * rows, chans), BF16),
            pltpu.VMEM((9, chans, chans), BF16),
            pltpu.VMEM((pixels, chans), F32),
            pltpu.SemaphoreType.DMA((4, 9)),
        ],
        compiler_params=pltpu.CompilerParams(vmem_limit_bytes=20 << 20),
        cost_estimate=pl.CostEstimate(flops=6 * 10**9, bytes_accessed=8 << 20, transcendentals=0),
        name="convolutions",
    )(slots, *placed(inputs))


def filter_kernel(group, rows, where_ref, slots_ref, *refs):
    count = (len(refs) - 9) // 2 - 1
    feats, grads = refs[: count + 1], refs[count + 1 : 2 * count + 2]
    keep_ref, give_ref, raw, lo, hi, ends, grad, total, sems = refs[-9:]
    pixels, lanes = raw.shape[1:]
    cols = pixels // rows
    pieces, taps, share, width = keep_ref.shape
    base = slots_ref[0] * share
    window = pl.multiple_of(base // lanes * lanes, lanes)
    inner = pl.multiple_of(base % lanes, 8)
    core = where_ref[1]
    cut = pl.ds(window, lanes)
    for i in range(count):
        j = slots_ref[i] + 1
        start_map(feats, i, raw.at[j], sems.at[0], cut)
        start_rest(feats, i, ends.at[j], sems.at[1], cut)
        start_map(grads, i, grad.at[j - 1], sems.at[2])
    inside = pl.ds(1, count)
    arrived(raw.at[inside], sems.at[0])
    arrived(ends.at[inside], sems.at[1])
    for j, h in ((0, rows - 1), (count + 1, 0)):
        for ref in (raw, lo, hi):
            ref[j, h * cols : (h + 1) * cols] = jnp.zeros((cols, lanes), BF16)
    for j in range(1, count + 1):
        side = ends[j].astype(F32)
        for h in range(rows):
            shift_row(raw.at[j], lo.at[j], hi.at[j], h, cols, side)
    arrived(grad, sems.at[2])
    chans = grad.shape[2]
    maps = [ref.reshape((count + 2) * pixels, lanes) for ref in (lo, raw, hi)]
    for a in range(3):
        for b, src in enumerate(maps):
            t = 3 * a + b
            for g in range(0, count, group):
                start = pixels * (g + 1) + (a - 1) * cols
                term = lax.dot_general(
                    src[start : start + group * pixels],
                    grad[g : g + group].reshape(group * pixels, chans),
                    (((0,), (0,)), ((), ())),
                    preferred_element_type=F32,
                )
                if g:
                    total[...] += term
                else:
                    total[...] = term
            mine = total[pl.ds(inner, share), :]
            for i in range(pieces):
                even = mine[:, 2 * i * width : (2 * i + 1) * width]
                odd = mine[:, (2 * i + 1) * width : (2 * i + 2) * width]
                keep_ref[i, t] = jnp.where(core == 0, even, odd)
                give_ref[i, t] = jnp.where(core == 0, odd, even).astype(BF16)


def filter_terms(where, slots, feats, grads, rows, share, col_count):
    pixels, chans = grads[0].shape
    count = len(feats) - 1
    lanes = 128
    shape = (col_count // 2, 9, share, chans // col_count)
    window = pltpu.VMEM((count + 2, pixels, lanes), BF16)
    inputs = feats + grads
    return pl.pallas_call(
        functools.partial(filter_kernel, GROUP, rows),
        out_shape=[jax.ShapeDtypeStruct(shape, F32), jax.ShapeDtypeStruct(shape, BF16)],
        in_specs=[SMEM, SMEM] + [ANY] * len(inputs),
        out_specs=[VMEM, VMEM],
        scratch_shapes=[
            window,
            window,
            window,
            pltpu.VMEM((count + 2, 4 * rows, lanes), BF16),
            pltpu.VMEM((count, pixels, chans), BF16),
            pltpu.VMEM((lanes, chans), F32),
            pltpu.SemaphoreType.DMA((3,)),
        ],
        compiler_params=pltpu.CompilerParams(vmem_limit_bytes=(8 + count) << 20),
        cost_estimate=pl.CostEstimate(flops=5 * 10**9, bytes_accessed=4 << 20, transcendentals=0),
        name="filter_terms",
    )(where, slots, *placed(inputs))


def ring_row(place, count):
    return jnp.where(place < count // 2, 2 * place, 2 * (count - 1 - place) + 1)


def ring_place(row, count):
    return jnp.where(row % 2 == 0, row // 2, count - 1 - row // 2)


def after(value, *earlier):
    return lax.optimization_barrier((value,) + earlier)[0]


def body(features, kernel, out_grad, projector, mixers):
    rows, cols, chans = features.shape
    row_count, col_count = lax.axis_size("rows"), lax.axis_size("cols")
    row, col = lax.axis_index("rows"), lax.axis_index("cols")
    rank = projector.shape[0]
    levels = col_count.bit_length() - 1
    half_way, pixels = row_count // 2, rows * cols

    order = list(range(0, row_count, 2)) + list(range(row_count - 1, 0, -2))
    east = [(i, i + 1) for i in range(col_count - 1)]
    west = [(j, i) for i, j in east]
    steps = [0] + [d for s in range(1, half_way) for d in (-s, s)] + [half_way]
    place = ring_place(row, row_count)
    slots = jnp.stack([ring_row((place + d) % row_count, row_count) for d in steps]).astype(jnp.int32)
    where = jnp.stack([row, col % 2, col, row]).astype(jnp.int32)

    def send(value, d):
        hop = [(order[i], order[(i + d) % row_count]) for i in range(row_count)]
        return lax.ppermute(value, "rows", hop)

    packed = rank * pixels // chans
    tail = jnp.concatenate([projector[n : n + packed] for n in range(0, rank, packed)], axis=1)
    own_grad = out_grad.reshape(pixels, chans)
    flat = features.reshape(pixels, chans)
    near = []
    for at, perm in ((cols - 1, east), (0, west)):
        edge = jnp.concatenate([x[at : at + pixels - cols + 1 : cols] for x in (flat, own_grad)])
        near.append(lax.ppermute(edge, "cols", perm))
    size = pixels + packed
    message = jnp.pad(jnp.concatenate([flat, tail], axis=0), ((0, 4 * rows), (0, 0)))
    message = lax.dynamic_update_slice(message, jnp.concatenate(near, axis=0), (size, 0))
    feats = {0: message}
    for s in range(1, half_way):
        for d in (1, -1):
            feats[-s * d] = send(feats[(1 - s) * d], d)
    top, bottom = lax.optimization_barrier((feats[1 - half_way], feats[half_way - 1]))
    mid = message.shape[0] // 2
    feats[half_way] = [send(top[:mid], 1), send(bottom[mid:], -1)]

    grads = {0: own_grad}
    late_grad = after(own_grad, top, bottom)
    for d in (1, 2):
        grads[-d], grads[d] = send(late_grad, d), send(late_grad, -d)

    def listed(found, split=False):
        values = [found[d] for d in steps]
        return values[:-1] + list(values[-1]) if split else values

    feats = listed(feats, True)
    groups = [
        row_tree(slots, mixers[0], feats, start, rows, pixels)
        for start in range(0, row_count, GROUP)
    ]
    while len(groups) > 1:
        straight = where.at[0].set(0)
        groups = [
            merge(straight, mixers[0], groups[i], [groups[i + 1]])[0]
            for i in range(0, len(groups), 2)
        ]
    sketch = groups[0]

    def swap(value, level):
        return lax.ppermute(value, "cols", [(i, i ^ 1 << level) for i in range(col_count)])

    def turn(level):
        return where.at[0].set(col >> level & 1)

    swapped = swap(after(sketch, grads[1], grads[-1], grads[2], grads[-2]), 0)
    top, bottom, _ = lax.optimization_barrier((grads[-2], grads[2], sketch))
    grads[-2], grads[2] = top, bottom
    for s in range(3, half_way):
        for d in (1, -1):
            grads[-s * d] = send(grads[(1 - s) * d], d)
    split, reach = pixels // 2, half_way - 2
    grads[half_way] = [send(top[:split], reach), send(bottom[split:], -reach)]
    result = merge(turn(0), mixers[1], sketch, [swapped])
    sketch, half = result
    grads = listed(grads, True)

    output, grad_features = convolutions(
        after(slots, half), kernel, feats, grads, rows
    )
    share = chans // row_count
    terms, give = filter_terms(
        after(where, grad_features), slots, feats, grads, rows, share, col_count
    )
    filtered = give
    for level in range(levels):
        if level:
            pairs = terms.reshape((-1, 2) + terms.shape[1:])
            bit = col >> level & 1
            terms = lax.dynamic_index_in_dim(pairs, bit, 1, keepdims=False)
            give = lax.dynamic_index_in_dim(pairs, 1 - bit, 1, keepdims=False).astype(BF16)
        got = swap(give, level)
        if level < levels - 1:
            terms = terms + got.astype(F32)

    for level in range(1, levels):
        mine = swap(half, level)
        if level == 1:
            mine = after(mine, filtered)
        others = [mine, swap(mine, 0)]
        final = level == levels - 1
        share = (rank // col_count, sketch.shape[1] // row_count) if final else None
        result = merge(turn(level), mixers[1], sketch, others, share)
        sketch = result[0]
        if not final:
            half = result[1]
    grad_kernel = (terms + after(got, sketch).astype(F32))[0]
    return (
        output.reshape(features.shape),
        grad_features.reshape(features.shape),
        grad_kernel,
        sketch,
    )


def solution(mesh):
    in_specs = (P("rows", "cols", None), P(), P("rows", "cols", None), P("rows", "cols"), P())
    out_specs = (
        P("rows", "cols", None),
        P("rows", "cols", None),
        P(None, "rows", "cols"),
        P("cols", "rows"),
    )
    return jax.shard_map(body, mesh=mesh, in_specs=in_specs, out_specs=out_specs, check_vma=False)
```

time: 192 us -> 117 us (0.61)
  local copies, waits for them, and re-layouts: 45.2 us -> 7.79 us
  waiting for transfers between devices: 51.9 us -> 32.9 us
  starting transfers between devices: 40.3 us -> 26.4 us
  matrix products: 3.71 us -> 0 us
  other arithmetic: 5.56 us -> 2.83 us
  Pallas kernels: 42.6 us -> 44.7 us
    ppermute x37 -> x23, waiting for transfers between devices: 51.9 us -> 32.9 us  [the longest x16 30.8 us: send(): return lax.ppermute(value, 'rows', hop)]
    dynamic_update_slice x26 -> x0, local copies, waits for them, and re-layouts: 14.3 us -> none  [the longest x18 8.47 us: put_map(): return lax.dynamic_update_slice(band, value[None], (at + 1, offset, 0, 0))]
    ppermute x37 -> x23, starting transfers between devices: 40.3 us -> 26.4 us  [the longest x16 20.9 us: send(): return lax.ppermute(value, 'rows', hop)]
    dot_general x2 -> x0, local copies, waits for them, and re-layouts: 8.36 us -> none  [body(): lax.dot_general(patches, flat_grad, (((0,), (0,)), ((), ())), preferred_e...]
    concatenate x2 -> x0, local copies, waits for them, and re-layouts: 6.79 us -> none  [the longest x1 6.79 us: body(): jnp.concatenate([padded[rows - 1 + a:rows - 1 + a + height, b:b + cols] f...]
    dot_general x1 -> x0, matrix products: 3.71 us -> none  [body(): lax.dot_general(patches, flat_grad, (((0,), (0,)), ((), ())), preferred_e...]
    pallas_call x2 -> x3, Pallas kernels: 30 us -> 33.7 us  [the longest x1 22.2 us: row_tree(): pl.pallas_call(functools.partial(row_tree_kernel, first, 1536, rows), out...]
    concatenate x1 -> x2, other arithmetic: 3.36 us -> 0.01 us  [body(): jnp.concatenate([x[at:at + pixels - cols + 1:cols] for x in (flat, own_gr...]
  transfers between devices with their start and end apart: 37 -> 23, of which waited for: 18 -> 10; matrix products, arithmetic and copies ran while one was open for 26% -> 3% of each run, Pallas kernels for 19% -> 39%
where the time goes in v1:
time: 117 us; the launch traced here: 116 us
  Pallas kernels  44.7 us (38%)
  waiting for transfers between devices  32.9 us (28%)
  starting transfers between devices  26.4 us (23%)
  local copies, waits for them, and re-layouts  7.79 us (7%)
  other arithmetic  2.83 us (2%)
    ppermute x16, waiting for transfers between devices, send(): return lax.ppermute(value, 'rows', hop)  30.8 us
    pallas_call x1, Pallas kernels, row_tree(): pl.pallas_call(functools.partial(row_tree_kernel, first, 1536, rows), out...  22.2 us
    ppermute x16, starting transfers between devices, send(): return lax.ppermute(value, 'rows', hop)  20.9 us
    pallas_call x2, Pallas kernels, merge(): pl.pallas_call(functools.partial(merge_kernel, 1152, len(others) == 2, sh...  11 us
    pallas_call x1, Pallas kernels, convolutions(): pl.pallas_call(functools.partial(conv_kernel, rows), out_shape=[block, bl...  6.41 us
    pallas_call x1, Pallas kernels, filter_terms(): pl.pallas_call(functools.partial(filter_kernel, GROUP, rows), out_shape=[...  5.08 us
    ppermute x2, starting transfers between devices, body(): near.append(lax.ppermute(edge, 'cols', perm))  4.32 us
    slice x4, local copies, waits for them, and re-layouts, body(): x[at:at + pixels - cols + 1:cols]  3.95 us
  transfers between devices with their start and end apart: 23, of which 10 were waited for; matrix products, arithmetic and copies ran while one was open for 3% of the time, Pallas kernels for 39%

profile of v1, /device:TPU:0, one launch (start us, length us, event | category | flops | bytes accessed | tf_op | source)
XLA Modules:
  0.0 115.7 jit_solution(12060207677135312525)
XLA Ops:
  0.7 1.0 slice.63
  2.7 1.3 %collective-permute-start.1 = (bf16[16,512]{1,0:T(8,128)(2,1)S(1)}, bf16[16,512]{1,0:T(8,128)(2,1)S(1)}, u32[]{:S(2)}, u32[]{:S(2)}) collective-permute-start(bf16[16,512]{1,0:T(8,128)(2,1)S(1)} %pad_maximum_fusion.2), channel_id=1, source_target_pairs={{1,0},{2,1},{3,2},{5,4},{6,5},{7,6},{9,8},{10,9},{11,10},{13,12},{... | collective-permute-start | bytes 49160 | tf_op jit(solution)/shard_map/ppermute | solution.py:478
  5.9 3.0 %collective-permute-start = (bf16[16,512]{1,0:T(8,128)(2,1)S(1)}, bf16[16,512]{1,0:T(8,128)(2,1)S(1)}, u32[]{:S(2)}, u32[]{:S(2)}) collective-permute-start(bf16[16,512]{1,0:T(8,128)(2,1)S(1)} %pad_maximum_fusion.1), channel_id=1, source_target_pairs={{0,1},{1,2},{2,3},{4,5},{5,6},{6,7},{8,9},{9,10},{10,11},{12,13},{... | collective-permute-start | bytes 49160 | tf_op jit(solution)/shard_map/ppermute | solution.py:478
  10.8 3.1 %collective-permute-start.2 = (bf16[352,512]{1,0:T(8,128)(2,1)S(1)}, bf16[352,512]{1,0:T(8,128)(2,1)S(1)}, u32[]{:S(2)}, u32[]{:S(2)}) collective-permute-start(bf16[352,512]{1,0:T(8,128)(2,1)S(1)} %pad_maximum_fusion.refs_0_), channel_id=1, source_target_pairs={{0,8},{8,16},{16,24},{24,28},{28,20},{20,12},{12,4},{4,0},{1,9},{9... | collective-permute-start | bytes 1081352 | tf_op jit(solution)/shard_map/ppermute | solution.py:469
  13.8 8.6 %collective-permute-done.2.refs_1_ = bf16[352,512]{1,0:T(8,128)(2,1)S(1)} collective-permute-done((bf16[352,512]{1,0:T(8,128)(2,1)S(1)}, bf16[352,512]{1,0:T(8,128)(2,1)S(1)}, u32[]{:S(2)}, u32[]{:S(2)}) %collective-permute-start.2) | collective-permute-done | bytes 360480 | tf_op jit(solution)/shard_map/ppermute | solution.py:469
  22.4 2.5 %collective-permute-start.4 = (bf16[352,512]{1,0:T(8,128)(2,1)S(1)}, bf16[352,512]{1,0:T(8,128)(2,1)S(1)}, u32[]{:S(2)}, u32[]{:S(2)}) collective-permute-start(bf16[352,512]{1,0:T(8,128)(2,1)S(1)} %collective-permute-done.2.refs_1_), channel_id=1, source_target_pairs={{0,8},{8,16},{16,24},{24,28},{28,20},{20,12},{12,4},{4,0},{1,9},{9... | collective-permute-start | bytes 1081352 | tf_op jit(solution)/shard_map/ppermute | solution.py:469
  25.1 8.5 %collective-permute-done.4.refs_3_ = bf16[352,512]{1,0:T(8,128)(2,1)S(1)} collective-permute-done((bf16[352,512]{1,0:T(8,128)(2,1)S(1)}, bf16[352,512]{1,0:T(8,128)(2,1)S(1)}, u32[]{:S(2)}, u32[]{:S(2)}) %collective-permute-start.4) | collective-permute-done | bytes 360480 | tf_op jit(solution)/shard_map/ppermute | solution.py:469
  33.5 2.0 %collective-permute-start.6 = (bf16[352,512]{1,0:T(8,128)(2,1)S(1)}, bf16[352,512]{1,0:T(8,128)(2,1)S(1)}, u32[]{:S(2)}, u32[]{:S(2)}) collective-permute-start(bf16[352,512]{1,0:T(8,128)(2,1)S(1)} %collective-permute-done.4.refs_3_), channel_id=1, source_target_pairs={{0,8},{8,16},{16,24},{24,28},{28,20},{20,12},{12,4},{4,0},{1,9},{9... | collective-permute-start | bytes 1081352 | tf_op jit(solution)/shard_map/ppermute | solution.py:469
  35.9 7.6 %collective-permute-done.6.refs_5_ = bf16[352,512]{1,0:T(8,128)(2,1)S(1)} collective-permute-done((bf16[352,512]{1,0:T(8,128)(2,1)S(1)}, bf16[352,512]{1,0:T(8,128)(2,1)S(1)}, u32[]{:S(2)}, u32[]{:S(2)}) %collective-permute-start.6) | collective-permute-done | bytes 360480 | tf_op jit(solution)/shard_map/ppermute | solution.py:469
  43.5 1.7 %collective-permute-done.7.refs_6_ = bf16[352,512]{1,0:T(8,128)(2,1)S(1)} collective-permute-done((bf16[352,512]{1,0:T(8,128)(2,1)S(1)}, bf16[352,512]{1,0:T(8,128)(2,1)S(1)}, u32[]{:S(2)}, u32[]{:S(2)}) %collective-permute-start.7) | collective-permute-done | bytes 360480 | tf_op jit(solution)/shard_map/ppermute | solution.py:469
  45.2 1.6 %collective-permute-start.8 = (bf16[176,512]{1,0:T(8,128)(2,1)S(1)}, bf16[176,512]{1,0:T(8,128)(2,1)S(1)}, u32[]{:S(2)}, u32[]{:S(2)}) collective-permute-start(bf16[176,512]{1,0:T(8,128)(2,1)S(1)} %slice.64), channel_id=1, source_target_pairs={{0,8},{8,16},{16,24},{24,28},{28,20},{20,12},{12,4},{4,0},{1,9},{9... | collective-permute-start | bytes 540680 | tf_op jit(solution)/shard_map/ppermute | solution.py:469
  47.7 1.7 %collective-permute-start.11 = (bf16[256,512]{1,0:T(8,128)(2,1)S(1)}, bf16[256,512]{1,0:T(8,128)(2,1)S(1)}, u32[]{:S(2)}, u32[]{:S(2)}) collective-permute-start(bf16[256,512]{1,0:T(8,128)(2,1)S(1)} %bitcast.31), channel_id=1, source_target_pairs={{0,8},{8,16},{16,24},{24,28},{28,20},{20,12},{12,4},{4,0},{1,9},{9... | collective-permute-start | bytes 786440 | tf_op jit(solution)/shard_map/ppermute | solution.py:469
  49.4 1.2 %collective-permute-start.12 = (bf16[256,512]{1,0:T(8,128)(2,1)S(1)}, bf16[256,512]{1,0:T(8,128)(2,1)S(1)}, u32[]{:S(2)}, u32[]{:S(2)}) collective-permute-start(bf16[256,512]{1,0:T(8,128)(2,1)S(1)} %bitcast.32), channel_id=1, source_target_pairs={{0,12},{8,4},{16,0},{24,8},{28,16},{20,24},{12,28},{4,20},{1,13},{... | collective-permute-start | bytes 786440 | tf_op jit(solution)/shard_map/ppermute | solution.py:469
  50.7 1.9 %collective-permute-done.8.refs_7_ = bf16[176,512]{1,0:T(8,128)(2,1)S(1)} collective-permute-done((bf16[176,512]{1,0:T(8,128)(2,1)S(1)}, bf16[176,512]{1,0:T(8,128)(2,1)S(1)}, u32[]{:S(2)}, u32[]{:S(2)}) %collective-permute-start.8) | collective-permute-done | bytes 180256 | tf_op jit(solution)/shard_map/ppermute | solution.py:469
  52.6 2.7 %collective-permute-start.13 = (bf16[256,512]{1,0:T(8,128)(2,1)S(1)}, bf16[256,512]{1,0:T(8,128)(2,1)S(1)}, u32[]{:S(2)}, u32[]{:S(2)}) collective-permute-start(bf16[256,512]{1,0:T(8,128)(2,1)S(1)} %bitcast.33), channel_id=1, source_target_pairs={{0,16},{8,24},{16,28},{24,20},{28,12},{20,4},{12,0},{4,8},{1,17},{... | collective-permute-start | bytes 786440 | tf_op jit(solution)/shard_map/ppermute | solution.py:469
  56.0 22.2 %row_tree.1.refs_0_ = bf16[128,4608]{1,0:T(8,128)(2,1)S(1)} custom-call(s32[8]{0:T(128)S(1)} %stack.48.rows_ref.slots_ref, bf16[128,256]{1,0:T(8,128)(2,1)S(1)} %get-tuple-element.60.mix_ref, bf16[352,512]{1,0:T(8,128)(2,1)} %copy-done.1, bf16[352,512]{1,0:T(8,128)(2,1)} %copy-done.8, bf16[352,512]{1,0:T(8,128)(2,1)} %copy-done.9, ...), custom_call_target="tpu_custom_call" | custom-call | flops 20000000000 | bytes 8388608 | tf_op jit(solution)/shard_map/row_tree/pallas_call | solution.py:182
  79.1 1.8 %collective-permute-start.15 = (bf16[256,512]{1,0:T(8,128)(2,1)S(1)}, bf16[256,512]{1,0:T(8,128)(2,1)S(1)}, u32[]{:S(2)}, u32[]{:S(2)}) collective-permute-start(bf16[256,512]{1,0:T(8,128)(2,1)S(1)} %collective-permute-done.13.refs_12_), channel_id=1, source_target_pairs={{0,8},{8,16},{16,24},{24,28},{28,20},{20,12},{12,4},{4,0},{1,9},{9... | collective-permute-start | bytes 786440 | tf_op jit(solution)/shard_map/ppermute | solution.py:469
  81.2 2.1 %collective-permute-start.17 = (bf16[128,512]{1,0:T(8,128)(2,1)S(1)}, bf16[128,512]{1,0:T(8,128)(2,1)S(1)}, u32[]{:S(2)}, u32[]{:S(2)}) collective-permute-start(bf16[128,512]{1,0:T(8,128)(2,1)S(1)} %slice.66), channel_id=1, source_target_pairs={{0,16},{8,24},{16,28},{24,20},{28,12},{20,4},{12,0},{4,8},{1,17},{... | collective-permute-start | bytes 393224 | tf_op jit(solution)/shard_map/ppermute | solution.py:469
  84.2 6.2 %merge.2 = (bf16[128,4608]{1,0:T(8,128)(2,1)}, bf16[128,2304]{1,0:T(8,128)(2,1)S(1)}) custom-call(s32[4]{0:T(128)S(1)} %constant_dynamic-update-slice_fusion.1.where_ref, bf16[128,256]{1,0:T(8,128)(2,1)S(1)} %get-tuple-element.61.mix_ref, bf16[128,4608]{1,0:T(8,128)(2,1)S(1)} %row_tree.1.refs_0_, bf16[128,4608]{1,0:T(8,128)(2,1)S(1)} %collective-permute-done.14.refs_1_), custom_call_target="tpu_custom_call" | custom-call | flops 4000000000 | bytes 4194304 | tf_op jit(solution)/shard_map/merge/pallas_call | solution.py:265
  91.5 1.7 %collective-permute-done.18.refs_17_ = bf16[128,512]{1,0:T(8,128)(2,1)S(1)} collective-permute-done((bf16[128,512]{1,0:T(8,128)(2,1)S(1)}, bf16[128,512]{1,0:T(8,128)(2,1)S(1)}, u32[]{:S(2)}, u32[]{:S(2)}) %collective-permute-start.18) | collective-permute-done | bytes 131104 | tf_op jit(solution)/shard_map/ppermute | solution.py:469
  94.6 6.4 %convolutions.1 = (bf16[256,512]{1,0:T(8,128)(2,1)}, bf16[256,512]{1,0:T(8,128)(2,1)}) custom-call(s32[8]{0:T(128)S(1)} %stack.48.rows_ref.slots_ref, bf16[4608,512]{1,0:T(8,128)(2,1)} %kernel_ref.1, bf16[352,512]{1,0:T(8,128)(2,1)} %copy-done.1, bf16[352,512]{1,0:T(8,128)(2,1)} %copy-done.8, bf16[352,512]{1,0:T(8,128)(2,1)} %copy-done.9, ...), custom_call_target="tpu_custom_call" | custom-call | flops 6000000000 | bytes 8388608 | tf_op jit(solution)/shard_map/convolutions/pallas_call | solution.py:339
  101.1 5.1 %filter_terms.1 = (f32[2,9,64,128]{3,2,1,0:T(8,128)S(1)}, bf16[2,9,64,128]{3,2,1,0:T(8,128)(2,1)S(1)}) custom-call(s32[4]{0:T(128)S(1)} %pad_add_fusion.where_ref, s32[8]{0:T(128)S(1)} %stack.48.rows_ref.slots_ref, bf16[352,512]{1,0:T(8,128)(2,1)} %copy-done.1, bf16[352,512]{1,0:T(8,128)(2,1)} %copy-done.8, bf16[352,512]{1,0:T(8,128)(2,1)} %copy-done.9, ...), custom_call_target="tpu_custom_call" | custom-call | flops 5000000000 | bytes 4194304 | tf_op jit(solution)/shard_map/filter_terms/pallas_call | solution.py:419
  106.8 1.2 %collective-permute-done.19 = bf16[2,9,64,128]{3,2,1,0:T(8,128)(2,1)} collective-permute-done((bf16[2,9,64,128]{3,2,1,0:T(8,128)(2,1)S(1)}, bf16[2,9,64,128]{3,2,1,0:T(8,128)(2,1)}, u32[]{:S(2)}, u32[]{:S(2)}) %collective-permute-start.19) | collective-permute-done | bytes 294944 | tf_op jit(solution)/shard_map/ppermute | solution.py:513
  109.3 4.9 %merge.3 = bf16[32,576]{1,0:T(8,128)(2,1)} custom-call(s32[4]{0:T(128)S(1)} %constant_dynamic-update-slice_fusion.where_ref, bf16[128,256]{1,0:T(8,128)(2,1)S(1)} %get-tuple-element.61.mix_ref, bf16[128,4608]{1,0:T(8,128)(2,1)S(1)} %copy-done, bf16[128,2304]{1,0:T(8,128)(2,1)S(1)} %collective-permute-done.21.refs_1_, ...), custom_call_target="tpu_custom_call" | custom-call | flops 4000000000 | bytes 4194304 | tf_op jit(solution)/shard_map/merge/pallas_call | solution.py:265
  (88 shorter events, 14.7 us)
Async XLA Ops:
  0.6 46.7 %copy-start.7 = (bf16[8,32,512]{2,1,0:T(8,128)(2,1)S(1)}, bf16[8,32,512]{2,1,0:T(8,128)(2,1)}, u32[]{:S(2)}) copy-start(bf16[8,32,512]{2,1,0:T(8,128)(2,1)} %param.11) | copy-start | bytes 786436
  2.7 7.1 %collective-permute-start.1 = (bf16[16,512]{1,0:T(8,128)(2,1)S(1)}, bf16[16,512]{1,0:T(8,128)(2,1)S(1)}, u32[]{:S(2)}, u32[]{:S(2)}) collective-permute-start(bf16[16,512]{1,0:T(8,128)(2,1)S(1)} %pad_maximum_fusion.2), channel_id=1, source_target_pairs={{1,0},{2,1},{3,2},{5,4},{6,5},{7,6},{9,8},{10,9},{11,10},{13,12},{... | collective-permute-start | bytes 49160 | tf_op jit(solution)/shard_map/ppermute | solution.py:478
  5.9 3.9 %collective-permute-start = (bf16[16,512]{1,0:T(8,128)(2,1)S(1)}, bf16[16,512]{1,0:T(8,128)(2,1)S(1)}, u32[]{:S(2)}, u32[]{:S(2)}) collective-permute-start(bf16[16,512]{1,0:T(8,128)(2,1)S(1)} %pad_maximum_fusion.1), channel_id=1, source_target_pairs={{0,1},{1,2},{2,3},{4,5},{5,6},{6,7},{8,9},{9,10},{10,11},{12,13},{... | collective-permute-start | bytes 49160 | tf_op jit(solution)/shard_map/ppermute | solution.py:478
  10.8 11.7 %collective-permute-start.2 = (bf16[352,512]{1,0:T(8,128)(2,1)S(1)}, bf16[352,512]{1,0:T(8,128)(2,1)S(1)}, u32[]{:S(2)}, u32[]{:S(2)}) collective-permute-start(bf16[352,512]{1,0:T(8,128)(2,1)S(1)} %pad_maximum_fusion.refs_0_), channel_id=1, source_target_pairs={{0,8},{8,16},{16,24},{24,28},{28,20},{20,12},{12,4},{4,0},{1,9},{9... | collective-permute-start | bytes 1081352 | tf_op jit(solution)/shard_map/ppermute | solution.py:469
  13.8 11.2 %collective-permute-start.3 = (bf16[352,512]{1,0:T(8,128)(2,1)S(1)}, bf16[352,512]{1,0:T(8,128)(2,1)S(1)}, u32[]{:S(2)}, u32[]{:S(2)}) collective-permute-start(bf16[352,512]{1,0:T(8,128)(2,1)S(1)} %pad_maximum_fusion.refs_0_), channel_id=1, source_target_pairs={{0,4},{8,0},{16,8},{24,16},{28,24},{20,28},{12,20},{4,12},{1,5},{9... | collective-permute-start | bytes 1081352 | tf_op jit(solution)/shard_map/ppermute | solution.py:469
  22.4 11.1 %collective-permute-start.4 = (bf16[352,512]{1,0:T(8,128)(2,1)S(1)}, bf16[352,512]{1,0:T(8,128)(2,1)S(1)}, u32[]{:S(2)}, u32[]{:S(2)}) collective-permute-start(bf16[352,512]{1,0:T(8,128)(2,1)S(1)} %collective-permute-done.2.refs_1_), channel_id=1, source_target_pairs={{0,8},{8,16},{16,24},{24,28},{28,20},{20,12},{12,4},{4,0},{1,9},{9... | collective-permute-start | bytes 1081352 | tf_op jit(solution)/shard_map/ppermute | solution.py:469
  25.0 10.5 %collective-permute-start.5 = (bf16[352,512]{1,0:T(8,128)(2,1)S(1)}, bf16[352,512]{1,0:T(8,128)(2,1)S(1)}, u32[]{:S(2)}, u32[]{:S(2)}) collective-permute-start(bf16[352,512]{1,0:T(8,128)(2,1)S(1)} %collective-permute-done.3.refs_2_), channel_id=1, source_target_pairs={{0,4},{8,0},{16,8},{24,16},{28,24},{20,28},{12,20},{4,12},{1,5},{9... | collective-permute-start | bytes 1081352 | tf_op jit(solution)/shard_map/ppermute | solution.py:469
  33.5 9.9 %collective-permute-start.6 = (bf16[352,512]{1,0:T(8,128)(2,1)S(1)}, bf16[352,512]{1,0:T(8,128)(2,1)S(1)}, u32[]{:S(2)}, u32[]{:S(2)}) collective-permute-start(bf16[352,512]{1,0:T(8,128)(2,1)S(1)} %collective-permute-done.4.refs_3_), channel_id=1, source_target_pairs={{0,8},{8,16},{16,24},{24,28},{28,20},{20,12},{12,4},{4,0},{1,9},{9... | collective-permute-start | bytes 1081352 | tf_op jit(solution)/shard_map/ppermute | solution.py:469
  35.6 9.6 %collective-permute-start.7 = (bf16[352,512]{1,0:T(8,128)(2,1)S(1)}, bf16[352,512]{1,0:T(8,128)(2,1)S(1)}, u32[]{:S(2)}, u32[]{:S(2)}) collective-permute-start(bf16[352,512]{1,0:T(8,128)(2,1)S(1)} %collective-permute-done.5.refs_4_), channel_id=1, source_target_pairs={{0,4},{8,0},{16,8},{24,16},{28,24},{20,28},{12,20},{4,12},{1,5},{9... | collective-permute-start | bytes 1081352 | tf_op jit(solution)/shard_map/ppermute | solution.py:469
  45.2 7.4 %collective-permute-start.8 = (bf16[176,512]{1,0:T(8,128)(2,1)S(1)}, bf16[176,512]{1,0:T(8,128)(2,1)S(1)}, u32[]{:S(2)}, u32[]{:S(2)}) collective-permute-start(bf16[176,512]{1,0:T(8,128)(2,1)S(1)} %slice.64), channel_id=1, source_target_pairs={{0,8},{8,16},{16,24},{24,28},{28,20},{20,12},{12,4},{4,0},{1,9},{9... | collective-permute-start | bytes 540680 | tf_op jit(solution)/shard_map/ppermute | solution.py:469
  46.8 8.5 %collective-permute-start.9 = (bf16[176,512]{1,0:T(8,128)(2,1)S(1)}, bf16[176,512]{1,0:T(8,128)(2,1)S(1)}, u32[]{:S(2)}, u32[]{:S(2)}) collective-permute-start(bf16[176,512]{1,0:T(8,128)(2,1)S(1)} %slice.65), channel_id=1, source_target_pairs={{0,4},{8,0},{16,8},{24,16},{28,24},{20,28},{12,20},{4,12},{1,5},{9... | collective-permute-start | bytes 540680 | tf_op jit(solution)/shard_map/ppermute | solution.py:469
  47.4 30.8 %collective-permute-start.10 = (bf16[256,512]{1,0:T(8,128)(2,1)S(1)}, bf16[256,512]{1,0:T(8,128)(2,1)S(1)}, u32[]{:S(2)}, u32[]{:S(2)}) collective-permute-start(bf16[256,512]{1,0:T(8,128)(2,1)S(1)} %bitcast.30), channel_id=1, source_target_pairs={{0,4},{8,0},{16,8},{24,16},{28,24},{20,28},{12,20},{4,12},{1,5},{9... | collective-permute-start | bytes 786440 | tf_op jit(solution)/shard_map/ppermute | solution.py:469
  47.7 30.5 %collective-permute-start.11 = (bf16[256,512]{1,0:T(8,128)(2,1)S(1)}, bf16[256,512]{1,0:T(8,128)(2,1)S(1)}, u32[]{:S(2)}, u32[]{:S(2)}) collective-permute-start(bf16[256,512]{1,0:T(8,128)(2,1)S(1)} %bitcast.31), channel_id=1, source_target_pairs={{0,8},{8,16},{16,24},{24,28},{28,20},{20,12},{12,4},{4,0},{1,9},{9... | collective-permute-start | bytes 786440 | tf_op jit(solution)/shard_map/ppermute | solution.py:469
  49.4 28.8 %collective-permute-start.12 = (bf16[256,512]{1,0:T(8,128)(2,1)S(1)}, bf16[256,512]{1,0:T(8,128)(2,1)S(1)}, u32[]{:S(2)}, u32[]{:S(2)}) collective-permute-start(bf16[256,512]{1,0:T(8,128)(2,1)S(1)} %bitcast.32), channel_id=1, source_target_pairs={{0,12},{8,4},{16,0},{24,8},{28,16},{20,24},{12,28},{4,20},{1,13},{... | collective-permute-start | bytes 786440 | tf_op jit(solution)/shard_map/ppermute | solution.py:469
  52.6 25.6 %collective-permute-start.13 = (bf16[256,512]{1,0:T(8,128)(2,1)S(1)}, bf16[256,512]{1,0:T(8,128)(2,1)S(1)}, u32[]{:S(2)}, u32[]{:S(2)}) collective-permute-start(bf16[256,512]{1,0:T(8,128)(2,1)S(1)} %bitcast.33), channel_id=1, source_target_pairs={{0,16},{8,24},{16,28},{24,20},{28,12},{20,4},{12,0},{4,8},{1,17},{... | collective-permute-start | bytes 786440 | tf_op jit(solution)/shard_map/ppermute | solution.py:469
  79.0 5.2 %collective-permute-start.14 = (bf16[128,4608]{1,0:T(8,128)(2,1)S(1)}, bf16[128,4608]{1,0:T(8,128)(2,1)S(1)}, u32[]{:S(2)}, u32[]{:S(2)}) collective-permute-start(bf16[128,4608]{1,0:T(8,128)(2,1)S(1)} %row_tree.1.refs_0_), channel_id=1, source_target_pairs={{0,1},{1,0},{2,3},{3,2},{4,5},{5,4},{6,7},{7,6},{8,9},{9,8},{10,11... | collective-permute-start | bytes 3538952 | tf_op jit(solution)/shard_map/ppermute | solution.py:513
  79.1 14.1 %collective-permute-start.15 = (bf16[256,512]{1,0:T(8,128)(2,1)S(1)}, bf16[256,512]{1,0:T(8,128)(2,1)S(1)}, u32[]{:S(2)}, u32[]{:S(2)}) collective-permute-start(bf16[256,512]{1,0:T(8,128)(2,1)S(1)} %collective-permute-done.13.refs_12_), channel_id=1, source_target_pairs={{0,8},{8,16},{16,24},{24,28},{28,20},{20,12},{12,4},{4,0},{1,9},{9... | collective-permute-start | bytes 786440 | tf_op jit(solution)/shard_map/ppermute | solution.py:469
  80.9 12.3 %collective-permute-start.16 = (bf16[256,512]{1,0:T(8,128)(2,1)S(1)}, bf16[256,512]{1,0:T(8,128)(2,1)S(1)}, u32[]{:S(2)}, u32[]{:S(2)}) collective-permute-start(bf16[256,512]{1,0:T(8,128)(2,1)S(1)} %collective-permute-done.12.refs_13_), channel_id=1, source_target_pairs={{0,4},{8,0},{16,8},{24,16},{28,24},{20,28},{12,20},{4,12},{1,5},{9... | collective-permute-start | bytes 786440 | tf_op jit(solution)/shard_map/ppermute | solution.py:469
  81.2 10.2 %collective-permute-start.17 = (bf16[128,512]{1,0:T(8,128)(2,1)S(1)}, bf16[128,512]{1,0:T(8,128)(2,1)S(1)}, u32[]{:S(2)}, u32[]{:S(2)}) collective-permute-start(bf16[128,512]{1,0:T(8,128)(2,1)S(1)} %slice.66), channel_id=1, source_target_pairs={{0,16},{8,24},{16,28},{24,20},{28,12},{20,4},{12,0},{4,8},{1,17},{... | collective-permute-start | bytes 393224 | tf_op jit(solution)/shard_map/ppermute | solution.py:469
  83.3 9.9 %collective-permute-start.18 = (bf16[128,512]{1,0:T(8,128)(2,1)S(1)}, bf16[128,512]{1,0:T(8,128)(2,1)S(1)}, u32[]{:S(2)}, u32[]{:S(2)}) collective-permute-start(bf16[128,512]{1,0:T(8,128)(2,1)S(1)} %slice.67), channel_id=1, source_target_pairs={{0,12},{8,4},{16,0},{24,8},{28,16},{20,24},{12,28},{4,20},{1,13},{... | collective-permute-start | bytes 393224 | tf_op jit(solution)/shard_map/ppermute | solution.py:469
  90.4 15.9 %collective-permute-start.21 = (bf16[128,2304]{1,0:T(8,128)(2,1)S(1)}, bf16[128,2304]{1,0:T(8,128)(2,1)S(1)}, u32[]{:S(2)}, u32[]{:S(2)}) collective-permute-start(bf16[128,2304]{1,0:T(8,128)(2,1)S(1)} %get-tuple-element.48), channel_id=1, source_target_pairs={{0,2},{1,3},{2,0},{3,1},{4,6},{5,7},{6,4},{7,5},{8,10},{9,11},{10,... | collective-permute-start | bytes 1769480 | tf_op jit(solution)/shard_map/ppermute | solution.py:513
  106.2 1.8 %collective-permute-start.19 = (bf16[2,9,64,128]{3,2,1,0:T(8,128)(2,1)S(1)}, bf16[2,9,64,128]{3,2,1,0:T(8,128)(2,1)}, u32[]{:S(2)}, u32[]{:S(2)}) collective-permute-start(bf16[2,9,64,128]{3,2,1,0:T(8,128)(2,1)S(1)} %get-tuple-element.56), channel_id=1, source_target_pairs={{0,1},{1,0},{2,3},{3,2},{4,5},{5,4},{6,7},{7,6},{8,9},{9,8},{10,11... | collective-permute-start | bytes 884744 | tf_op jit(solution)/shard_map/ppermute | solution.py:513
  106.3 3.0 %collective-permute-start.22 = (bf16[128,2304]{1,0:T(8,128)(2,1)S(1)}, bf16[128,2304]{1,0:T(8,128)(2,1)S(1)}, u32[]{:S(2)}, u32[]{:S(2)}) collective-permute-start(bf16[128,2304]{1,0:T(8,128)(2,1)S(1)} %collective-permute-done.21.refs_1_), channel_id=1, source_target_pairs={{0,1},{1,0},{2,3},{3,2},{4,5},{5,4},{6,7},{7,6},{8,9},{9,8},{10,11... | collective-permute-start | bytes 1769480 | tf_op jit(solution)/shard_map/ppermute | solution.py:513
  109.0 6.0 %collective-permute-start.20 = (bf16[1,9,64,128]{3,2,1,0:T(8,128)(2,1)S(1)}, bf16[1,9,64,128]{3,2,1,0:T(8,128)(2,1)S(1)}, u32[]{:S(2)}, u32[]{:S(2)}) collective-permute-start(bf16[1,9,64,128]{3,2,1,0:T(8,128)(2,1)S(1)} %dynamic-slice_convert_fusion), channel_id=1, source_target_pairs={{0,2},{1,3},{2,0},{3,1},{4,6},{5,7},{6,4},{7,5},{8,10},{9,11},{10,... | collective-permute-start | bytes 442376 | tf_op jit(solution)/shard_map/ppermute | solution.py:513
  (19 other events, 214.8 us)

commit v2 on v1

--- a/solution.py
+++ b/solution.py
@@ -33,7 +33,7 @@
         trace = total(jnp.where(diagonal, gram, 0.0))
         spread = gram / (trace + 1e-06) - jnp.where(diagonal, 1.0 / size, 0.0)
         spreads.append(spread / (jnp.sqrt(total(spread * spread)) + 1e-06))
-    for sweep in range(NS_STEPS):
+    for sweep in range(NS_STEPS - 1):
         low = [y.astype(BF16) for y in spreads]
         squares = [mm(y, y).astype(BF16) for y in low]
         spreads = [1.5 * s - 0.5 * mm(y, z) for s, y, z in zip(spreads, low, squares)]
@@ -41,7 +41,11 @@
 
 
 def combiner(mix, spread):
-    return (0.5 * (mix.astype(F32) + mm(mix, spread.astype(BF16)))).astype(BF16)
+    low = spread.astype(BF16)
+    square = mm(low, low).astype(BF16)
+    once = mm(mix, low)
+    turned = 1.5 * once - 0.5 * mm(once.astype(BF16), square)
+    return (0.5 * (mix.astype(F32) + turned)).astype(BF16)
 
 
 def gram_terms(parts):
@@ -249,11 +253,11 @@
         own_columns(where_ref, own, others, mixed, outs[0])
         return
     for place, part in spans():
-        merged[:, pl.ds(place, step)] = mm(mixed, part).astype(BF16)
-    copy = pltpu.make_async_copy(merged, outs[0], sem)
-    copy.start()
+        span = pl.ds(place, step)
+        merged[:, span] = mm(mixed, part).astype(BF16)
+        pltpu.make_async_copy(merged.at[:, span], outs[0].at[:, span], sem).start()
     outs[1][...] = merged[:, pl.ds(pl.multiple_of(core * half, 128), half)]
-    copy.wait()
+    pltpu.make_async_copy(merged, outs[0], sem).wait()
 
 
 def merge(where, mix, own, others, share=None):
@@ -274,11 +278,10 @@
     )(where, mix, own, *others)
 
 
-def conv_kernel(rows, slots_ref, kernel_ref, *refs):
-    count = (len(refs) - 9) // 2 - 1
-    feats, grads = refs[: count + 1], refs[count + 1 : 2 * count + 2]
-    out_ref, back_ref, raw, lo, hi, ends, weights, total, sems = refs[-9:]
-    pixels, chans = raw.shape[2:]
+def conv_steps(rows, back, slots_ref, kernel_ref, feats, grads, out_ref, scratch):
+    count = len(feats) - 1
+    raw, lo, hi, ends, weights, total, sems = scratch
+    pixels, chans = raw.shape[1:]
     cols = pixels // rows
     row = slots_ref[0]
     for i in range(count):
@@ -286,80 +289,94 @@
 
         @pl.when((j >= 0) & (j < 3))
         def fetch(i=i, j=j):
-            start_map(feats, i, raw.at[0, j], sems.at[0, j])
-            start_rest(feats, i, ends.at[j], sems.at[2, j])
-            start_map(grads, i, raw.at[1, j], sems.at[1, j])
+            start_map(grads if back else feats, i, raw.at[j], sems.at[0, j])
+            start_rest(feats, i, ends.at[j], sems.at[1, j])
 
     for t in range(9):
         pltpu.make_async_copy(
-            kernel_ref.at[pl.ds(t * chans, chans)], weights.at[t], sems.at[3, t]
+            kernel_ref.at[pl.ds(t * chans, chans)], weights.at[t], sems.at[2, t]
         ).start()
-
-    def waits(n, j):
-        arrived(raw.at[n, j], sems.at[n, j])
-        if n == 0:
-            arrived(ends.at[j], sems.at[2, j])
-
-    for n, out in enumerate((out_ref, back_ref)):
-        for j, inside in ((0, row > 0), (2, row < count - 1)):
-
-            @pl.when(jnp.logical_not(inside))
-            def clear(n=n, j=j):
-                raw[n, j] = jnp.zeros((pixels, chans), BF16)
-                if n == 0:
-                    ends[j] = jnp.zeros(ends.shape[1:], BF16)
-
-            pl.when(inside)(functools.partial(waits, n, j))
-        waits(n, 1)
-        sides = [ends[j].astype(F32) for j in range(3)]
-        for k in range(rows - 1, 2 * rows + 1):
-            j, h = divmod(k, rows)
-            shift_row(raw.at[n, j], lo.at[n, j], hi.at[n, j], h, cols, sides[j], n)
-        for t in range(9):
-            a, b = divmod(t, 3)
-            if n == 0:
-                arrived(weights.at[t], sems.at[3, t])
-                term = mm(rows_at((lo, raw, hi)[b].at[n], 1, a, cols), weights[t])
-            else:
-                term = lax.dot_general(
-                    rows_at((lo, raw, hi)[2 - b].at[n], 1, 2 - a, cols),
-                    weights[t],
-                    NT,
-                    preferred_element_type=F32,
-                )
-            total[...] = total[...] + term if t else term
-        out[...] = total[...].astype(BF16)
-
-
-def convolutions(slots, kernel, feats, grads, rows):
-    pixels, chans = grads[0].shape
-    block = jax.ShapeDtypeStruct((pixels, chans), BF16)
-    scratch = pltpu.VMEM((2, 3, pixels, chans), BF16)
-    inputs = [kernel] + feats + grads
+    yield
+
+    def waits(j):
+        arrived(raw.at[j], sems.at[0, j])
+        arrived(ends.at[j], sems.at[1, j])
+
+    for j, inside in ((0, row > 0), (2, row < count - 1)):
+
+        @pl.when(jnp.logical_not(inside))
+        def clear(j=j):
+            raw[j] = jnp.zeros((pixels, chans), BF16)
+            ends[j] = jnp.zeros(ends.shape[1:], BF16)
+
+        pl.when(inside)(functools.partial(waits, j))
+    waits(1)
+    sides = [ends[j].astype(F32) for j in range(3)]
+    for k in range(rows - 1, 2 * rows + 1):
+        j, h = divmod(k, rows)
+        shift_row(raw.at[j], lo.at[j], hi.at[j], h, cols, sides[j], int(back))
+    for t in range(9):
+        a, b = divmod(t, 3)
+        arrived(weights.at[t], sems.at[2, t])
+        if back:
+            term = lax.dot_general(
+                rows_at((lo, raw, hi)[2 - b], 1, 2 - a, cols),
+                weights[t],
+                NT,
+                preferred_element_type=F32,
+            )
+        else:
+            term = mm(rows_at((lo, raw, hi)[b], 1, a, cols), weights[t])
+        total[...] = total[...] + term if t else term
+    out_ref[...] = total[...].astype(BF16)
+
+
+def conv_scratch(rows, pixels, chans):
+    near = pltpu.VMEM((3, pixels, chans), BF16)
+    return [
+        near,
+        near,
+        near,
+        pltpu.VMEM((3, 4 * rows, chans), BF16),
+        pltpu.VMEM((9, chans, chans), BF16),
+        pltpu.VMEM((pixels, chans), F32),
+        pltpu.SemaphoreType.DMA((3, 9)),
+    ]
+
+
+def finish(*parts):
+    for part in parts:
+        next(part)
+    for part in parts:
+        for _ in part:
+            pass
+
+
+def conv_kernel(rows, back, slots_ref, kernel_ref, *refs):
+    maps, out_ref, scratch = refs[:-8], refs[-8], refs[-7:]
+    feats, grads = (maps[: len(maps) // 2], maps[len(maps) // 2 :]) if back else (maps, None)
+    finish(conv_steps(rows, back, slots_ref, kernel_ref, feats, grads, out_ref, scratch))
+
+
+def convolution(slots, kernel, feats, rows, pixels, grads=()):
+    chans = kernel.shape[1]
+    inputs = [kernel] + feats + list(grads)
     return pl.pallas_call(
-        functools.partial(conv_kernel, rows),
-        out_shape=[block, block],
+        functools.partial(conv_kernel, rows, bool(grads)),
+        out_shape=jax.ShapeDtypeStruct((pixels, chans), BF16),
         in_specs=[SMEM] + [ANY] * len(inputs),
-        out_specs=[VMEM, VMEM],
-        scratch_shapes=[
-            scratch,
-            scratch,
-            scratch,
-            pltpu.VMEM((3, 4 * rows, chans), BF16),
-            pltpu.VMEM((9, chans, chans), BF16),
-            pltpu.VMEM((pixels, chans), F32),
-            pltpu.SemaphoreType.DMA((4, 9)),
-        ],
-        compiler_params=pltpu.CompilerParams(vmem_limit_bytes=20 << 20),
-        cost_estimate=pl.CostEstimate(flops=6 * 10**9, bytes_accessed=8 << 20, transcendentals=0),
-        name="convolutions",
+        out_specs=VMEM,
+        scratch_shapes=conv_scratch(rows, pixels, chans),
+        compiler_params=pltpu.CompilerParams(vmem_limit_bytes=16 << 20),
+        cost_estimate=pl.CostEstimate(flops=4 * 10**9, bytes_accessed=6 << 20, transcendentals=0),
+        name="backward" if grads else "forward",
     )(slots, *placed(inputs))
 
 
-def filter_kernel(group, rows, where_ref, slots_ref, *refs):
-    count = (len(refs) - 9) // 2 - 1
-    feats, grads = refs[: count + 1], refs[count + 1 : 2 * count + 2]
-    keep_ref, give_ref, raw, lo, hi, ends, grad, total, sems = refs[-9:]
+def filter_steps(group, rows, where_ref, slots_ref, feats, grads, outs, scratch):
+    count = len(feats) - 1
+    keep_ref, give_ref = outs
+    raw, lo, hi, ends, grad, total, sems = scratch
     pixels, lanes = raw.shape[1:]
     cols = pixels // rows
     pieces, taps, share, width = keep_ref.shape
@@ -373,6 +390,7 @@
         start_map(feats, i, raw.at[j], sems.at[0], cut)
         start_rest(feats, i, ends.at[j], sems.at[1], cut)
         start_map(grads, i, grad.at[j - 1], sems.at[2])
+    yield
     inside = pl.ds(1, count)
     arrived(raw.at[inside], sems.at[0])
     arrived(ends.at[inside], sems.at[1])
@@ -409,18 +427,23 @@
                 give_ref[i, t] = jnp.where(core == 0, odd, even).astype(BF16)
 
 
+def filter_kernel(rows, where_ref, slots_ref, *refs):
+    maps, outs, scratch = refs[:-9], refs[-9:-7], refs[-7:]
+    feats, grads = maps[: len(maps) // 2], maps[len(maps) // 2 :]
+    finish(filter_steps(GROUP, rows, where_ref, slots_ref, feats, grads, outs, scratch))
+
+
 def filter_terms(where, slots, feats, grads, rows, share, col_count):
     pixels, chans = grads[0].shape
-    count = len(feats) - 1
-    lanes = 128
+    count, lanes = len(feats) - 1, 128
     shape = (col_count // 2, 9, share, chans // col_count)
     window = pltpu.VMEM((count + 2, pixels, lanes), BF16)
     inputs = feats + grads
     return pl.pallas_call(
-        functools.partial(filter_kernel, GROUP, rows),
+        functools.partial(filter_kernel, rows),
         out_shape=[jax.ShapeDtypeStruct(shape, F32), jax.ShapeDtypeStruct(shape, BF16)],
         in_specs=[SMEM, SMEM] + [ANY] * len(inputs),
-        out_specs=[VMEM, VMEM],
+        out_specs=[VMEM] * 2,
         scratch_shapes=[
             window,
             window,
@@ -436,6 +459,37 @@
     )(where, slots, *placed(inputs))
 
 
+def edge_kernel(rows, feat_ref, grad_ref, first_ref, last_ref, maps, sems):
+    cols = maps.shape[1] // rows
+    loads = [
+        pltpu.make_async_copy(ref, maps.at[n], sems.at[n])
+        for n, ref in enumerate((feat_ref, grad_ref))
+    ]
+    for copy in loads:
+        copy.start()
+    for copy in loads:
+        copy.wait()
+    for out, at in ((first_ref, 0), (last_ref, cols - 1)):
+        cells = [
+            maps[n, h * cols + at : h * cols + at + 1, :].astype(F32)
+            for n in range(2)
+            for h in range(rows)
+        ]
+        out[...] = jnp.concatenate(cells, axis=0).astype(BF16)
+
+
+def edges(feat, grad, rows):
+    edge = jax.ShapeDtypeStruct((2 * rows, feat.shape[1]), BF16)
+    return pl.pallas_call(
+        functools.partial(edge_kernel, rows),
+        out_shape=[edge, edge],
+        in_specs=[ANY, ANY],
+        out_specs=[VMEM, VMEM],
+        scratch_shapes=[pltpu.VMEM((2,) + feat.shape, BF16), pltpu.SemaphoreType.DMA((2,))],
+        name="edges",
+    )(*placed([feat, grad]))
+
+
 def ring_row(place, count):
     return jnp.where(place < count // 2, 2 * place, 2 * (count - 1 - place) + 1)
 
@@ -468,26 +522,23 @@
         hop = [(order[i], order[(i + d) % row_count]) for i in range(row_count)]
         return lax.ppermute(value, "rows", hop)
 
+    flat, own_grad = features.reshape(pixels, chans), out_grad.reshape(pixels, chans)
+    first, last = edges(flat, own_grad, rows)
+    near = [lax.ppermute(last, "cols", east), lax.ppermute(first, "cols", west)]
     packed = rank * pixels // chans
-    tail = jnp.concatenate([projector[n : n + packed] for n in range(0, rank, packed)], axis=1)
-    own_grad = out_grad.reshape(pixels, chans)
-    flat = features.reshape(pixels, chans)
-    near = []
-    for at, perm in ((cols - 1, east), (0, west)):
-        edge = jnp.concatenate([x[at : at + pixels - cols + 1 : cols] for x in (flat, own_grad)])
-        near.append(lax.ppermute(edge, "cols", perm))
-    size = pixels + packed
-    message = jnp.pad(jnp.concatenate([flat, tail], axis=0), ((0, 4 * rows), (0, 0)))
-    message = lax.dynamic_update_slice(message, jnp.concatenate(near, axis=0), (size, 0))
+    tail = [projector[n : n + packed] for n in range(0, rank, packed)]
+    message = jnp.concatenate([flat, jnp.concatenate(tail, axis=1)], axis=0)
+    message = jnp.pad(message, ((0, 4 * rows), (0, 0)))
+    message = lax.optimization_barrier(message)
+    grads = {0: own_grad}
+    size = message.shape[0]
+    message = lax.dynamic_update_slice(message, jnp.concatenate(near), (size - 4 * rows, 0))
     feats = {0: message}
     for s in range(1, half_way):
         for d in (1, -1):
             feats[-s * d] = send(feats[(1 - s) * d], d)
-    top, bottom = lax.optimization_barrier((feats[1 - half_way], feats[half_way - 1]))
-    mid = message.shape[0] // 2
-    feats[half_way] = [send(top[:mid], 1), send(bottom[mid:], -1)]
-
-    grads = {0: own_grad}
+    top, bottom = feats[1 - half_way], feats[half_way - 1]
+    feats[half_way] = [send(top[: size // 2], 1), send(bottom[size // 2 :], -1)]
     late_grad = after(own_grad, top, bottom)
     for d in (1, 2):
         grads[-d], grads[d] = send(late_grad, d), send(late_grad, -d)
@@ -527,14 +578,10 @@
     sketch, half = result
     grads = listed(grads, True)
 
-    output, grad_features = convolutions(
-        after(slots, half), kernel, feats, grads, rows
-    )
     share = chans // row_count
-    terms, give = filter_terms(
-        after(where, grad_features), slots, feats, grads, rows, share, col_count
-    )
-    filtered = give
+    output = convolution(after(slots, half), kernel, feats, rows, pixels)
+    terms, give = filter_terms(after(where, output), slots, feats, grads, rows, share, col_count)
+    grad_features = convolution(after(slots, give), kernel, feats, rows, pixels, grads)
     for level in range(levels):
         if level:
             pairs = terms.reshape((-1, 2) + terms.shape[1:])
@@ -543,12 +590,12 @@
             give = lax.dynamic_index_in_dim(pairs, 1 - bit, 1, keepdims=False).astype(BF16)
         got = swap(give, level)
         if level < levels - 1:
-            terms = terms + got.astype(F32)
+            terms = terms + after(got, grad_features).astype(F32)
 
     for level in range(1, levels):
         mine = swap(half, level)
         if level == 1:
-            mine = after(mine, filtered)
+            mine = after(mine, grad_features)
         others = [mine, swap(mine, 0)]
         final = level == levels - 1
         share = (rank // col_count, sketch.shape[1] // row_count) if final else None

time: 117 us -> 113 us (0.966)
  waiting for transfers between devices: 32.9 us -> 24.8 us
  Pallas kernels: 44.7 us -> 48.8 us
  starting transfers between devices: 26.4 us -> 30.4 us
  local copies, waits for them, and re-layouts: 7.79 us -> 4.84 us
    ppermute x16, waiting for transfers between devices: 30.8 us -> 24.8 us  [send(): return lax.ppermute(value, 'rows', hop)]
    pallas_call x2 -> x4, Pallas kernels: 11.5 us -> 16.2 us  [the longest x2 9.4 us: convolution(): pl.pallas_call(functools.partial(conv_kernel, rows, bool(grads)), out_sha...]
    slice x7 -> x3, local copies, waits for them, and re-layouts: 4.75 us -> 0.81 us  [the longest x1 0.78 us: body(): tail = [projector[n:n + packed] for n in range(0, rank, packed)]]
    ppermute x16, starting transfers between devices: 20.9 us -> 23.1 us  [send(): return lax.ppermute(value, 'rows', hop)]
    ppermute x5, waiting for transfers between devices: 2 us -> 0.01 us  [swap(): lax.ppermute(value, 'cols', [(i, i ^ 1 << level) for i in range(col_count)])]
    ppermute x5, starting transfers between devices: 1.2 us -> 2.75 us  [swap(): lax.ppermute(value, 'cols', [(i, i ^ 1 << level) for i in range(col_count)])]
    unnamed x41 -> x39, local copies, waits for them, and re-layouts: 2.86 us -> 2.92 us
  transfers between devices with their start and end apart: 23 -> 23, of which waited for: 10 -> 4; matrix products, arithmetic and copies ran while one was open for 3% -> 4% of each run, Pallas kernels for 39% -> 42%
where the time goes in v2:
time: 113 us
  Pallas kernels  48.8 us (43%)
  starting transfers between devices  30.4 us (27%)
  waiting for transfers between devices  24.8 us (22%)
  local copies, waits for them, and re-layouts  4.84 us (4%)
  other arithmetic  2.83 us (3%)
  between operations  1.17 us (1%)
    ppermute x16, waiting for transfers between devices, send(): return lax.ppermute(value, 'rows', hop)  24.8 us
    ppermute x16, starting transfers between devices, send(): return lax.ppermute(value, 'rows', hop)  23.1 us
    pallas_call x1, Pallas kernels, row_tree(): pl.pallas_call(functools.partial(row_tree_kernel, first, 1536, rows), out...  22.2 us
    pallas_call x2, Pallas kernels, merge(): pl.pallas_call(functools.partial(merge_kernel, 1152, len(others) == 2, sh...  10.4 us
    pallas_call x2, Pallas kernels, convolution(): pl.pallas_call(functools.partial(conv_kernel, rows, bool(grads)), out_sha...  9.4 us
    pallas_call x1, Pallas kernels, filter_terms(): pl.pallas_call(functools.partial(filter_kernel, rows), out_shape=[jax.Sha...  5.06 us
    ppermute x2, starting transfers between devices, body(): near = [lax.ppermute(last, 'cols', east), lax.ppermute(first, 'cols', west)]  4.45 us
    unnamed x39, local copies, waits for them, and re-layouts  2.92 us
  transfers between devices with their start and end apart: 23, of which 4 were waited for; matrix products, arithmetic and copies ran while one was open for 4% of the time, Pallas kernels for 42%

profile of v2, /device:TPU:0, one launch (start us, length us, event | category | flops | bytes accessed | tf_op | source)
XLA Modules:
  0.0 112.8 jit_solution(3721967767808737255)
XLA Ops:
  0.6 1.7 %edges.1 = (bf16[16,512]{1,0:T(8,128)(2,1)}, bf16[16,512]{1,0:T(8,128)(2,1)}) custom-call(bf16[256,512]{1,0:T(8,128)(2,1)} %bitcast.23, bf16[256,512]{1,0:T(8,128)(2,1)} %bitcast.25), custom_call_target="tpu_custom_call" | custom-call | tf_op jit(solution)/shard_map/edges/pallas_call | solution.py:483
  2.4 1.4 %collective-permute-start.1 = (bf16[16,512]{1,0:T(8,128)(2,1)}, bf16[16,512]{1,0:T(8,128)(2,1)S(1)}, u32[]{:S(2)}, u32[]{:S(2)}) collective-permute-start(bf16[16,512]{1,0:T(8,128)(2,1)} %get-tuple-element.45), channel_id=1, source_target_pairs={{1,0},{2,1},{3,2},{5,4},{6,5},{7,6},{9,8},{10,9},{11,10},{13,12},{... | collective-permute-start | bytes 49160 | tf_op jit(solution)/shard_map/ppermute | solution.py:527
  3.8 3.0 %collective-permute-start = (bf16[16,512]{1,0:T(8,128)(2,1)}, bf16[16,512]{1,0:T(8,128)(2,1)S(1)}, u32[]{:S(2)}, u32[]{:S(2)}) collective-permute-start(bf16[16,512]{1,0:T(8,128)(2,1)} %get-tuple-element.44), channel_id=1, source_target_pairs={{0,1},{1,2},{2,3},{4,5},{5,6},{6,7},{8,9},{9,10},{10,11},{12,13},{... | collective-permute-start | bytes 49160 | tf_op jit(solution)/shard_map/ppermute | solution.py:527
  7.7 1.0 fusion.3
  8.7 3.1 %collective-permute-start.2 = (bf16[352,512]{1,0:T(8,128)(2,1)S(1)}, bf16[352,512]{1,0:T(8,128)(2,1)S(1)}, u32[]{:S(2)}, u32[]{:S(2)}) collective-permute-start(bf16[352,512]{1,0:T(8,128)(2,1)S(1)} %maximum_dynamic-update-slice_fusion.refs_0_), channel_id=1, source_target_pairs={{0,8},{8,16},{16,24},{24,28},{28,20},{20,12},{12,4},{4,0},{1,9},{9... | collective-permute-start | bytes 1081352 | tf_op jit(solution)/shard_map/ppermute | solution.py:523
  11.8 8.6 %collective-permute-done.2.refs_1_ = bf16[352,512]{1,0:T(8,128)(2,1)S(1)} collective-permute-done((bf16[352,512]{1,0:T(8,128)(2,1)S(1)}, bf16[352,512]{1,0:T(8,128)(2,1)S(1)}, u32[]{:S(2)}, u32[]{:S(2)}) %collective-permute-start.2) | collective-permute-done | bytes 360480 | tf_op jit(solution)/shard_map/ppermute | solution.py:523
  20.4 2.5 %collective-permute-start.4 = (bf16[352,512]{1,0:T(8,128)(2,1)S(1)}, bf16[352,512]{1,0:T(8,128)(2,1)S(1)}, u32[]{:S(2)}, u32[]{:S(2)}) collective-permute-start(bf16[352,512]{1,0:T(8,128)(2,1)S(1)} %collective-permute-done.2.refs_1_), channel_id=1, source_target_pairs={{0,8},{8,16},{16,24},{24,28},{28,20},{20,12},{12,4},{4,0},{1,9},{9... | collective-permute-start | bytes 1081352 | tf_op jit(solution)/shard_map/ppermute | solution.py:523
  22.9 8.5 %collective-permute-done.4.refs_3_ = bf16[352,512]{1,0:T(8,128)(2,1)S(1)} collective-permute-done((bf16[352,512]{1,0:T(8,128)(2,1)S(1)}, bf16[352,512]{1,0:T(8,128)(2,1)S(1)}, u32[]{:S(2)}, u32[]{:S(2)}) %collective-permute-start.4) | collective-permute-done | bytes 360480 | tf_op jit(solution)/shard_map/ppermute | solution.py:523
  31.5 2.0 %collective-permute-start.6 = (bf16[352,512]{1,0:T(8,128)(2,1)S(1)}, bf16[352,512]{1,0:T(8,128)(2,1)S(1)}, u32[]{:S(2)}, u32[]{:S(2)}) collective-permute-start(bf16[352,512]{1,0:T(8,128)(2,1)S(1)} %collective-permute-done.4.refs_3_), channel_id=1, source_target_pairs={{0,8},{8,16},{16,24},{24,28},{28,20},{20,12},{12,4},{4,0},{1,9},{9... | collective-permute-start | bytes 1081352 | tf_op jit(solution)/shard_map/ppermute | solution.py:523
  33.8 7.6 %collective-permute-done.6.refs_5_ = bf16[352,512]{1,0:T(8,128)(2,1)S(1)} collective-permute-done((bf16[352,512]{1,0:T(8,128)(2,1)S(1)}, bf16[352,512]{1,0:T(8,128)(2,1)S(1)}, u32[]{:S(2)}, u32[]{:S(2)}) %collective-permute-start.6) | collective-permute-done | bytes 360480 | tf_op jit(solution)/shard_map/ppermute | solution.py:523
  41.4 1.9 %collective-permute-start.8 = (bf16[176,512]{1,0:T(8,128)(2,1)S(1)}, bf16[176,512]{1,0:T(8,128)(2,1)S(1)}, u32[]{:S(2)}, u32[]{:S(2)}) collective-permute-start(bf16[176,512]{1,0:T(8,128)(2,1)S(1)} %slice.52), channel_id=1, source_target_pairs={{0,8},{8,16},{16,24},{24,28},{28,20},{20,12},{12,4},{4,0},{1,9},{9... | collective-permute-start | bytes 540680 | tf_op jit(solution)/shard_map/ppermute | solution.py:523
  43.6 1.7 %collective-permute-start.10 = (bf16[256,512]{1,0:T(8,128)(2,1)S(1)}, bf16[256,512]{1,0:T(8,128)(2,1)S(1)}, u32[]{:S(2)}, u32[]{:S(2)}) collective-permute-start(bf16[256,512]{1,0:T(8,128)(2,1)S(1)} %bitcast.28), channel_id=1, source_target_pairs={{0,4},{8,0},{16,8},{24,16},{28,24},{20,28},{12,20},{4,12},{1,5},{9... | collective-permute-start | bytes 786440 | tf_op jit(solution)/shard_map/ppermute | solution.py:523
  45.7 2.8 %collective-permute-start.12 = (bf16[256,512]{1,0:T(8,128)(2,1)S(1)}, bf16[256,512]{1,0:T(8,128)(2,1)}, u32[]{:S(2)}, u32[]{:S(2)}) collective-permute-start(bf16[256,512]{1,0:T(8,128)(2,1)S(1)} %bitcast.30), channel_id=1, source_target_pairs={{0,12},{8,4},{16,0},{24,8},{28,16},{20,24},{12,28},{4,20},{1,13},{... | collective-permute-start | bytes 786440 | tf_op jit(solution)/shard_map/ppermute | solution.py:523
  48.5 3.4 %collective-permute-start.13 = (bf16[256,512]{1,0:T(8,128)(2,1)S(1)}, bf16[256,512]{1,0:T(8,128)(2,1)S(1)}, u32[]{:S(2)}, u32[]{:S(2)}) collective-permute-start(bf16[256,512]{1,0:T(8,128)(2,1)S(1)} %bitcast.31), channel_id=1, source_target_pairs={{0,16},{8,24},{16,28},{24,20},{28,12},{20,4},{12,0},{4,8},{1,17},{... | collective-permute-start | bytes 786440 | tf_op jit(solution)/shard_map/ppermute | solution.py:523
  52.5 22.2 %row_tree.1.refs_0_ = bf16[128,4608]{1,0:T(8,128)(2,1)S(1)} custom-call(s32[8]{0:T(128)S(1)} %stack.48.rows_ref.slots_ref, bf16[128,256]{1,0:T(8,128)(2,1)S(1)} %get-tuple-element.60.mix_ref, bf16[352,512]{1,0:T(8,128)(2,1)} %copy-done.1, bf16[352,512]{1,0:T(8,128)(2,1)} %copy-done.7, bf16[352,512]{1,0:T(8,128)(2,1)} %copy-done.8, ...), custom_call_target="tpu_custom_call" | custom-call | flops 20000000000 | bytes 8388608 | tf_op jit(solution)/shard_map/row_tree/pallas_call | solution.py:186
  75.6 1.9 %collective-permute-start.15 = (bf16[256,512]{1,0:T(8,128)(2,1)S(1)}, bf16[256,512]{1,0:T(8,128)(2,1)S(1)}, u32[]{:S(2)}, u32[]{:S(2)}) collective-permute-start(bf16[256,512]{1,0:T(8,128)(2,1)S(1)} %collective-permute-done.13.refs_12_), channel_id=1, source_target_pairs={{0,8},{8,16},{16,24},{24,28},{28,20},{20,12},{12,4},{4,0},{1,9},{9... | collective-permute-start | bytes 786440 | tf_op jit(solution)/shard_map/ppermute | solution.py:523
  78.7 3.0 %collective-permute-start.17 = (bf16[128,512]{1,0:T(8,128)(2,1)S(1)}, bf16[128,512]{1,0:T(8,128)(2,1)S(1)}, u32[]{:S(2)}, u32[]{:S(2)}) collective-permute-start(bf16[128,512]{1,0:T(8,128)(2,1)S(1)} %slice.50), channel_id=1, source_target_pairs={{0,16},{8,24},{16,28},{24,20},{28,12},{20,4},{12,0},{4,8},{1,17},{... | collective-permute-start | bytes 393224 | tf_op jit(solution)/shard_map/ppermute | solution.py:523
  81.7 5.7 %merge.2 = (bf16[128,4608]{1,0:T(8,128)(2,1)}, bf16[128,2304]{1,0:T(8,128)(2,1)S(1)}) custom-call(s32[4]{0:T(128)S(1)} %constant_dynamic-update-slice_fusion.1.where_ref, bf16[128,256]{1,0:T(8,128)(2,1)S(1)} %get-tuple-element.61.mix_ref, bf16[128,4608]{1,0:T(8,128)(2,1)S(1)} %row_tree.1.refs_0_, bf16[128,4608]{1,0:T(8,128)(2,1)S(1)} %collective-permute-done.14.refs_1_), custom_call_target="tpu_custom_call" | custom-call | flops 4000000000 | bytes 4194304 | tf_op jit(solution)/shard_map/merge/pallas_call | solution.py:269
  87.5 4.5 %forward.1 = bf16[256,512]{1,0:T(8,128)(2,1)} custom-call(s32[8]{0:T(128)S(1)} %stack.48.rows_ref.slots_ref, bf16[4608,512]{1,0:T(8,128)(2,1)} %kernel_ref.3, bf16[352,512]{1,0:T(8,128)(2,1)} %copy-done.1, bf16[352,512]{1,0:T(8,128)(2,1)} %copy-done.7, bf16[352,512]{1,0:T(8,128)(2,1)} %copy-done.8, bf16[352,512]{1,0:T(8,128)(2,1)} %copy-done.9, ...), custom_call_target="tpu_custom_call" | custom-call | flops 4000000000 | bytes 6291456 | tf_op jit(solution)/shard_map/forward/pallas_call | solution.py:364
  93.6 5.1 %filter_terms.1 = (f32[2,9,64,128]{3,2,1,0:T(8,128)S(1)}, bf16[2,9,64,128]{3,2,1,0:T(8,128)(2,1)S(1)}) custom-call(s32[4]{0:T(128)S(1)} %pad_add_fusion.where_ref, s32[8]{0:T(128)S(1)} %stack.48.rows_ref.slots_ref, bf16[352,512]{1,0:T(8,128)(2,1)} %copy-done.1, bf16[352,512]{1,0:T(8,128)(2,1)} %copy-done.7, bf16[352,512]{1,0:T(8,128)(2,1)} %copy-done.8, ...), custom_call_target="tpu_custom_call" | custom-call | flops 5000000000 | bytes 4194304 | tf_op jit(solution)/shard_map/filter_terms/pallas_call | solution.py:442
  98.7 4.9 %backward.1 = bf16[256,512]{1,0:T(8,128)(2,1)} custom-call(s32[8]{0:T(128)S(1)} %stack.48.rows_ref.slots_ref, bf16[4608,512]{1,0:T(8,128)(2,1)} %kernel_ref.3, bf16[352,512]{1,0:T(8,128)(2,1)} %copy-done.1, bf16[352,512]{1,0:T(8,128)(2,1)} %copy-done.7, bf16[352,512]{1,0:T(8,128)(2,1)} %copy-done.8, bf16[352,512]{1,0:T(8,128)(2,1)} %copy-done.9, ...), custom_call_target="tpu_custom_call" | custom-call | flops 4000000000 | bytes 6291456 | tf_op jit(solution)/shard_map/backward/pallas_call | solution.py:364
  104.2 1.0 convert_add_fusion
  105.3 2.1 %collective-permute-start.20 = (bf16[1,9,64,128]{3,2,1,0:T(8,128)(2,1)S(1)}, bf16[1,9,64,128]{3,2,1,0:T(8,128)(2,1)S(1)}, u32[]{:S(2)}, u32[]{:S(2)}) collective-permute-start(bf16[1,9,64,128]{3,2,1,0:T(8,128)(2,1)S(1)} %dynamic-slice_convert_fusion), channel_id=1, source_target_pairs={{0,2},{1,3},{2,0},{3,1},{4,6},{5,7},{6,4},{7,5},{8,10},{9,11},{10,... | collective-permute-start | bytes 442376 | tf_op jit(solution)/shard_map/ppermute | solution.py:564
  107.3 4.7 %merge.3 = bf16[32,576]{1,0:T(8,128)(2,1)} custom-call(s32[4]{0:T(128)S(1)} %constant_dynamic-update-slice_fusion.where_ref, bf16[128,256]{1,0:T(8,128)(2,1)S(1)} %get-tuple-element.61.mix_ref, bf16[128,4608]{1,0:T(8,128)(2,1)S(1)} %copy-done, bf16[128,2304]{1,0:T(8,128)(2,1)S(1)} %collective-permute-done.21.refs_1_, ...), custom_call_target="tpu_custom_call" | custom-call | flops 4000000000 | bytes 4194304 | tf_op jit(solution)/shard_map/merge/pallas_call | solution.py:269
  (83 shorter events, 7.4 us)
Async XLA Ops:
  2.4 6.2 %collective-permute-start.1 = (bf16[16,512]{1,0:T(8,128)(2,1)}, bf16[16,512]{1,0:T(8,128)(2,1)S(1)}, u32[]{:S(2)}, u32[]{:S(2)}) collective-permute-start(bf16[16,512]{1,0:T(8,128)(2,1)} %get-tuple-element.45), channel_id=1, source_target_pairs={{1,0},{2,1},{3,2},{5,4},{6,5},{7,6},{9,8},{10,9},{11,10},{13,12},{... | collective-permute-start | bytes 49160 | tf_op jit(solution)/shard_map/ppermute | solution.py:527
  3.8 4.8 %collective-permute-start = (bf16[16,512]{1,0:T(8,128)(2,1)}, bf16[16,512]{1,0:T(8,128)(2,1)S(1)}, u32[]{:S(2)}, u32[]{:S(2)}) collective-permute-start(bf16[16,512]{1,0:T(8,128)(2,1)} %get-tuple-element.44), channel_id=1, source_target_pairs={{0,1},{1,2},{2,3},{4,5},{5,6},{6,7},{8,9},{9,10},{10,11},{12,13},{... | collective-permute-start | bytes 49160 | tf_op jit(solution)/shard_map/ppermute | solution.py:527
  8.7 43.2 %copy-start.1 = (bf16[352,512]{1,0:T(8,128)(2,1)}, bf16[352,512]{1,0:T(8,128)(2,1)S(1)}, u32[]{:S(2)}) copy-start(bf16[352,512]{1,0:T(8,128)(2,1)S(1)} %maximum_dynamic-update-slice_fusion.refs_0_) | copy-start | bytes 1081348
  8.7 11.7 %collective-permute-start.2 = (bf16[352,512]{1,0:T(8,128)(2,1)S(1)}, bf16[352,512]{1,0:T(8,128)(2,1)S(1)}, u32[]{:S(2)}, u32[]{:S(2)}) collective-permute-start(bf16[352,512]{1,0:T(8,128)(2,1)S(1)} %maximum_dynamic-update-slice_fusion.refs_0_), channel_id=1, source_target_pairs={{0,8},{8,16},{16,24},{24,28},{28,20},{20,12},{12,4},{4,0},{1,9},{9... | collective-permute-start | bytes 1081352 | tf_op jit(solution)/shard_map/ppermute | solution.py:523
  11.7 11.2 %collective-permute-start.3 = (bf16[352,512]{1,0:T(8,128)(2,1)S(1)}, bf16[352,512]{1,0:T(8,128)(2,1)S(1)}, u32[]{:S(2)}, u32[]{:S(2)}) collective-permute-start(bf16[352,512]{1,0:T(8,128)(2,1)S(1)} %maximum_dynamic-update-slice_fusion.refs_0_), channel_id=1, source_target_pairs={{0,4},{8,0},{16,8},{24,16},{28,24},{20,28},{12,20},{4,12},{1,5},{9... | collective-permute-start | bytes 1081352 | tf_op jit(solution)/shard_map/ppermute | solution.py:523
  20.4 11.1 %collective-permute-start.4 = (bf16[352,512]{1,0:T(8,128)(2,1)S(1)}, bf16[352,512]{1,0:T(8,128)(2,1)S(1)}, u32[]{:S(2)}, u32[]{:S(2)}) collective-permute-start(bf16[352,512]{1,0:T(8,128)(2,1)S(1)} %collective-permute-done.2.refs_1_), channel_id=1, source_target_pairs={{0,8},{8,16},{16,24},{24,28},{28,20},{20,12},{12,4},{4,0},{1,9},{9... | collective-permute-start | bytes 1081352 | tf_op jit(solution)/shard_map/ppermute | solution.py:523
  22.9 10.6 %collective-permute-start.5 = (bf16[352,512]{1,0:T(8,128)(2,1)S(1)}, bf16[352,512]{1,0:T(8,128)(2,1)S(1)}, u32[]{:S(2)}, u32[]{:S(2)}) collective-permute-start(bf16[352,512]{1,0:T(8,128)(2,1)S(1)} %collective-permute-done.3.refs_2_), channel_id=1, source_target_pairs={{0,4},{8,0},{16,8},{24,16},{28,24},{20,28},{12,20},{4,12},{1,5},{9... | collective-permute-start | bytes 1081352 | tf_op jit(solution)/shard_map/ppermute | solution.py:523
  31.5 9.9 %collective-permute-start.6 = (bf16[352,512]{1,0:T(8,128)(2,1)S(1)}, bf16[352,512]{1,0:T(8,128)(2,1)S(1)}, u32[]{:S(2)}, u32[]{:S(2)}) collective-permute-start(bf16[352,512]{1,0:T(8,128)(2,1)S(1)} %collective-permute-done.4.refs_3_), channel_id=1, source_target_pairs={{0,8},{8,16},{16,24},{24,28},{28,20},{20,12},{12,4},{4,0},{1,9},{9... | collective-permute-start | bytes 1081352 | tf_op jit(solution)/shard_map/ppermute | solution.py:523
  33.5 9.9 %collective-permute-start.7 = (bf16[352,512]{1,0:T(8,128)(2,1)S(1)}, bf16[352,512]{1,0:T(8,128)(2,1)S(1)}, u32[]{:S(2)}, u32[]{:S(2)}) collective-permute-start(bf16[352,512]{1,0:T(8,128)(2,1)S(1)} %collective-permute-done.5.refs_4_), channel_id=1, source_target_pairs={{0,4},{8,0},{16,8},{24,16},{28,24},{20,28},{12,20},{4,12},{1,5},{9... | collective-permute-start | bytes 1081352 | tf_op jit(solution)/shard_map/ppermute | solution.py:523
  41.4 7.1 %collective-permute-start.8 = (bf16[176,512]{1,0:T(8,128)(2,1)S(1)}, bf16[176,512]{1,0:T(8,128)(2,1)S(1)}, u32[]{:S(2)}, u32[]{:S(2)}) collective-permute-start(bf16[176,512]{1,0:T(8,128)(2,1)S(1)} %slice.52), channel_id=1, source_target_pairs={{0,8},{8,16},{16,24},{24,28},{28,20},{20,12},{12,4},{4,0},{1,9},{9... | collective-permute-start | bytes 540680 | tf_op jit(solution)/shard_map/ppermute | solution.py:523
  43.4 8.5 %collective-permute-start.9 = (bf16[176,512]{1,0:T(8,128)(2,1)S(1)}, bf16[176,512]{1,0:T(8,128)(2,1)S(1)}, u32[]{:S(2)}, u32[]{:S(2)}) collective-permute-start(bf16[176,512]{1,0:T(8,128)(2,1)S(1)} %slice.53), channel_id=1, source_target_pairs={{0,4},{8,0},{16,8},{24,16},{28,24},{20,28},{12,20},{4,12},{1,5},{9... | collective-permute-start | bytes 540680 | tf_op jit(solution)/shard_map/ppermute | solution.py:523
  43.6 31.1 %collective-permute-start.10 = (bf16[256,512]{1,0:T(8,128)(2,1)S(1)}, bf16[256,512]{1,0:T(8,128)(2,1)S(1)}, u32[]{:S(2)}, u32[]{:S(2)}) collective-permute-start(bf16[256,512]{1,0:T(8,128)(2,1)S(1)} %bitcast.28), channel_id=1, source_target_pairs={{0,4},{8,0},{16,8},{24,16},{28,24},{20,28},{12,20},{4,12},{1,5},{9... | collective-permute-start | bytes 786440 | tf_op jit(solution)/shard_map/ppermute | solution.py:523
  45.3 29.5 %collective-permute-start.11 = (bf16[256,512]{1,0:T(8,128)(2,1)S(1)}, bf16[256,512]{1,0:T(8,128)(2,1)S(1)}, u32[]{:S(2)}, u32[]{:S(2)}) collective-permute-start(bf16[256,512]{1,0:T(8,128)(2,1)S(1)} %bitcast.29), channel_id=1, source_target_pairs={{0,8},{8,16},{16,24},{24,28},{28,20},{20,12},{12,4},{4,0},{1,9},{9... | collective-permute-start | bytes 786440 | tf_op jit(solution)/shard_map/ppermute | solution.py:523
  45.7 29.1 %collective-permute-start.12 = (bf16[256,512]{1,0:T(8,128)(2,1)S(1)}, bf16[256,512]{1,0:T(8,128)(2,1)}, u32[]{:S(2)}, u32[]{:S(2)}) collective-permute-start(bf16[256,512]{1,0:T(8,128)(2,1)S(1)} %bitcast.30), channel_id=1, source_target_pairs={{0,12},{8,4},{16,0},{24,8},{28,16},{20,24},{12,28},{4,20},{1,13},{... | collective-permute-start | bytes 786440 | tf_op jit(solution)/shard_map/ppermute | solution.py:523
  48.5 26.3 %collective-permute-start.13 = (bf16[256,512]{1,0:T(8,128)(2,1)S(1)}, bf16[256,512]{1,0:T(8,128)(2,1)S(1)}, u32[]{:S(2)}, u32[]{:S(2)}) collective-permute-start(bf16[256,512]{1,0:T(8,128)(2,1)S(1)} %bitcast.31), channel_id=1, source_target_pairs={{0,16},{8,24},{16,28},{24,20},{28,12},{20,4},{12,0},{4,8},{1,17},{... | collective-permute-start | bytes 786440 | tf_op jit(solution)/shard_map/ppermute | solution.py:523
  75.5 6.2 %collective-permute-start.14 = (bf16[128,4608]{1,0:T(8,128)(2,1)S(1)}, bf16[128,4608]{1,0:T(8,128)(2,1)S(1)}, u32[]{:S(2)}, u32[]{:S(2)}) collective-permute-start(bf16[128,4608]{1,0:T(8,128)(2,1)S(1)} %row_tree.1.refs_0_), channel_id=1, source_target_pairs={{0,1},{1,0},{2,3},{3,2},{4,5},{5,4},{6,7},{7,6},{8,9},{9,8},{10,11... | collective-permute-start | bytes 3538952 | tf_op jit(solution)/shard_map/ppermute | solution.py:564
  75.6 16.4 %collective-permute-start.15 = (bf16[256,512]{1,0:T(8,128)(2,1)S(1)}, bf16[256,512]{1,0:T(8,128)(2,1)S(1)}, u32[]{:S(2)}, u32[]{:S(2)}) collective-permute-start(bf16[256,512]{1,0:T(8,128)(2,1)S(1)} %collective-permute-done.13.refs_12_), channel_id=1, source_target_pairs={{0,8},{8,16},{16,24},{24,28},{28,20},{20,12},{12,4},{4,0},{1,9},{9... | collective-permute-start | bytes 786440 | tf_op jit(solution)/shard_map/ppermute | solution.py:523
  77.5 14.6 %collective-permute-start.16 = (bf16[256,512]{1,0:T(8,128)(2,1)}, bf16[256,512]{1,0:T(8,128)(2,1)S(1)}, u32[]{:S(2)}, u32[]{:S(2)}) collective-permute-start(bf16[256,512]{1,0:T(8,128)(2,1)} %collective-permute-done.12.refs_13_), channel_id=1, source_target_pairs={{0,4},{8,0},{16,8},{24,16},{28,24},{20,28},{12,20},{4,12},{1,5},{9... | collective-permute-start | bytes 786440 | tf_op jit(solution)/shard_map/ppermute | solution.py:523
  78.7 13.3 %collective-permute-start.17 = (bf16[128,512]{1,0:T(8,128)(2,1)S(1)}, bf16[128,512]{1,0:T(8,128)(2,1)S(1)}, u32[]{:S(2)}, u32[]{:S(2)}) collective-permute-start(bf16[128,512]{1,0:T(8,128)(2,1)S(1)} %slice.50), channel_id=1, source_target_pairs={{0,16},{8,24},{16,28},{24,20},{28,12},{20,4},{12,0},{4,8},{1,17},{... | collective-permute-start | bytes 393224 | tf_op jit(solution)/shard_map/ppermute | solution.py:523
  81.7 10.3 %collective-permute-start.18 = (bf16[128,512]{1,0:T(8,128)(2,1)S(1)}, bf16[128,512]{1,0:T(8,128)(2,1)S(1)}, u32[]{:S(2)}, u32[]{:S(2)}) collective-permute-start(bf16[128,512]{1,0:T(8,128)(2,1)S(1)} %slice.51), channel_id=1, source_target_pairs={{0,12},{8,4},{16,0},{24,8},{28,16},{20,24},{12,28},{4,20},{1,13},{... | collective-permute-start | bytes 393224 | tf_op jit(solution)/shard_map/ppermute | solution.py:523
  87.4 16.2 %collective-permute-start.21 = (bf16[128,2304]{1,0:T(8,128)(2,1)S(1)}, bf16[128,2304]{1,0:T(8,128)(2,1)S(1)}, u32[]{:S(2)}, u32[]{:S(2)}) collective-permute-start(bf16[128,2304]{1,0:T(8,128)(2,1)S(1)} %get-tuple-element.48), channel_id=1, source_target_pairs={{0,2},{1,3},{2,0},{3,1},{4,6},{5,7},{6,4},{7,5},{8,10},{9,11},{10,... | collective-permute-start | bytes 1769480 | tf_op jit(solution)/shard_map/ppermute | solution.py:564
  98.7 5.5 %collective-permute-start.19 = (bf16[2,9,64,128]{3,2,1,0:T(8,128)(2,1)S(1)}, bf16[2,9,64,128]{3,2,1,0:T(8,128)(2,1)}, u32[]{:S(2)}, u32[]{:S(2)}) collective-permute-start(bf16[2,9,64,128]{3,2,1,0:T(8,128)(2,1)S(1)} %get-tuple-element.53), channel_id=1, source_target_pairs={{0,1},{1,0},{2,3},{3,2},{4,5},{5,4},{6,7},{7,6},{8,9},{9,8},{10,11... | collective-permute-start | bytes 884744 | tf_op jit(solution)/shard_map/ppermute | solution.py:564
  103.6 3.7 %collective-permute-start.22 = (bf16[128,2304]{1,0:T(8,128)(2,1)S(1)}, bf16[128,2304]{1,0:T(8,128)(2,1)S(1)}, u32[]{:S(2)}, u32[]{:S(2)}) collective-permute-start(bf16[128,2304]{1,0:T(8,128)(2,1)S(1)} %collective-permute-done.21.refs_1_), channel_id=1, source_target_pairs={{0,1},{1,0},{2,3},{3,2},{4,5},{5,4},{6,7},{7,6},{8,9},{9,8},{10,11... | collective-permute-start | bytes 1769480 | tf_op jit(solution)/shard_map/ppermute | solution.py:564
  105.3 6.8 %collective-permute-start.20 = (bf16[1,9,64,128]{3,2,1,0:T(8,128)(2,1)S(1)}, bf16[1,9,64,128]{3,2,1,0:T(8,128)(2,1)S(1)}, u32[]{:S(2)}, u32[]{:S(2)}) collective-permute-start(bf16[1,9,64,128]{3,2,1,0:T(8,128)(2,1)S(1)} %dynamic-slice_convert_fusion), channel_id=1, source_target_pairs={{0,2},{1,3},{2,0},{3,1},{4,6},{5,7},{6,4},{7,5},{8,10},{9,11},{10,... | collective-permute-start | bytes 442376 | tf_op jit(solution)/shard_map/ppermute | solution.py:564
  (18 other events, 199.4 us)

commit v3 on v2

--- a/solution.py
+++ b/solution.py
@@ -74,11 +74,10 @@
     return jnp.concatenate([src[j, cols:size], src[j + 1, :cols]], axis=0)
 
 
-def shift_row(raw, lo, hi, h, cols, side, n=0):
-    rows = side.shape[0] // 4
+def shift_row(raw, lo, hi, h, cols, side):
+    rows = side.shape[0] // 2
     at = slice(h * cols, (h + 1) * cols)
-    left, right = n * rows + h, (2 + n) * rows + h
-    lo[at], hi[at] = shifted(raw[at], side[left : left + 1], side[right : right + 1])
+    lo[at], hi[at] = shifted(raw[at], side[h : h + 1], side[rows + h : rows + h + 1])
 
 
 def placed(values):
@@ -90,7 +89,7 @@
     if i < len(refs) - 2:
         pltpu.make_async_copy(refs[i].at[pl.ds(0, size), cut], target, sem).start()
     else:
-        mid = refs[-1].shape[0]
+        mid = refs[-2].shape[0]
         pltpu.make_async_copy(refs[-2].at[:, cut], target.at[pl.ds(0, mid)], sem).start()
         pltpu.make_async_copy(refs[-1].at[pl.ds(0, size - mid), cut], target.at[pl.ds(mid, size - mid)], sem).start()
 
@@ -192,7 +191,7 @@
             maps,
             maps,
             maps,
-            pltpu.VMEM((blocks, 4 * rows, chans), BF16),
+            pltpu.VMEM((blocks, 2 * rows, chans), BF16),
             pltpu.VMEM((blocks, rank, pixels), BF16),
             pltpu.VMEM((GROUP // 2, 2 * rank, width), BF16),
             pltpu.SemaphoreType.DMA((3, blocks)),
@@ -278,105 +277,100 @@
     )(where, mix, own, *others)
 
 
-def conv_steps(rows, back, slots_ref, kernel_ref, feats, grads, out_ref, scratch):
-    count = len(feats) - 1
-    raw, lo, hi, ends, weights, total, sems = scratch
-    pixels, chans = raw.shape[1:]
-    cols = pixels // rows
-    row = slots_ref[0]
-    for i in range(count):
-        j = slots_ref[i] - row + 1
-
-        @pl.when((j >= 0) & (j < 3))
-        def fetch(i=i, j=j):
-            start_map(grads if back else feats, i, raw.at[j], sems.at[0, j])
-            start_rest(feats, i, ends.at[j], sems.at[1, j])
-
+def start_weights(kernel_ref, weights, sems):
+    chans = weights.shape[1]
     for t in range(9):
         pltpu.make_async_copy(
-            kernel_ref.at[pl.ds(t * chans, chans)], weights.at[t], sems.at[2, t]
+            kernel_ref.at[pl.ds(t * chans, chans)], weights.at[t], sems.at[t]
         ).start()
-    yield
-
-    def waits(j):
-        arrived(raw.at[j], sems.at[0, j])
-        arrived(ends.at[j], sems.at[1, j])
-
-    for j, inside in ((0, row > 0), (2, row < count - 1)):
-
-        @pl.when(jnp.logical_not(inside))
-        def clear(j=j):
-            raw[j] = jnp.zeros((pixels, chans), BF16)
-            ends[j] = jnp.zeros(ends.shape[1:], BF16)
-
-        pl.when(inside)(functools.partial(waits, j))
-    waits(1)
-    sides = [ends[j].astype(F32) for j in range(3)]
-    for k in range(rows - 1, 2 * rows + 1):
-        j, h = divmod(k, rows)
-        shift_row(raw.at[j], lo.at[j], hi.at[j], h, cols, sides[j], int(back))
+
+
+def tap_sums(patch, weights, sems, totals):
     for t in range(9):
-        a, b = divmod(t, 3)
-        arrived(weights.at[t], sems.at[2, t])
-        if back:
-            term = lax.dot_general(
-                rows_at((lo, raw, hi)[2 - b], 1, 2 - a, cols),
-                weights[t],
-                NT,
-                preferred_element_type=F32,
-            )
-        else:
-            term = mm(rows_at((lo, raw, hi)[b], 1, a, cols), weights[t])
-        total[...] = total[...] + term if t else term
-    out_ref[...] = total[...].astype(BF16)
-
-
-def conv_scratch(rows, pixels, chans):
-    near = pltpu.VMEM((3, pixels, chans), BF16)
-    return [
-        near,
-        near,
-        near,
-        pltpu.VMEM((3, 4 * rows, chans), BF16),
-        pltpu.VMEM((9, chans, chans), BF16),
-        pltpu.VMEM((pixels, chans), F32),
-        pltpu.SemaphoreType.DMA((3, 9)),
+        arrived(weights.at[t], sems.at[t])
+        terms = [
+            mm(patch(0, t // 3, t % 3), weights[t]),
+            lax.dot_general(
+                patch(1, 2 - t // 3, 2 - t % 3), weights[t], NT, preferred_element_type=F32
+            ),
+        ]
+        for n, term in enumerate(terms):
+            totals[n] = totals[n] + term if t else term
+
+
+def conv_kernel(rows, kernel_ref, feat_ref, grad_ref, above_ref, below_ref, west_ref, east_ref, out_ref, back_ref, raw, lo, hi, sides, weights, totals, sems):
+    pixels, chans = feat_ref.shape
+    cols = pixels // rows
+    loads = [
+        (feat_ref, raw.at[0, pl.ds(cols, pixels)]),
+        (grad_ref, raw.at[1, pl.ds(cols, pixels)]),
+        (west_ref, sides.at[0]),
+        (east_ref, sides.at[1]),
     ]
-
-
-def finish(*parts):
-    for part in parts:
-        next(part)
-    for part in parts:
-        for _ in part:
-            pass
-
-
-def conv_kernel(rows, back, slots_ref, kernel_ref, *refs):
-    maps, out_ref, scratch = refs[:-8], refs[-8], refs[-7:]
-    feats, grads = (maps[: len(maps) // 2], maps[len(maps) // 2 :]) if back else (maps, None)
-    finish(conv_steps(rows, back, slots_ref, kernel_ref, feats, grads, out_ref, scratch))
-
-
-def convolution(slots, kernel, feats, rows, pixels, grads=()):
-    chans = kernel.shape[1]
-    inputs = [kernel] + feats + list(grads)
+    for k, ref in enumerate((above_ref, below_ref)):
+        for n in range(2):
+            part = raw.at[n, pl.ds(k * (cols + pixels), cols)]
+            loads.append((ref.at[pl.ds(n * cols, cols)], part))
+        loads.append((ref.at[pl.ds(2 * cols, 2 * rows)], sides.at[2 + k]))
+    loads = [pltpu.make_async_copy(*load, sems.at[9 + n]) for n, load in enumerate(loads)]
+    for copy in loads:
+        copy.start()
+    start_weights(kernel_ref, weights, sems)
+    for copy in loads:
+        copy.wait()
+    west, east, above, below = [sides[n].astype(F32) for n in range(4)]
+    for n in range(2):
+        mine = slice(n * rows, (n + 1) * rows)
+        corner = [2 * n, 2 * n + 1]
+        side = jnp.concatenate(
+            [
+                piece
+                for k, cells in zip(corner, (west, east))
+                for piece in (above[k : k + 1], cells[mine], below[k : k + 1])
+            ],
+            axis=0,
+        )
+        for h in range(rows + 2):
+            shift_row(raw.at[n], lo.at[n], hi.at[n], h, cols, side)
+
+    def patch(n, a, b):
+        return (lo, raw, hi)[b][n, a * cols : a * cols + pixels]
+
+    tap_sums(patch, weights, sems, totals)
+    for n, ref in enumerate((out_ref, back_ref)):
+        ref[...] = totals[n].astype(BF16)
+
+
+def convolutions(kernel, feat, grad, beyond, near, rows):
+    pixels, chans = feat.shape
+    cols = pixels // rows
+    block = jax.ShapeDtypeStruct((pixels, chans), BF16)
+    maps = pltpu.VMEM((2, pixels + 2 * cols, chans), BF16)
     return pl.pallas_call(
-        functools.partial(conv_kernel, rows, bool(grads)),
-        out_shape=jax.ShapeDtypeStruct((pixels, chans), BF16),
-        in_specs=[SMEM] + [ANY] * len(inputs),
-        out_specs=VMEM,
-        scratch_shapes=conv_scratch(rows, pixels, chans),
+        functools.partial(conv_kernel, rows),
+        out_shape=[block, block],
+        in_specs=[ANY] * 7,
+        out_specs=[VMEM, VMEM],
+        scratch_shapes=[
+            maps,
+            maps,
+            maps,
+            pltpu.VMEM((4, 2 * rows, chans), BF16),
+            pltpu.VMEM((9, chans, chans), BF16),
+            pltpu.VMEM((2, pixels, chans), F32),
+            pltpu.SemaphoreType.DMA((19,)),
+        ],
         compiler_params=pltpu.CompilerParams(vmem_limit_bytes=16 << 20),
-        cost_estimate=pl.CostEstimate(flops=4 * 10**9, bytes_accessed=6 << 20, transcendentals=0),
-        name="backward" if grads else "forward",
-    )(slots, *placed(inputs))
-
-
-def filter_steps(group, rows, where_ref, slots_ref, feats, grads, outs, scratch):
+        cost_estimate=pl.CostEstimate(flops=6 * 10**9, bytes_accessed=6 << 20, transcendentals=0),
+        name="convolutions",
+    )(*placed([kernel, feat, grad] + beyond + near))
+
+
+def filter_kernel(group, rows, where_ref, slots_ref, *refs):
+    maps, refs = refs[:-9], refs[-9:]
+    feats, grads = maps[: len(maps) // 2], maps[len(maps) // 2 :]
     count = len(feats) - 1
-    keep_ref, give_ref = outs
-    raw, lo, hi, ends, grad, total, sems = scratch
+    keep_ref, give_ref, raw, lo, hi, ends, grad, total, sems = refs
     pixels, lanes = raw.shape[1:]
     cols = pixels // rows
     pieces, taps, share, width = keep_ref.shape
@@ -390,7 +384,6 @@
         start_map(feats, i, raw.at[j], sems.at[0], cut)
         start_rest(feats, i, ends.at[j], sems.at[1], cut)
         start_map(grads, i, grad.at[j - 1], sems.at[2])
-    yield
     inside = pl.ds(1, count)
     arrived(raw.at[inside], sems.at[0])
     arrived(ends.at[inside], sems.at[1])
@@ -427,12 +420,6 @@
                 give_ref[i, t] = jnp.where(core == 0, odd, even).astype(BF16)
 
 
-def filter_kernel(rows, where_ref, slots_ref, *refs):
-    maps, outs, scratch = refs[:-9], refs[-9:-7], refs[-7:]
-    feats, grads = maps[: len(maps) // 2], maps[len(maps) // 2 :]
-    finish(filter_steps(GROUP, rows, where_ref, slots_ref, feats, grads, outs, scratch))
-
-
 def filter_terms(where, slots, feats, grads, rows, share, col_count):
     pixels, chans = grads[0].shape
     count, lanes = len(feats) - 1, 128
@@ -440,7 +427,7 @@
     window = pltpu.VMEM((count + 2, pixels, lanes), BF16)
     inputs = feats + grads
     return pl.pallas_call(
-        functools.partial(filter_kernel, rows),
+        functools.partial(filter_kernel, GROUP, rows),
         out_shape=[jax.ShapeDtypeStruct(shape, F32), jax.ShapeDtypeStruct(shape, BF16)],
         in_specs=[SMEM, SMEM] + [ANY] * len(inputs),
         out_specs=[VMEM] * 2,
@@ -448,7 +435,7 @@
             window,
             window,
             window,
-            pltpu.VMEM((count + 2, 4 * rows, lanes), BF16),
+            pltpu.VMEM((count + 2, 2 * rows, lanes), BF16),
             pltpu.VMEM((count, pixels, chans), BF16),
             pltpu.VMEM((lanes, chans), F32),
             pltpu.SemaphoreType.DMA((3,)),
@@ -528,17 +515,32 @@
     packed = rank * pixels // chans
     tail = [projector[n : n + packed] for n in range(0, rank, packed)]
     message = jnp.concatenate([flat, jnp.concatenate(tail, axis=1)], axis=0)
-    message = jnp.pad(message, ((0, 4 * rows), (0, 0)))
+    message = jnp.pad(message, ((0, 2 * rows), (0, 0)))
     message = lax.optimization_barrier(message)
-    grads = {0: own_grad}
     size = message.shape[0]
-    message = lax.dynamic_update_slice(message, jnp.concatenate(near), (size - 4 * rows, 0))
+    sides = jnp.concatenate([x[:rows] for x in near])
+    message = lax.dynamic_update_slice(message, sides, (size - 2 * rows, 0))
     feats = {0: message}
+    beyond = []
+    south = [(i, i + 1) for i in range(row_count - 1)]
+    north = [(j, i) for i, j in south]
+    for h, perm in ((rows - 1, south), (0, north)):
+        cells = [x[n * rows + h : n * rows + h + 1] for n in range(2) for x in near]
+        row_of = [x[h * cols : (h + 1) * cols] for x in (flat, own_grad)]
+        parcel = jnp.concatenate(row_of + cells)
+        parcel = jnp.pad(parcel, ((0, 2 * rows - len(cells)), (0, 0)))
+        beyond.append(lax.ppermute(parcel, "rows", perm))
     for s in range(1, half_way):
         for d in (1, -1):
             feats[-s * d] = send(feats[(1 - s) * d], d)
+    output, grad_features = convolutions(kernel, flat, own_grad, beyond, near, rows)
+    feats[1 - half_way], feats[half_way - 1], output, grad_features = lax.optimization_barrier(
+        (feats[1 - half_way], feats[half_way - 1], output, grad_features)
+    )
     top, bottom = feats[1 - half_way], feats[half_way - 1]
-    feats[half_way] = [send(top[: size // 2], 1), send(bottom[size // 2 :], -1)]
+    mid = size // 32 * 16
+    feats[half_way] = [send(top[:mid], 1), send(bottom[mid:], -1)]
+    grads = {0: own_grad}
     late_grad = after(own_grad, top, bottom)
     for d in (1, 2):
         grads[-d], grads[d] = send(late_grad, d), send(late_grad, -d)
@@ -579,9 +581,8 @@
     grads = listed(grads, True)
 
     share = chans // row_count
-    output = convolution(after(slots, half), kernel, feats, rows, pixels)
-    terms, give = filter_terms(after(where, output), slots, feats, grads, rows, share, col_count)
-    grad_features = convolution(after(slots, give), kernel, feats, rows, pixels, grads)
+    terms, give = filter_terms(after(where, half), slots, feats, grads, rows, share, col_count)
+    filtered = give
     for level in range(levels):
         if level:
             pairs = terms.reshape((-1, 2) + terms.shape[1:])
@@ -590,12 +591,12 @@
             give = lax.dynamic_index_in_dim(pairs, 1 - bit, 1, keepdims=False).astype(BF16)
         got = swap(give, level)
         if level < levels - 1:
-            terms = terms + after(got, grad_features).astype(F32)
+            terms = terms + got.astype(F32)
 
     for level in range(1, levels):
         mine = swap(half, level)
         if level == 1:
-            mine = after(mine, grad_features)
+            mine = after(mine, filtered)
         others = [mine, swap(mine, 0)]
         final = level == levels - 1
         share = (rank // col_count, sketch.shape[1] // row_count) if final else None

time: 113 us -> 111 us (0.982)
  starting transfers between devices: 30.4 us -> 36.1 us
  waiting for transfers between devices: 24.8 us -> 19.9 us
  Pallas kernels: 48.8 us -> 44.5 us
  local copies, waits for them, and re-layouts: 4.84 us -> 6.07 us
    ppermute x16, waiting for transfers between devices: 24.8 us -> 14.2 us  [send(): return lax.ppermute(value, 'rows', hop)]
    ppermute x5, waiting for transfers between devices: 0.01 us -> 5.21 us  [swap(): lax.ppermute(value, 'cols', [(i, i ^ 1 << level) for i in range(col_count)])]
    ppermute x0 -> x2, starting transfers between devices: none -> 5.14 us  [body(): beyond.append(lax.ppermute(parcel, 'rows', perm))]
    pallas_call x3 -> x2, Pallas kernels: 14.5 us -> 10.2 us  [the longest x1 5.21 us: convolutions(): pl.pallas_call(functools.partial(conv_kernel, rows), out_shape=[block, bl...]
    unnamed x39 -> x49, local copies, waits for them, and re-layouts: 2.92 us -> 4.15 us
  transfers between devices with their start and end apart: 23 -> 25, of which waited for: 4 -> 9; matrix products, arithmetic and copies ran while one was open for 4% -> 4% of each run, Pallas kernels for 42% -> 39%
where the time goes in v3:
time: 111 us
  Pallas kernels  44.5 us (40%)
  starting transfers between devices  36.1 us (33%)
  waiting for transfers between devices  19.9 us (18%)
  local copies, waits for them, and re-layouts  6.07 us (5%)
  other arithmetic  2.83 us (3%)
  between operations  1.24 us (1%)
    ppermute x16, starting transfers between devices, send(): return lax.ppermute(value, 'rows', hop)  24 us
    pallas_call x1, Pallas kernels, row_tree(): pl.pallas_call(functools.partial(row_tree_kernel, first, 1536, rows), out...  22.2 us
    ppermute x16, waiting for transfers between devices, send(): return lax.ppermute(value, 'rows', hop)  14.2 us
    pallas_call x2, Pallas kernels, merge(): pl.pallas_call(functools.partial(merge_kernel, 1152, len(others) == 2, sh...  10.4 us
    ppermute x5, waiting for transfers between devices, swap(): lax.ppermute(value, 'cols', [(i, i ^ 1 << level) for i in range(col_count)])  5.21 us
    pallas_call x1, Pallas kernels, convolutions(): pl.pallas_call(functools.partial(conv_kernel, rows), out_shape=[block, bl...  5.21 us
    ppermute x2, starting transfers between devices, body(): beyond.append(lax.ppermute(parcel, 'rows', perm))  5.14 us
    pallas_call x1, Pallas kernels, filter_terms(): pl.pallas_call(functools.partial(filter_kernel, GROUP, rows), out_shape=[...  5.01 us
  transfers between devices with their start and end apart: 25, of which 9 were waited for; matrix products, arithmetic and copies ran while one was open for 4% of the time, Pallas kernels for 39%

profile of v3, /device:TPU:0, one launch (start us, length us, event | category | flops | bytes accessed | tf_op | source)
XLA Modules:
  0.0 110.7 jit_solution(8870899151323370703)
XLA Ops:
  0.6 1.7 %edges.1 = (bf16[16,512]{1,0:T(8,128)(2,1)}, bf16[16,512]{1,0:T(8,128)(2,1)}) custom-call(bf16[256,512]{1,0:T(8,128)(2,1)} %bitcast.31, bf16[256,512]{1,0:T(8,128)(2,1)} %bitcast.34), custom_call_target="tpu_custom_call" | custom-call | tf_op jit(solution)/shard_map/edges/pallas_call | solution.py:470
  2.3 1.3 %collective-permute-start.1 = (bf16[16,512]{1,0:T(8,128)(2,1)}, bf16[16,512]{1,0:T(8,128)(2,1)S(1)}, u32[]{:S(2)}, u32[]{:S(2)}) collective-permute-start(bf16[16,512]{1,0:T(8,128)(2,1)} %get-tuple-element.48), channel_id=1, source_target_pairs={{1,0},{2,1},{3,2},{5,4},{6,5},{7,6},{9,8},{10,9},{11,10},{13,12},{... | collective-permute-start | bytes 49160 | tf_op jit(solution)/shard_map/ppermute | solution.py:514
  3.6 3.0 %collective-permute-start = (bf16[16,512]{1,0:T(8,128)(2,1)}, bf16[16,512]{1,0:T(8,128)(2,1)S(1)}, u32[]{:S(2)}, u32[]{:S(2)}) collective-permute-start(bf16[16,512]{1,0:T(8,128)(2,1)} %get-tuple-element.47), channel_id=1, source_target_pairs={{0,1},{1,2},{2,3},{4,5},{5,6},{6,7},{8,9},{9,10},{10,11},{12,13},{... | collective-permute-start | bytes 49160 | tf_op jit(solution)/shard_map/ppermute | solution.py:514
  8.5 3.1 %collective-permute-start.2 = (bf16[336,512]{1,0:T(8,128)(2,1)S(1)}, bf16[336,512]{1,0:T(8,128)(2,1)S(1)}, u32[]{:S(2)}, u32[]{:S(2)}) collective-permute-start(bf16[336,512]{1,0:T(8,128)(2,1)S(1)} %maximum_dynamic-update-slice_fusion.refs_0_), channel_id=1, source_target_pairs={{0,8},{8,16},{16,24},{24,28},{28,20},{20,12},{12,4},{4,0},{1,9},{9... | collective-permute-start | bytes 1032200 | tf_op jit(solution)/shard_map/ppermute | solution.py:510
  12.4 7.5 %collective-permute-done.2.refs_1_ = bf16[336,512]{1,0:T(8,128)(2,1)S(1)} collective-permute-done((bf16[336,512]{1,0:T(8,128)(2,1)S(1)}, bf16[336,512]{1,0:T(8,128)(2,1)S(1)}, u32[]{:S(2)}, u32[]{:S(2)}) %collective-permute-start.2) | collective-permute-done | bytes 344096 | tf_op jit(solution)/shard_map/ppermute | solution.py:510
  19.9 2.5 %collective-permute-start.3 = (bf16[336,512]{1,0:T(8,128)(2,1)S(1)}, bf16[336,512]{1,0:T(8,128)(2,1)S(1)}, u32[]{:S(2)}, u32[]{:S(2)}) collective-permute-start(bf16[336,512]{1,0:T(8,128)(2,1)S(1)} %collective-permute-done.2.refs_1_), channel_id=1, source_target_pairs={{0,8},{8,16},{16,24},{24,28},{28,20},{20,12},{12,4},{4,0},{1,9},{9... | collective-permute-start | bytes 1032200 | tf_op jit(solution)/shard_map/ppermute | solution.py:510
  22.5 3.8 %collective-permute-start.8 = (bf16[80,512]{1,0:T(8,128)(2,1)S(1)}, bf16[80,512]{1,0:T(8,128)(2,1)S(1)}, u32[]{:S(2)}, u32[]{:S(2)}) collective-permute-start(bf16[80,512]{1,0:T(8,128)(2,1)S(1)} %pad.16), channel_id=1, source_target_pairs={{0,4},{4,8},{8,12},{12,16},{16,20},{20,24},{24,28},{1,5},{5,9},{9,... | collective-permute-start | bytes 245768 | tf_op jit(solution)/shard_map/ppermute | solution.py:532
  26.4 1.3 %collective-permute-start.9 = (bf16[80,512]{1,0:T(8,128)(2,1)S(1)}, bf16[80,512]{1,0:T(8,128)(2,1)S(1)}, u32[]{:S(2)}, u32[]{:S(2)}) collective-permute-start(bf16[80,512]{1,0:T(8,128)(2,1)S(1)} %pad.17), channel_id=1, source_target_pairs={{4,0},{8,4},{12,8},{16,12},{20,16},{24,20},{28,24},{5,1},{9,5},{13... | collective-permute-start | bytes 245768 | tf_op jit(solution)/shard_map/ppermute | solution.py:532
  28.0 2.8 %collective-permute-done.3.refs_3_ = bf16[336,512]{1,0:T(8,128)(2,1)S(1)} collective-permute-done((bf16[336,512]{1,0:T(8,128)(2,1)S(1)}, bf16[336,512]{1,0:T(8,128)(2,1)S(1)}, u32[]{:S(2)}, u32[]{:S(2)}) %collective-permute-start.3) | collective-permute-done | bytes 344096 | tf_op jit(solution)/shard_map/ppermute | solution.py:510
  30.8 1.8 %collective-permute-start.4 = (bf16[336,512]{1,0:T(8,128)(2,1)S(1)}, bf16[336,512]{1,0:T(8,128)(2,1)S(1)}, u32[]{:S(2)}, u32[]{:S(2)}) collective-permute-start(bf16[336,512]{1,0:T(8,128)(2,1)S(1)} %collective-permute-done.3.refs_3_), channel_id=1, source_target_pairs={{0,8},{8,16},{16,24},{24,28},{28,20},{20,12},{12,4},{4,0},{1,9},{9... | collective-permute-start | bytes 1032200 | tf_op jit(solution)/shard_map/ppermute | solution.py:510
  35.5 5.2 %convolutions.1 = (bf16[256,512]{1,0:T(8,128)(2,1)}, bf16[256,512]{1,0:T(8,128)(2,1)}) custom-call(bf16[4608,512]{1,0:T(8,128)(2,1)} %kernel_ref.1, bf16[256,512]{1,0:T(8,128)(2,1)} %bitcast.33, bf16[256,512]{1,0:T(8,128)(2,1)} %bitcast.35, bf16[80,512]{1,0:T(8,128)(2,1)} %copy-done.22, bf16[80,512]{1,0:T(8,128)(2,1)} %copy-done.23, ...), custom_call_target="tpu_custom_call" | custom-call | flops 6000000000 | bytes 6291456 | tf_op jit(solution)/shard_map/convolutions/pallas_call | solution.py:349
  41.8 1.6 %collective-permute-start.10 = (bf16[160,512]{1,0:T(8,128)(2,1)S(1)}, bf16[160,512]{1,0:T(8,128)(2,1)S(1)}, u32[]{:S(2)}, u32[]{:S(2)}) collective-permute-start(bf16[160,512]{1,0:T(8,128)(2,1)S(1)} %slice.120), channel_id=1, source_target_pairs={{0,8},{8,16},{16,24},{24,28},{28,20},{20,12},{12,4},{4,0},{1,9},{9... | collective-permute-start | bytes 491528 | tf_op jit(solution)/shard_map/ppermute | solution.py:510
  44.0 1.8 %collective-permute-start.12 = (bf16[256,512]{1,0:T(8,128)(2,1)S(1)}, bf16[256,512]{1,0:T(8,128)(2,1)S(1)}, u32[]{:S(2)}, u32[]{:S(2)}) collective-permute-start(bf16[256,512]{1,0:T(8,128)(2,1)S(1)} %bitcast.37), channel_id=1, source_target_pairs={{0,4},{8,0},{16,8},{24,16},{28,24},{20,28},{12,20},{4,12},{1,5},{9... | collective-permute-start | bytes 786440 | tf_op jit(solution)/shard_map/ppermute | solution.py:510
  46.1 2.0 %collective-permute-start.14 = (bf16[256,512]{1,0:T(8,128)(2,1)S(1)}, bf16[256,512]{1,0:T(8,128)(2,1)S(1)}, u32[]{:S(2)}, u32[]{:S(2)}) collective-permute-start(bf16[256,512]{1,0:T(8,128)(2,1)S(1)} %bitcast.39), channel_id=1, source_target_pairs={{0,12},{8,4},{16,0},{24,8},{28,16},{20,24},{12,28},{4,20},{1,13},{... | collective-permute-start | bytes 786440 | tf_op jit(solution)/shard_map/ppermute | solution.py:510
  48.1 4.2 %collective-permute-start.15 = (bf16[256,512]{1,0:T(8,128)(2,1)S(1)}, bf16[256,512]{1,0:T(8,128)(2,1)S(1)}, u32[]{:S(2)}, u32[]{:S(2)}) collective-permute-start(bf16[256,512]{1,0:T(8,128)(2,1)S(1)} %bitcast.40), channel_id=1, source_target_pairs={{0,16},{8,24},{16,28},{24,20},{28,12},{20,4},{12,0},{4,8},{1,17},{... | collective-permute-start | bytes 786440 | tf_op jit(solution)/shard_map/ppermute | solution.py:510
  52.9 22.2 %row_tree.1.refs_0_ = bf16[128,4608]{1,0:T(8,128)(2,1)S(1)} custom-call(s32[8]{0:T(128)S(1)} %stack.52.rows_ref.slots_ref, bf16[128,256]{1,0:T(8,128)(2,1)S(1)} %get-tuple-element.70.mix_ref, bf16[336,512]{1,0:T(8,128)(2,1)} %copy-done.2, bf16[336,512]{1,0:T(8,128)(2,1)} %copy-done.10, bf16[336,512]{1,0:T(8,128)(2,1)} %copy-done.11, ...), custom_call_target="tpu_custom_call" | custom-call | flops 20000000000 | bytes 8388608 | tf_op jit(solution)/shard_map/row_tree/pallas_call | solution.py:185
  76.0 2.8 %collective-permute-start.17 = (bf16[256,512]{1,0:T(8,128)(2,1)S(1)}, bf16[256,512]{1,0:T(8,128)(2,1)S(1)}, u32[]{:S(2)}, u32[]{:S(2)}) collective-permute-start(bf16[256,512]{1,0:T(8,128)(2,1)S(1)} %collective-permute-done.15.refs_12_), channel_id=1, source_target_pairs={{0,8},{8,16},{16,24},{24,28},{28,20},{20,12},{12,4},{4,0},{1,9},{9... | collective-permute-start | bytes 786440 | tf_op jit(solution)/shard_map/ppermute | solution.py:510
  78.9 2.6 %collective-permute-start.19 = (bf16[128,512]{1,0:T(8,128)(2,1)S(1)}, bf16[128,512]{1,0:T(8,128)(2,1)S(1)}, u32[]{:S(2)}, u32[]{:S(2)}) collective-permute-start(bf16[128,512]{1,0:T(8,128)(2,1)S(1)} %slice.122), channel_id=1, source_target_pairs={{0,16},{8,24},{16,28},{24,20},{28,12},{20,4},{12,0},{4,8},{1,17},{... | collective-permute-start | bytes 393224 | tf_op jit(solution)/shard_map/ppermute | solution.py:510
  81.9 5.7 %merge.2 = (bf16[128,4608]{1,0:T(8,128)(2,1)}, bf16[128,2304]{1,0:T(8,128)(2,1)S(1)}) custom-call(s32[4]{0:T(128)S(1)} %constant_dynamic-update-slice_fusion.1.where_ref, bf16[128,256]{1,0:T(8,128)(2,1)S(1)} %get-tuple-element.71.mix_ref, bf16[128,4608]{1,0:T(8,128)(2,1)S(1)} %row_tree.1.refs_0_, bf16[128,4608]{1,0:T(8,128)(2,1)S(1)} %collective-permute-done.16.refs_1_), custom_call_target="tpu_custom_call" | custom-call | flops 4000000000 | bytes 4194304 | tf_op jit(solution)/shard_map/merge/pallas_call | solution.py:268
  88.9 2.2 %collective-permute-done.20.refs_17_ = bf16[128,512]{1,0:T(8,128)(2,1)S(1)} collective-permute-done((bf16[128,512]{1,0:T(8,128)(2,1)S(1)}, bf16[128,512]{1,0:T(8,128)(2,1)S(1)}, u32[]{:S(2)}, u32[]{:S(2)}) %collective-permute-start.20) | collective-permute-done | bytes 131104 | tf_op jit(solution)/shard_map/ppermute | solution.py:510
  92.5 5.0 %filter_terms.1 = (f32[2,9,64,128]{3,2,1,0:T(8,128)S(1)}, bf16[2,9,64,128]{3,2,1,0:T(8,128)(2,1)S(1)}) custom-call(s32[4]{0:T(128)S(1)} %pad_add_fusion.where_ref, s32[8]{0:T(128)S(1)} %stack.52.rows_ref.slots_ref, bf16[336,512]{1,0:T(8,128)(2,1)} %copy-done.2, bf16[336,512]{1,0:T(8,128)(2,1)} %copy-done.10, bf16[336,512]{1,0:T(8,128)(2,1)} %copy-done.11, ...), custom_call_target="tpu_custom_call" | custom-call | flops 5000000000 | bytes 4194304 | tf_op jit(solution)/shard_map/filter_terms/pallas_call | solution.py:429
  97.6 4.9 %collective-permute-done.23.refs_1_ = bf16[128,2304]{1,0:T(8,128)(2,1)S(1)} collective-permute-done((bf16[128,2304]{1,0:T(8,128)(2,1)S(1)}, bf16[128,2304]{1,0:T(8,128)(2,1)S(1)}, u32[]{:S(2)}, u32[]{:S(2)}) %collective-permute-start.23) | collective-permute-done | bytes 589856 | tf_op jit(solution)/shard_map/ppermute | solution.py:566
  103.6 1.3 %collective-permute-start.22 = (bf16[1,9,64,128]{3,2,1,0:T(8,128)(2,1)S(1)}, bf16[1,9,64,128]{3,2,1,0:T(8,128)(2,1)S(1)}, u32[]{:S(2)}, u32[]{:S(2)}) collective-permute-start(bf16[1,9,64,128]{3,2,1,0:T(8,128)(2,1)S(1)} %dynamic-slice_convert_fusion), channel_id=1, source_target_pairs={{0,2},{1,3},{2,0},{3,1},{4,6},{5,7},{6,4},{7,5},{8,10},{9,11},{10,... | collective-permute-start | bytes 442376 | tf_op jit(solution)/shard_map/ppermute | solution.py:566
  104.9 4.7 %merge.3 = bf16[32,576]{1,0:T(8,128)(2,1)} custom-call(s32[4]{0:T(128)S(1)} %constant_dynamic-update-slice_fusion.where_ref, bf16[128,256]{1,0:T(8,128)(2,1)S(1)} %get-tuple-element.71.mix_ref, bf16[128,4608]{1,0:T(8,128)(2,1)S(1)} %copy-done, bf16[128,2304]{1,0:T(8,128)(2,1)S(1)} %collective-permute-done.23.refs_1_, ...), custom_call_target="tpu_custom_call" | custom-call | flops 4000000000 | bytes 4194304 | tf_op jit(solution)/shard_map/merge/pallas_call | solution.py:268
  (105 shorter events, 14.5 us)
Async XLA Ops:
  2.3 6.1 %collective-permute-start.1 = (bf16[16,512]{1,0:T(8,128)(2,1)}, bf16[16,512]{1,0:T(8,128)(2,1)S(1)}, u32[]{:S(2)}, u32[]{:S(2)}) collective-permute-start(bf16[16,512]{1,0:T(8,128)(2,1)} %get-tuple-element.48), channel_id=1, source_target_pairs={{1,0},{2,1},{3,2},{5,4},{6,5},{7,6},{9,8},{10,9},{11,10},{13,12},{... | collective-permute-start | bytes 49160 | tf_op jit(solution)/shard_map/ppermute | solution.py:514
  3.6 4.8 %collective-permute-start = (bf16[16,512]{1,0:T(8,128)(2,1)}, bf16[16,512]{1,0:T(8,128)(2,1)S(1)}, u32[]{:S(2)}, u32[]{:S(2)}) collective-permute-start(bf16[16,512]{1,0:T(8,128)(2,1)} %get-tuple-element.47), channel_id=1, source_target_pairs={{0,1},{1,2},{2,3},{4,5},{5,6},{6,7},{8,9},{9,10},{10,11},{12,13},{... | collective-permute-start | bytes 49160 | tf_op jit(solution)/shard_map/ppermute | solution.py:514
  8.5 11.4 %collective-permute-start.2 = (bf16[336,512]{1,0:T(8,128)(2,1)S(1)}, bf16[336,512]{1,0:T(8,128)(2,1)S(1)}, u32[]{:S(2)}, u32[]{:S(2)}) collective-permute-start(bf16[336,512]{1,0:T(8,128)(2,1)S(1)} %maximum_dynamic-update-slice_fusion.refs_0_), channel_id=1, source_target_pairs={{0,8},{8,16},{16,24},{24,28},{28,20},{20,12},{12,4},{4,0},{1,9},{9... | collective-permute-start | bytes 1032200 | tf_op jit(solution)/shard_map/ppermute | solution.py:510
  11.6 10.8 %collective-permute-start.5 = (bf16[336,512]{1,0:T(8,128)(2,1)S(1)}, bf16[336,512]{1,0:T(8,128)(2,1)S(1)}, u32[]{:S(2)}, u32[]{:S(2)}) collective-permute-start(bf16[336,512]{1,0:T(8,128)(2,1)S(1)} %maximum_dynamic-update-slice_fusion.refs_0_), channel_id=1, source_target_pairs={{0,4},{8,0},{16,8},{24,16},{28,24},{20,28},{12,20},{4,12},{1,5},{9... | collective-permute-start | bytes 1032200 | tf_op jit(solution)/shard_map/ppermute | solution.py:510
  19.9 10.9 %collective-permute-start.3 = (bf16[336,512]{1,0:T(8,128)(2,1)S(1)}, bf16[336,512]{1,0:T(8,128)(2,1)S(1)}, u32[]{:S(2)}, u32[]{:S(2)}) collective-permute-start(bf16[336,512]{1,0:T(8,128)(2,1)S(1)} %collective-permute-done.2.refs_1_), channel_id=1, source_target_pairs={{0,8},{8,16},{16,24},{24,28},{28,20},{20,12},{12,4},{4,0},{1,9},{9... | collective-permute-start | bytes 1032200 | tf_op jit(solution)/shard_map/ppermute | solution.py:510
  22.4 10.8 %collective-permute-start.6 = (bf16[336,512]{1,0:T(8,128)(2,1)S(1)}, bf16[336,512]{1,0:T(8,128)(2,1)S(1)}, u32[]{:S(2)}, u32[]{:S(2)}) collective-permute-start(bf16[336,512]{1,0:T(8,128)(2,1)S(1)} %collective-permute-done.5.refs_2_), channel_id=1, source_target_pairs={{0,4},{8,0},{16,8},{24,16},{28,24},{20,28},{12,20},{4,12},{1,5},{9... | collective-permute-start | bytes 1032200 | tf_op jit(solution)/shard_map/ppermute | solution.py:510
  22.5 11.7 %collective-permute-start.8 = (bf16[80,512]{1,0:T(8,128)(2,1)S(1)}, bf16[80,512]{1,0:T(8,128)(2,1)S(1)}, u32[]{:S(2)}, u32[]{:S(2)}) collective-permute-start(bf16[80,512]{1,0:T(8,128)(2,1)S(1)} %pad.16), channel_id=1, source_target_pairs={{0,4},{4,8},{8,12},{12,16},{16,20},{20,24},{24,28},{1,5},{5,9},{9,... | collective-permute-start | bytes 245768 | tf_op jit(solution)/shard_map/ppermute | solution.py:532
  26.4 7.8 %collective-permute-start.9 = (bf16[80,512]{1,0:T(8,128)(2,1)S(1)}, bf16[80,512]{1,0:T(8,128)(2,1)S(1)}, u32[]{:S(2)}, u32[]{:S(2)}) collective-permute-start(bf16[80,512]{1,0:T(8,128)(2,1)S(1)} %pad.17), channel_id=1, source_target_pairs={{4,0},{8,4},{12,8},{16,12},{20,16},{24,20},{28,24},{5,1},{9,5},{13... | collective-permute-start | bytes 245768 | tf_op jit(solution)/shard_map/ppermute | solution.py:532
  30.8 9.9 %collective-permute-start.4 = (bf16[336,512]{1,0:T(8,128)(2,1)S(1)}, bf16[336,512]{1,0:T(8,128)(2,1)S(1)}, u32[]{:S(2)}, u32[]{:S(2)}) collective-permute-start(bf16[336,512]{1,0:T(8,128)(2,1)S(1)} %collective-permute-done.3.refs_3_), channel_id=1, source_target_pairs={{0,8},{8,16},{16,24},{24,28},{28,20},{20,12},{12,4},{4,0},{1,9},{9... | collective-permute-start | bytes 1032200 | tf_op jit(solution)/shard_map/ppermute | solution.py:510
  33.3 8.5 %collective-permute-start.7 = (bf16[336,512]{1,0:T(8,128)(2,1)S(1)}, bf16[336,512]{1,0:T(8,128)(2,1)S(1)}, u32[]{:S(2)}, u32[]{:S(2)}) collective-permute-start(bf16[336,512]{1,0:T(8,128)(2,1)S(1)} %collective-permute-done.6.refs_4_), channel_id=1, source_target_pairs={{0,4},{8,0},{16,8},{24,16},{28,24},{20,28},{12,20},{4,12},{1,5},{9... | collective-permute-start | bytes 1032200 | tf_op jit(solution)/shard_map/ppermute | solution.py:510
  41.8 6.2 %collective-permute-start.10 = (bf16[160,512]{1,0:T(8,128)(2,1)S(1)}, bf16[160,512]{1,0:T(8,128)(2,1)S(1)}, u32[]{:S(2)}, u32[]{:S(2)}) collective-permute-start(bf16[160,512]{1,0:T(8,128)(2,1)S(1)} %slice.120), channel_id=1, source_target_pairs={{0,8},{8,16},{16,24},{24,28},{28,20},{20,12},{12,4},{4,0},{1,9},{9... | collective-permute-start | bytes 491528 | tf_op jit(solution)/shard_map/ppermute | solution.py:510
  43.5 8.7 %collective-permute-start.11 = (bf16[176,512]{1,0:T(8,128)(2,1)S(1)}, bf16[176,512]{1,0:T(8,128)(2,1)S(1)}, u32[]{:S(2)}, u32[]{:S(2)}) collective-permute-start(bf16[176,512]{1,0:T(8,128)(2,1)S(1)} %slice.121), channel_id=1, source_target_pairs={{0,4},{8,0},{16,8},{24,16},{28,24},{20,28},{12,20},{4,12},{1,5},{9... | collective-permute-start | bytes 540680 | tf_op jit(solution)/shard_map/ppermute | solution.py:510
  44.0 31.1 %collective-permute-start.12 = (bf16[256,512]{1,0:T(8,128)(2,1)S(1)}, bf16[256,512]{1,0:T(8,128)(2,1)S(1)}, u32[]{:S(2)}, u32[]{:S(2)}) collective-permute-start(bf16[256,512]{1,0:T(8,128)(2,1)S(1)} %bitcast.37), channel_id=1, source_target_pairs={{0,4},{8,0},{16,8},{24,16},{28,24},{20,28},{12,20},{4,12},{1,5},{9... | collective-permute-start | bytes 786440 | tf_op jit(solution)/shard_map/ppermute | solution.py:510
  45.8 29.3 %collective-permute-start.13 = (bf16[256,512]{1,0:T(8,128)(2,1)S(1)}, bf16[256,512]{1,0:T(8,128)(2,1)S(1)}, u32[]{:S(2)}, u32[]{:S(2)}) collective-permute-start(bf16[256,512]{1,0:T(8,128)(2,1)S(1)} %bitcast.38), channel_id=1, source_target_pairs={{0,8},{8,16},{16,24},{24,28},{28,20},{20,12},{12,4},{4,0},{1,9},{9... | collective-permute-start | bytes 786440 | tf_op jit(solution)/shard_map/ppermute | solution.py:510
  46.1 29.1 %collective-permute-start.14 = (bf16[256,512]{1,0:T(8,128)(2,1)S(1)}, bf16[256,512]{1,0:T(8,128)(2,1)S(1)}, u32[]{:S(2)}, u32[]{:S(2)}) collective-permute-start(bf16[256,512]{1,0:T(8,128)(2,1)S(1)} %bitcast.39), channel_id=1, source_target_pairs={{0,12},{8,4},{16,0},{24,8},{28,16},{20,24},{12,28},{4,20},{1,13},{... | collective-permute-start | bytes 786440 | tf_op jit(solution)/shard_map/ppermute | solution.py:510
  48.1 27.8 %collective-permute-start.15 = (bf16[256,512]{1,0:T(8,128)(2,1)S(1)}, bf16[256,512]{1,0:T(8,128)(2,1)S(1)}, u32[]{:S(2)}, u32[]{:S(2)}) collective-permute-start(bf16[256,512]{1,0:T(8,128)(2,1)S(1)} %bitcast.40), channel_id=1, source_target_pairs={{0,16},{8,24},{16,28},{24,20},{28,12},{20,4},{12,0},{4,8},{1,17},{... | collective-permute-start | bytes 786440 | tf_op jit(solution)/shard_map/ppermute | solution.py:510
  75.9 6.0 %collective-permute-start.16 = (bf16[128,4608]{1,0:T(8,128)(2,1)S(1)}, bf16[128,4608]{1,0:T(8,128)(2,1)S(1)}, u32[]{:S(2)}, u32[]{:S(2)}) collective-permute-start(bf16[128,4608]{1,0:T(8,128)(2,1)S(1)} %row_tree.1.refs_0_), channel_id=1, source_target_pairs={{0,1},{1,0},{2,3},{3,2},{4,5},{5,4},{6,7},{7,6},{8,9},{9,8},{10,11... | collective-permute-start | bytes 3538952 | tf_op jit(solution)/shard_map/ppermute | solution.py:566
  76.0 15.0 %collective-permute-start.17 = (bf16[256,512]{1,0:T(8,128)(2,1)S(1)}, bf16[256,512]{1,0:T(8,128)(2,1)S(1)}, u32[]{:S(2)}, u32[]{:S(2)}) collective-permute-start(bf16[256,512]{1,0:T(8,128)(2,1)S(1)} %collective-permute-done.15.refs_12_), channel_id=1, source_target_pairs={{0,8},{8,16},{16,24},{24,28},{28,20},{20,12},{12,4},{4,0},{1,9},{9... | collective-permute-start | bytes 786440 | tf_op jit(solution)/shard_map/ppermute | solution.py:510
  78.8 12.3 %collective-permute-start.18 = (bf16[256,512]{1,0:T(8,128)(2,1)S(1)}, bf16[256,512]{1,0:T(8,128)(2,1)S(1)}, u32[]{:S(2)}, u32[]{:S(2)}) collective-permute-start(bf16[256,512]{1,0:T(8,128)(2,1)S(1)} %collective-permute-done.14.refs_13_), channel_id=1, source_target_pairs={{0,4},{8,0},{16,8},{24,16},{28,24},{20,28},{12,20},{4,12},{1,5},{9... | collective-permute-start | bytes 786440 | tf_op jit(solution)/shard_map/ppermute | solution.py:510
  78.9 10.0 %collective-permute-start.19 = (bf16[128,512]{1,0:T(8,128)(2,1)S(1)}, bf16[128,512]{1,0:T(8,128)(2,1)S(1)}, u32[]{:S(2)}, u32[]{:S(2)}) collective-permute-start(bf16[128,512]{1,0:T(8,128)(2,1)S(1)} %slice.122), channel_id=1, source_target_pairs={{0,16},{8,24},{16,28},{24,20},{28,12},{20,4},{12,0},{4,8},{1,17},{... | collective-permute-start | bytes 393224 | tf_op jit(solution)/shard_map/ppermute | solution.py:510
  81.5 9.6 %collective-permute-start.20 = (bf16[128,512]{1,0:T(8,128)(2,1)S(1)}, bf16[128,512]{1,0:T(8,128)(2,1)S(1)}, u32[]{:S(2)}, u32[]{:S(2)}) collective-permute-start(bf16[128,512]{1,0:T(8,128)(2,1)S(1)} %slice.123), channel_id=1, source_target_pairs={{0,12},{8,4},{16,0},{24,8},{28,16},{20,24},{12,28},{4,20},{1,13},{... | collective-permute-start | bytes 393224 | tf_op jit(solution)/shard_map/ppermute | solution.py:510
  87.6 14.9 %collective-permute-start.23 = (bf16[128,2304]{1,0:T(8,128)(2,1)S(1)}, bf16[128,2304]{1,0:T(8,128)(2,1)S(1)}, u32[]{:S(2)}, u32[]{:S(2)}) collective-permute-start(bf16[128,2304]{1,0:T(8,128)(2,1)S(1)} %get-tuple-element.57), channel_id=1, source_target_pairs={{0,2},{1,3},{2,0},{3,1},{4,6},{5,7},{6,4},{7,5},{8,10},{9,11},{10,... | collective-permute-start | bytes 1769480 | tf_op jit(solution)/shard_map/ppermute | solution.py:566
  97.5 5.0 %collective-permute-start.21 = (bf16[2,9,64,128]{3,2,1,0:T(8,128)(2,1)S(1)}, bf16[2,9,64,128]{3,2,1,0:T(8,128)(2,1)}, u32[]{:S(2)}, u32[]{:S(2)}) collective-permute-start(bf16[2,9,64,128]{3,2,1,0:T(8,128)(2,1)S(1)} %get-tuple-element.62), channel_id=1, source_target_pairs={{0,1},{1,0},{2,3},{3,2},{4,5},{5,4},{6,7},{7,6},{8,9},{9,8},{10,11... | collective-permute-start | bytes 884744 | tf_op jit(solution)/shard_map/ppermute | solution.py:566
  103.6 6.3 %collective-permute-start.22 = (bf16[1,9,64,128]{3,2,1,0:T(8,128)(2,1)S(1)}, bf16[1,9,64,128]{3,2,1,0:T(8,128)(2,1)S(1)}, u32[]{:S(2)}, u32[]{:S(2)}) collective-permute-start(bf16[1,9,64,128]{3,2,1,0:T(8,128)(2,1)S(1)} %dynamic-slice_convert_fusion), channel_id=1, source_target_pairs={{0,2},{1,3},{2,0},{3,1},{4,6},{5,7},{6,4},{7,5},{8,10},{9,11},{10,... | collective-permute-start | bytes 442376 | tf_op jit(solution)/shard_map/ppermute | solution.py:566
  (25 other events, 239.2 us)

commit v4 on v3

--- a/solution.py
+++ b/solution.py
@@ -366,24 +366,32 @@
     )(*placed([kernel, feat, grad] + beyond + near))
 
 
-def filter_kernel(group, rows, where_ref, slots_ref, *refs):
-    maps, refs = refs[:-9], refs[-9:]
-    feats, grads = maps[: len(maps) // 2], maps[len(maps) // 2 :]
+def tap_term(maps, slot_row, t, grad):
+    pixels, cols = grad.shape[0], maps[3]
+    start = pl.multiple_of((slot_row + 1) * pixels + (t // 3 - 1) * cols, cols)
+    return lax.dot_general(
+        maps[t % 3][pl.ds(start, pixels), :],
+        grad[...],
+        (((0,), (0,)), ((), ())),
+        preferred_element_type=F32,
+    )
+
+
+def early_filter_kernel(rows, share, slots_ref, *refs):
+    *maps, lo, raw, hi, total, ends, grad, sems = refs
+    known = grad.shape[0]
+    feats, grads = maps[:-known], maps[-known:]
     count = len(feats) - 1
-    keep_ref, give_ref, raw, lo, hi, ends, grad, total, sems = refs
     pixels, lanes = raw.shape[1:]
     cols = pixels // rows
-    pieces, taps, share, width = keep_ref.shape
-    base = slots_ref[0] * share
-    window = pl.multiple_of(base // lanes * lanes, lanes)
-    inner = pl.multiple_of(base % lanes, 8)
-    core = where_ref[1]
+    window = pl.multiple_of(slots_ref[0] * share // lanes * lanes, lanes)
     cut = pl.ds(window, lanes)
     for i in range(count):
         j = slots_ref[i] + 1
         start_map(feats, i, raw.at[j], sems.at[0], cut)
         start_rest(feats, i, ends.at[j], sems.at[1], cut)
-        start_map(grads, i, grad.at[j - 1], sems.at[2])
+    for i, ref in enumerate(grads):
+        pltpu.make_async_copy(ref, grad.at[i], sems.at[2]).start()
     inside = pl.ds(1, count)
     arrived(raw.at[inside], sems.at[0])
     arrived(ends.at[inside], sems.at[1])
@@ -395,55 +403,76 @@
         for h in range(rows):
             shift_row(raw.at[j], lo.at[j], hi.at[j], h, cols, side)
     arrived(grad, sems.at[2])
-    chans = grad.shape[2]
-    maps = [ref.reshape((count + 2) * pixels, lanes) for ref in (lo, raw, hi)]
-    for a in range(3):
-        for b, src in enumerate(maps):
-            t = 3 * a + b
-            for g in range(0, count, group):
-                start = pixels * (g + 1) + (a - 1) * cols
-                term = lax.dot_general(
-                    src[start : start + group * pixels],
-                    grad[g : g + group].reshape(group * pixels, chans),
-                    (((0,), (0,)), ((), ())),
-                    preferred_element_type=F32,
-                )
-                if g:
-                    total[...] += term
-                else:
-                    total[...] = term
-            mine = total[pl.ds(inner, share), :]
-            for i in range(pieces):
-                even = mine[:, 2 * i * width : (2 * i + 1) * width]
-                odd = mine[:, (2 * i + 1) * width : (2 * i + 2) * width]
-                keep_ref[i, t] = jnp.where(core == 0, even, odd)
-                give_ref[i, t] = jnp.where(core == 0, odd, even).astype(BF16)
-
-
-def filter_terms(where, slots, feats, grads, rows, share, col_count):
+    flat = [ref.reshape((count + 2) * pixels, lanes) for ref in (lo, raw, hi)] + [cols]
+    for t in range(9):
+        terms = [tap_term(flat, slots_ref[i], t, grad.at[i]) for i in range(known)]
+        total[t] = functools.reduce(jnp.add, terms)
+
+
+def early_filter(slots, feats, grads, rows, share):
     pixels, chans = grads[0].shape
     count, lanes = len(feats) - 1, 128
-    shape = (col_count // 2, 9, share, chans // col_count)
-    window = pltpu.VMEM((count + 2, pixels, lanes), BF16)
+    window = jax.ShapeDtypeStruct((count + 2, pixels, lanes), BF16)
     inputs = feats + grads
     return pl.pallas_call(
-        functools.partial(filter_kernel, GROUP, rows),
+        functools.partial(early_filter_kernel, rows, share),
+        out_shape=[window] * 3 + [jax.ShapeDtypeStruct((9, lanes, chans), F32)],
+        in_specs=[SMEM] + [ANY] * len(inputs),
+        out_specs=[VMEM] * 4,
+        scratch_shapes=[
+            pltpu.VMEM((count + 2, 2 * rows, lanes), BF16),
+            pltpu.VMEM((len(grads), pixels, chans), BF16),
+            pltpu.SemaphoreType.DMA((3,)),
+        ],
+        compiler_params=pltpu.CompilerParams(vmem_limit_bytes=(12 + count) << 20),
+        cost_estimate=pl.CostEstimate(flops=4 * 10**9, bytes_accessed=4 << 20, transcendentals=0),
+        name="early_filter",
+    )(slots, *placed(inputs))
+
+
+def late_filter_kernel(known, rows, where_ref, slots_ref, lo, raw, hi, early_ref, *refs):
+    *grads, keep_ref, give_ref, grad, total, sem = refs
+    pixels, lanes = raw.shape[1:]
+    cols = pixels // rows
+    pieces, taps, share, width = keep_ref.shape
+    inner = pl.multiple_of(slots_ref[0] * share % lanes, 8)
+    core = where_ref[1]
+    for i in range(grad.shape[0]):
+        start_map(grads, i, grad.at[i], sem)
+    arrived(grad, sem)
+    flat = [ref.reshape(raw.shape[0] * pixels, lanes) for ref in (lo, raw, hi)] + [cols]
+    for t in range(9):
+        terms = [
+            tap_term(flat, slots_ref[known + i], t, grad.at[i]) for i in range(grad.shape[0])
+        ]
+        total[...] = functools.reduce(jnp.add, terms, early_ref[t])
+        mine = total[pl.ds(inner, share), :]
+        for i in range(pieces):
+            even = mine[:, 2 * i * width : (2 * i + 1) * width]
+            odd = mine[:, (2 * i + 1) * width : (2 * i + 2) * width]
+            keep_ref[i, t] = jnp.where(core == 0, even, odd)
+            give_ref[i, t] = jnp.where(core == 0, odd, even).astype(BF16)
+
+
+def late_filter(where, slots, early, grads, known, rows, share, col_count):
+    count = len(grads) - 1
+    pixels, lanes = early[0].shape[1:]
+    chans = early[3].shape[2]
+    shape = (col_count // 2, 9, share, chans // col_count)
+    return pl.pallas_call(
+        functools.partial(late_filter_kernel, known, rows),
         out_shape=[jax.ShapeDtypeStruct(shape, F32), jax.ShapeDtypeStruct(shape, BF16)],
-        in_specs=[SMEM, SMEM] + [ANY] * len(inputs),
+        in_specs=[SMEM, SMEM] + [VMEM] * 4 + [ANY] * len(grads),
         out_specs=[VMEM] * 2,
         scratch_shapes=[
-            window,
-            window,
-            window,
-            pltpu.VMEM((count + 2, 2 * rows, lanes), BF16),
             pltpu.VMEM((count, pixels, chans), BF16),
             pltpu.VMEM((lanes, chans), F32),
-            pltpu.SemaphoreType.DMA((3,)),
+            pltpu.SemaphoreType.DMA,
         ],
-        compiler_params=pltpu.CompilerParams(vmem_limit_bytes=(8 + count) << 20),
-        cost_estimate=pl.CostEstimate(flops=5 * 10**9, bytes_accessed=4 << 20, transcendentals=0),
-        name="filter_terms",
-    )(where, slots, *placed(inputs))
+        compiler_params=pltpu.CompilerParams(vmem_limit_bytes=(16 + count) << 20),
+        cost_estimate=pl.CostEstimate(flops=2 * 10**9, bytes_accessed=4 << 20, transcendentals=0),
+        name="late_filter",
+    )(where, slots, *early, *placed(grads))
 
 
 def edge_kernel(rows, feat_ref, grad_ref, first_ref, last_ref, maps, sems):
@@ -569,19 +598,19 @@
         return where.at[0].set(col >> level & 1)
 
     swapped = swap(after(sketch, grads[1], grads[-1], grads[2], grads[-2]), 0)
-    top, bottom, _ = lax.optimization_barrier((grads[-2], grads[2], sketch))
-    grads[-2], grads[2] = top, bottom
+    grads[-2], grads[2], _ = lax.optimization_barrier((grads[-2], grads[2], sketch))
     for s in range(3, half_way):
         for d in (1, -1):
             grads[-s * d] = send(grads[(1 - s) * d], d)
-    split, reach = pixels // 2, half_way - 2
-    grads[half_way] = [send(top[:split], reach), send(bottom[split:], -reach)]
     result = merge(turn(0), mixers[1], sketch, [swapped])
     sketch, half = result
+    top, bottom, _ = lax.optimization_barrier((grads[1 - half_way], grads[half_way - 1], half))
+    split, known = pixels // 2, 5
+    grads[half_way] = [send(top[:split], 1), send(bottom[split:], -1)]
     grads = listed(grads, True)
-
     share = chans // row_count
-    terms, give = filter_terms(after(where, half), slots, feats, grads, rows, share, col_count)
+    early = early_filter(after(slots, half), feats, grads[:known], rows, share)
+    terms, give = late_filter(where, slots, early, grads[known:], known, rows, share, col_count)
     filtered = give
     for level in range(levels):
         if level:

time: 111 us -> 108 us (0.973)
  waiting for transfers between devices: 19.9 us -> 17.3 us
  Pallas kernels: 44.5 us -> 46.3 us
  local copies, waits for them, and re-layouts: 6.07 us -> 4.58 us
    ppermute x5, waiting for transfers between devices: 5.21 us -> 3.11 us  [swap(): lax.ppermute(value, 'cols', [(i, i ^ 1 << level) for i in range(col_count)])]
    pallas_call x1 -> x2, Pallas kernels: 5.01 us -> 6.78 us  [the longest x1 3.93 us: early_filter(): pl.pallas_call(functools.partial(early_filter_kernel, rows, share), out_s...]
    unnamed x49 -> x47, local copies, waits for them, and re-layouts: 4.15 us -> 2.66 us
  transfers between devices with their start and end apart: 25 -> 25, of which waited for: 9 -> 10; matrix products, arithmetic and copies ran while one was open for 4% -> 4% of each run, Pallas kernels for 39% -> 41%
where the time goes in v4:
time: 108 us; the launch traced here: 107 us
  Pallas kernels  46.3 us (43%)
  starting transfers between devices  35.2 us (33%)
  waiting for transfers between devices  17.3 us (16%)
  local copies, waits for them, and re-layouts  4.58 us (4%)
  other arithmetic  2.82 us (3%)
  between operations  1.28 us (1%)
    ppermute x16, starting transfers between devices, send(): return lax.ppermute(value, 'rows', hop)  23 us
    pallas_call x1, Pallas kernels, row_tree(): pl.pallas_call(functools.partial(row_tree_kernel, first, 1536, rows), out...  22.2 us
    ppermute x16, waiting for transfers between devices, send(): return lax.ppermute(value, 'rows', hop)  13.7 us
    pallas_call x2, Pallas kernels, merge(): pl.pallas_call(functools.partial(merge_kernel, 1152, len(others) == 2, sh...  10.4 us
    pallas_call x1, Pallas kernels, convolutions(): pl.pallas_call(functools.partial(conv_kernel, rows), out_shape=[block, bl...  5.21 us
    ppermute x2, starting transfers between devices, body(): beyond.append(lax.ppermute(parcel, 'rows', perm))  5.14 us
    ppermute x2, starting transfers between devices, body(): near = [lax.ppermute(last, 'cols', east), lax.ppermute(first, 'cols', west)]  4.32 us
    pallas_call x1, Pallas kernels, early_filter(): pl.pallas_call(functools.partial(early_filter_kernel, rows, share), out_s...  3.93 us
  transfers between devices with their start and end apart: 25, of which 10 were waited for; matrix products, arithmetic and copies ran while one was open for 4% of the time, Pallas kernels for 41%

profile of v4, /device:TPU:0, one launch (start us, length us, event | category | flops | bytes accessed | tf_op | source)
XLA Modules:
  0.0 107.5 jit_solution(2760149114576428124)
XLA Ops:
  0.6 1.7 %edges.1 = (bf16[16,512]{1,0:T(8,128)(2,1)}, bf16[16,512]{1,0:T(8,128)(2,1)}) custom-call(bf16[256,512]{1,0:T(8,128)(2,1)} %bitcast.31, bf16[256,512]{1,0:T(8,128)(2,1)} %bitcast.34), custom_call_target="tpu_custom_call" | custom-call | tf_op jit(solution)/shard_map/edges/pallas_call | solution.py:499
  2.3 1.3 %collective-permute-start.1 = (bf16[16,512]{1,0:T(8,128)(2,1)}, bf16[16,512]{1,0:T(8,128)(2,1)S(1)}, u32[]{:S(2)}, u32[]{:S(2)}) collective-permute-start(bf16[16,512]{1,0:T(8,128)(2,1)} %get-tuple-element.54), channel_id=1, source_target_pairs={{1,0},{2,1},{3,2},{5,4},{6,5},{7,6},{9,8},{10,9},{11,10},{13,12},{... | collective-permute-start | bytes 49160 | tf_op jit(solution)/shard_map/ppermute | solution.py:543
  3.6 3.0 %collective-permute-start = (bf16[16,512]{1,0:T(8,128)(2,1)}, bf16[16,512]{1,0:T(8,128)(2,1)S(1)}, u32[]{:S(2)}, u32[]{:S(2)}) collective-permute-start(bf16[16,512]{1,0:T(8,128)(2,1)} %get-tuple-element.53), channel_id=1, source_target_pairs={{0,1},{1,2},{2,3},{4,5},{5,6},{6,7},{8,9},{9,10},{10,11},{12,13},{... | collective-permute-start | bytes 49160 | tf_op jit(solution)/shard_map/ppermute | solution.py:543
  8.5 3.1 %collective-permute-start.2 = (bf16[336,512]{1,0:T(8,128)(2,1)S(1)}, bf16[336,512]{1,0:T(8,128)(2,1)S(1)}, u32[]{:S(2)}, u32[]{:S(2)}) collective-permute-start(bf16[336,512]{1,0:T(8,128)(2,1)S(1)} %maximum_dynamic-update-slice_fusion.refs_0_), channel_id=1, source_target_pairs={{0,8},{8,16},{16,24},{24,28},{28,20},{20,12},{12,4},{4,0},{1,9},{9... | collective-permute-start | bytes 1032200 | tf_op jit(solution)/shard_map/ppermute | solution.py:539
  12.4 7.5 %collective-permute-done.2.refs_1_ = bf16[336,512]{1,0:T(8,128)(2,1)S(1)} collective-permute-done((bf16[336,512]{1,0:T(8,128)(2,1)S(1)}, bf16[336,512]{1,0:T(8,128)(2,1)S(1)}, u32[]{:S(2)}, u32[]{:S(2)}) %collective-permute-start.2) | collective-permute-done | bytes 344096 | tf_op jit(solution)/shard_map/ppermute | solution.py:539
  19.9 2.5 %collective-permute-start.3 = (bf16[336,512]{1,0:T(8,128)(2,1)S(1)}, bf16[336,512]{1,0:T(8,128)(2,1)S(1)}, u32[]{:S(2)}, u32[]{:S(2)}) collective-permute-start(bf16[336,512]{1,0:T(8,128)(2,1)S(1)} %collective-permute-done.2.refs_1_), channel_id=1, source_target_pairs={{0,8},{8,16},{16,24},{24,28},{28,20},{20,12},{12,4},{4,0},{1,9},{9... | collective-permute-start | bytes 1032200 | tf_op jit(solution)/shard_map/ppermute | solution.py:539
  22.5 3.8 %collective-permute-start.8 = (bf16[80,512]{1,0:T(8,128)(2,1)S(1)}, bf16[80,512]{1,0:T(8,128)(2,1)S(1)}, u32[]{:S(2)}, u32[]{:S(2)}) collective-permute-start(bf16[80,512]{1,0:T(8,128)(2,1)S(1)} %pad.16), channel_id=1, source_target_pairs={{0,4},{4,8},{8,12},{12,16},{16,20},{20,24},{24,28},{1,5},{5,9},{9,... | collective-permute-start | bytes 245768 | tf_op jit(solution)/shard_map/ppermute | solution.py:561
  26.4 1.3 %collective-permute-start.9 = (bf16[80,512]{1,0:T(8,128)(2,1)S(1)}, bf16[80,512]{1,0:T(8,128)(2,1)S(1)}, u32[]{:S(2)}, u32[]{:S(2)}) collective-permute-start(bf16[80,512]{1,0:T(8,128)(2,1)S(1)} %pad.17), channel_id=1, source_target_pairs={{4,0},{8,4},{12,8},{16,12},{20,16},{24,20},{28,24},{5,1},{9,5},{13... | collective-permute-start | bytes 245768 | tf_op jit(solution)/shard_map/ppermute | solution.py:561
  28.0 2.8 %collective-permute-done.3.refs_3_ = bf16[336,512]{1,0:T(8,128)(2,1)S(1)} collective-permute-done((bf16[336,512]{1,0:T(8,128)(2,1)S(1)}, bf16[336,512]{1,0:T(8,128)(2,1)S(1)}, u32[]{:S(2)}, u32[]{:S(2)}) %collective-permute-start.3) | collective-permute-done | bytes 344096 | tf_op jit(solution)/shard_map/ppermute | solution.py:539
  30.8 1.8 %collective-permute-start.4 = (bf16[336,512]{1,0:T(8,128)(2,1)S(1)}, bf16[336,512]{1,0:T(8,128)(2,1)S(1)}, u32[]{:S(2)}, u32[]{:S(2)}) collective-permute-start(bf16[336,512]{1,0:T(8,128)(2,1)S(1)} %collective-permute-done.3.refs_3_), channel_id=1, source_target_pairs={{0,8},{8,16},{16,24},{24,28},{28,20},{20,12},{12,4},{4,0},{1,9},{9... | collective-permute-start | bytes 1032200 | tf_op jit(solution)/shard_map/ppermute | solution.py:539
  35.5 5.2 %convolutions.1 = (bf16[256,512]{1,0:T(8,128)(2,1)}, bf16[256,512]{1,0:T(8,128)(2,1)}) custom-call(bf16[4608,512]{1,0:T(8,128)(2,1)} %kernel_ref.1, bf16[256,512]{1,0:T(8,128)(2,1)} %bitcast.33, bf16[256,512]{1,0:T(8,128)(2,1)} %bitcast.35, bf16[80,512]{1,0:T(8,128)(2,1)} %copy-done.21, bf16[80,512]{1,0:T(8,128)(2,1)} %copy-done.22, ...), custom_call_target="tpu_custom_call" | custom-call | flops 6000000000 | bytes 6291456 | tf_op jit(solution)/shard_map/convolutions/pallas_call | solution.py:349
  41.8 1.6 %collective-permute-start.10 = (bf16[160,512]{1,0:T(8,128)(2,1)S(1)}, bf16[160,512]{1,0:T(8,128)(2,1)S(1)}, u32[]{:S(2)}, u32[]{:S(2)}) collective-permute-start(bf16[160,512]{1,0:T(8,128)(2,1)S(1)} %slice.120), channel_id=1, source_target_pairs={{0,8},{8,16},{16,24},{24,28},{28,20},{20,12},{12,4},{4,0},{1,9},{9... | collective-permute-start | bytes 491528 | tf_op jit(solution)/shard_map/ppermute | solution.py:539
  44.0 1.8 %collective-permute-start.12 = (bf16[256,512]{1,0:T(8,128)(2,1)S(1)}, bf16[256,512]{1,0:T(8,128)(2,1)S(1)}, u32[]{:S(2)}, u32[]{:S(2)}) collective-permute-start(bf16[256,512]{1,0:T(8,128)(2,1)S(1)} %bitcast.37), channel_id=1, source_target_pairs={{0,4},{8,0},{16,8},{24,16},{28,24},{20,28},{12,20},{4,12},{1,5},{9... | collective-permute-start | bytes 786440 | tf_op jit(solution)/shard_map/ppermute | solution.py:539
  46.1 2.0 %collective-permute-start.14 = (bf16[256,512]{1,0:T(8,128)(2,1)S(1)}, bf16[256,512]{1,0:T(8,128)(2,1)S(1)}, u32[]{:S(2)}, u32[]{:S(2)}) collective-permute-start(bf16[256,512]{1,0:T(8,128)(2,1)S(1)} %bitcast.39), channel_id=1, source_target_pairs={{0,12},{8,4},{16,0},{24,8},{28,16},{20,24},{12,28},{4,20},{1,13},{... | collective-permute-start | bytes 786440 | tf_op jit(solution)/shard_map/ppermute | solution.py:539
  48.1 4.2 %collective-permute-start.15 = (bf16[256,512]{1,0:T(8,128)(2,1)S(1)}, bf16[256,512]{1,0:T(8,128)(2,1)}, u32[]{:S(2)}, u32[]{:S(2)}) collective-permute-start(bf16[256,512]{1,0:T(8,128)(2,1)S(1)} %bitcast.40), channel_id=1, source_target_pairs={{0,16},{8,24},{16,28},{24,20},{28,12},{20,4},{12,0},{4,8},{1,17},{... | collective-permute-start | bytes 786440 | tf_op jit(solution)/shard_map/ppermute | solution.py:539
  52.9 22.2 %row_tree.1.refs_0_ = bf16[128,4608]{1,0:T(8,128)(2,1)S(1)} custom-call(s32[8]{0:T(128)S(1)} %stack.52.rows_ref.slots_ref, bf16[128,256]{1,0:T(8,128)(2,1)S(1)} %get-tuple-element.82.mix_ref, bf16[336,512]{1,0:T(8,128)(2,1)} %copy-done.2, bf16[336,512]{1,0:T(8,128)(2,1)} %copy-done.10, bf16[336,512]{1,0:T(8,128)(2,1)} %copy-done.11, ...), custom_call_target="tpu_custom_call" | custom-call | flops 20000000000 | bytes 8388608 | tf_op jit(solution)/shard_map/row_tree/pallas_call | solution.py:185
  75.3 2.8 %collective-permute-start.17 = (bf16[256,512]{1,0:T(8,128)(2,1)}, bf16[256,512]{1,0:T(8,128)(2,1)S(1)}, u32[]{:S(2)}, u32[]{:S(2)}) collective-permute-start(bf16[256,512]{1,0:T(8,128)(2,1)} %collective-permute-done.15.refs_12_), channel_id=1, source_target_pairs={{0,8},{8,16},{16,24},{24,28},{28,20},{20,12},{12,4},{4,0},{1,9},{9... | collective-permute-start | bytes 786440 | tf_op jit(solution)/shard_map/ppermute | solution.py:539
  78.1 5.7 %merge.2 = (bf16[128,4608]{1,0:T(8,128)(2,1)}, bf16[128,2304]{1,0:T(8,128)(2,1)S(1)}) custom-call(s32[4]{0:T(128)S(1)} %constant_dynamic-update-slice_fusion.1.where_ref, bf16[128,256]{1,0:T(8,128)(2,1)S(1)} %get-tuple-element.83.mix_ref, bf16[128,4608]{1,0:T(8,128)(2,1)S(1)} %row_tree.1.refs_0_, bf16[128,4608]{1,0:T(8,128)(2,1)S(1)} %collective-permute-done.16.refs_1_), custom_call_target="tpu_custom_call" | custom-call | flops 4000000000 | bytes 4194304 | tf_op jit(solution)/shard_map/merge/pallas_call | solution.py:268
  85.1 1.4 %collective-permute-done.18.refs_1_ = bf16[256,512]{1,0:T(8,128)(2,1)S(1)} collective-permute-done((bf16[256,512]{1,0:T(8,128)(2,1)S(1)}, bf16[256,512]{1,0:T(8,128)(2,1)S(1)}, u32[]{:S(2)}, u32[]{:S(2)}) %collective-permute-start.18) | collective-permute-done | bytes 262176 | tf_op jit(solution)/shard_map/ppermute | solution.py:539
  86.5 1.4 %collective-permute-start.19 = (bf16[128,512]{1,0:T(8,128)(2,1)S(1)}, bf16[128,512]{1,0:T(8,128)(2,1)S(1)}, u32[]{:S(2)}, u32[]{:S(2)}) collective-permute-start(bf16[128,512]{1,0:T(8,128)(2,1)S(1)} %slice.122), channel_id=1, source_target_pairs={{0,8},{8,16},{16,24},{24,28},{28,20},{20,12},{12,4},{4,0},{1,9},{9... | collective-permute-start | bytes 393224 | tf_op jit(solution)/shard_map/ppermute | solution.py:539
  88.7 3.9 %early_filter.1 = (bf16[10,256,128]{2,1,0:T(8,128)(2,1)S(1)}, bf16[10,256,128]{2,1,0:T(8,128)(2,1)S(1)}, bf16[10,256,128]{2,1,0:T(8,128)(2,1)S(1)}, f32[9,128,512]{2,1,0:T(8,128)S(1)}) custom-call(s32[8]{0:T(128)S(1)} %stack.52.rows_ref.slots_ref, bf16[336,512]{1,0:T(8,128)(2,1)} %copy-done.2, bf16[336,512]{1,0:T(8,128)(2,1)} %copy-done.10, ...), custom_call_target="tpu_custom_call" | custom-call | flops 4000000000 | bytes 4194304 | tf_op jit(solution)/shard_map/early_filter/pallas_call | solution.py:417
  93.6 2.9 %late_filter.1 = (f32[2,9,64,128]{3,2,1,0:T(8,128)S(1)}, bf16[2,9,64,128]{3,2,1,0:T(8,128)(2,1)S(1)}) custom-call(s32[4]{0:T(128)S(1)} %pad_add_fusion.where_ref, s32[8]{0:T(128)S(1)} %stack.52.rows_ref.slots_ref, bf16[10,256,128]{2,1,0:T(8,128)(2,1)S(1)} %get-tuple-element.67.lo, bf16[10,256,128]{2,1,0:T(8,128)(2,1)S(1)} %get-tuple-element.68.raw, ...), custom_call_target="tpu_custom_call" | custom-call | flops 2000000000 | bytes 4194304 | tf_op jit(solution)/shard_map/late_filter/pallas_call | solution.py:462
  96.5 2.8 %collective-permute-done.23.refs_1_ = bf16[128,2304]{1,0:T(8,128)(2,1)S(1)} collective-permute-done((bf16[128,2304]{1,0:T(8,128)(2,1)S(1)}, bf16[128,2304]{1,0:T(8,128)(2,1)S(1)}, u32[]{:S(2)}, u32[]{:S(2)}) %collective-permute-start.23) | collective-permute-done | bytes 589856 | tf_op jit(solution)/shard_map/ppermute | solution.py:595
  101.7 4.7 %merge.3 = bf16[32,576]{1,0:T(8,128)(2,1)} custom-call(s32[4]{0:T(128)S(1)} %constant_dynamic-update-slice_fusion.where_ref, bf16[128,256]{1,0:T(8,128)(2,1)S(1)} %get-tuple-element.83.mix_ref, bf16[128,4608]{1,0:T(8,128)(2,1)S(1)} %copy-done, bf16[128,2304]{1,0:T(8,128)(2,1)S(1)} %collective-permute-done.23.refs_1_, ...), custom_call_target="tpu_custom_call" | custom-call | flops 4000000000 | bytes 4194304 | tf_op jit(solution)/shard_map/merge/pallas_call | solution.py:268
  (104 shorter events, 15.0 us)
Async XLA Ops:
  2.3 6.1 %collective-permute-start.1 = (bf16[16,512]{1,0:T(8,128)(2,1)}, bf16[16,512]{1,0:T(8,128)(2,1)S(1)}, u32[]{:S(2)}, u32[]{:S(2)}) collective-permute-start(bf16[16,512]{1,0:T(8,128)(2,1)} %get-tuple-element.54), channel_id=1, source_target_pairs={{1,0},{2,1},{3,2},{5,4},{6,5},{7,6},{9,8},{10,9},{11,10},{13,12},{... | collective-permute-start | bytes 49160 | tf_op jit(solution)/shard_map/ppermute | solution.py:543
  3.6 4.8 %collective-permute-start = (bf16[16,512]{1,0:T(8,128)(2,1)}, bf16[16,512]{1,0:T(8,128)(2,1)S(1)}, u32[]{:S(2)}, u32[]{:S(2)}) collective-permute-start(bf16[16,512]{1,0:T(8,128)(2,1)} %get-tuple-element.53), channel_id=1, source_target_pairs={{0,1},{1,2},{2,3},{4,5},{5,6},{6,7},{8,9},{9,10},{10,11},{12,13},{... | collective-permute-start | bytes 49160 | tf_op jit(solution)/shard_map/ppermute | solution.py:543
  8.5 11.4 %collective-permute-start.2 = (bf16[336,512]{1,0:T(8,128)(2,1)S(1)}, bf16[336,512]{1,0:T(8,128)(2,1)S(1)}, u32[]{:S(2)}, u32[]{:S(2)}) collective-permute-start(bf16[336,512]{1,0:T(8,128)(2,1)S(1)} %maximum_dynamic-update-slice_fusion.refs_0_), channel_id=1, source_target_pairs={{0,8},{8,16},{16,24},{24,28},{28,20},{20,12},{12,4},{4,0},{1,9},{9... | collective-permute-start | bytes 1032200 | tf_op jit(solution)/shard_map/ppermute | solution.py:539
  11.6 10.8 %collective-permute-start.5 = (bf16[336,512]{1,0:T(8,128)(2,1)S(1)}, bf16[336,512]{1,0:T(8,128)(2,1)S(1)}, u32[]{:S(2)}, u32[]{:S(2)}) collective-permute-start(bf16[336,512]{1,0:T(8,128)(2,1)S(1)} %maximum_dynamic-update-slice_fusion.refs_0_), channel_id=1, source_target_pairs={{0,4},{8,0},{16,8},{24,16},{28,24},{20,28},{12,20},{4,12},{1,5},{9... | collective-permute-start | bytes 1032200 | tf_op jit(solution)/shard_map/ppermute | solution.py:539
  19.9 10.9 %collective-permute-start.3 = (bf16[336,512]{1,0:T(8,128)(2,1)S(1)}, bf16[336,512]{1,0:T(8,128)(2,1)S(1)}, u32[]{:S(2)}, u32[]{:S(2)}) collective-permute-start(bf16[336,512]{1,0:T(8,128)(2,1)S(1)} %collective-permute-done.2.refs_1_), channel_id=1, source_target_pairs={{0,8},{8,16},{16,24},{24,28},{28,20},{20,12},{12,4},{4,0},{1,9},{9... | collective-permute-start | bytes 1032200 | tf_op jit(solution)/shard_map/ppermute | solution.py:539
  22.4 10.8 %collective-permute-start.6 = (bf16[336,512]{1,0:T(8,128)(2,1)S(1)}, bf16[336,512]{1,0:T(8,128)(2,1)S(1)}, u32[]{:S(2)}, u32[]{:S(2)}) collective-permute-start(bf16[336,512]{1,0:T(8,128)(2,1)S(1)} %collective-permute-done.5.refs_2_), channel_id=1, source_target_pairs={{0,4},{8,0},{16,8},{24,16},{28,24},{20,28},{12,20},{4,12},{1,5},{9... | collective-permute-start | bytes 1032200 | tf_op jit(solution)/shard_map/ppermute | solution.py:539
  22.5 11.7 %collective-permute-start.8 = (bf16[80,512]{1,0:T(8,128)(2,1)S(1)}, bf16[80,512]{1,0:T(8,128)(2,1)S(1)}, u32[]{:S(2)}, u32[]{:S(2)}) collective-permute-start(bf16[80,512]{1,0:T(8,128)(2,1)S(1)} %pad.16), channel_id=1, source_target_pairs={{0,4},{4,8},{8,12},{12,16},{16,20},{20,24},{24,28},{1,5},{5,9},{9,... | collective-permute-start | bytes 245768 | tf_op jit(solution)/shard_map/ppermute | solution.py:561
  26.4 7.8 %collective-permute-start.9 = (bf16[80,512]{1,0:T(8,128)(2,1)S(1)}, bf16[80,512]{1,0:T(8,128)(2,1)S(1)}, u32[]{:S(2)}, u32[]{:S(2)}) collective-permute-start(bf16[80,512]{1,0:T(8,128)(2,1)S(1)} %pad.17), channel_id=1, source_target_pairs={{4,0},{8,4},{12,8},{16,12},{20,16},{24,20},{28,24},{5,1},{9,5},{13... | collective-permute-start | bytes 245768 | tf_op jit(solution)/shard_map/ppermute | solution.py:561
  30.8 9.9 %collective-permute-start.4 = (bf16[336,512]{1,0:T(8,128)(2,1)S(1)}, bf16[336,512]{1,0:T(8,128)(2,1)S(1)}, u32[]{:S(2)}, u32[]{:S(2)}) collective-permute-start(bf16[336,512]{1,0:T(8,128)(2,1)S(1)} %collective-permute-done.3.refs_3_), channel_id=1, source_target_pairs={{0,8},{8,16},{16,24},{24,28},{28,20},{20,12},{12,4},{4,0},{1,9},{9... | collective-permute-start | bytes 1032200 | tf_op jit(solution)/shard_map/ppermute | solution.py:539
  33.3 8.5 %collective-permute-start.7 = (bf16[336,512]{1,0:T(8,128)(2,1)S(1)}, bf16[336,512]{1,0:T(8,128)(2,1)S(1)}, u32[]{:S(2)}, u32[]{:S(2)}) collective-permute-start(bf16[336,512]{1,0:T(8,128)(2,1)S(1)} %collective-permute-done.6.refs_4_), channel_id=1, source_target_pairs={{0,4},{8,0},{16,8},{24,16},{28,24},{20,28},{12,20},{4,12},{1,5},{9... | collective-permute-start | bytes 1032200 | tf_op jit(solution)/shard_map/ppermute | solution.py:539
  41.8 6.2 %collective-permute-start.10 = (bf16[160,512]{1,0:T(8,128)(2,1)S(1)}, bf16[160,512]{1,0:T(8,128)(2,1)S(1)}, u32[]{:S(2)}, u32[]{:S(2)}) collective-permute-start(bf16[160,512]{1,0:T(8,128)(2,1)S(1)} %slice.120), channel_id=1, source_target_pairs={{0,8},{8,16},{16,24},{24,28},{28,20},{20,12},{12,4},{4,0},{1,9},{9... | collective-permute-start | bytes 491528 | tf_op jit(solution)/shard_map/ppermute | solution.py:539
  43.5 8.7 %collective-permute-start.11 = (bf16[176,512]{1,0:T(8,128)(2,1)S(1)}, bf16[176,512]{1,0:T(8,128)(2,1)S(1)}, u32[]{:S(2)}, u32[]{:S(2)}) collective-permute-start(bf16[176,512]{1,0:T(8,128)(2,1)S(1)} %slice.121), channel_id=1, source_target_pairs={{0,4},{8,0},{16,8},{24,16},{28,24},{20,28},{12,20},{4,12},{1,5},{9... | collective-permute-start | bytes 540680 | tf_op jit(solution)/shard_map/ppermute | solution.py:539
  44.0 31.1 %collective-permute-start.12 = (bf16[256,512]{1,0:T(8,128)(2,1)S(1)}, bf16[256,512]{1,0:T(8,128)(2,1)S(1)}, u32[]{:S(2)}, u32[]{:S(2)}) collective-permute-start(bf16[256,512]{1,0:T(8,128)(2,1)S(1)} %bitcast.37), channel_id=1, source_target_pairs={{0,4},{8,0},{16,8},{24,16},{28,24},{20,28},{12,20},{4,12},{1,5},{9... | collective-permute-start | bytes 786440 | tf_op jit(solution)/shard_map/ppermute | solution.py:539
  45.8 29.3 %collective-permute-start.13 = (bf16[256,512]{1,0:T(8,128)(2,1)S(1)}, bf16[256,512]{1,0:T(8,128)(2,1)S(1)}, u32[]{:S(2)}, u32[]{:S(2)}) collective-permute-start(bf16[256,512]{1,0:T(8,128)(2,1)S(1)} %bitcast.38), channel_id=1, source_target_pairs={{0,8},{8,16},{16,24},{24,28},{28,20},{20,12},{12,4},{4,0},{1,9},{9... | collective-permute-start | bytes 786440 | tf_op jit(solution)/shard_map/ppermute | solution.py:539
  46.1 29.1 %collective-permute-start.14 = (bf16[256,512]{1,0:T(8,128)(2,1)S(1)}, bf16[256,512]{1,0:T(8,128)(2,1)S(1)}, u32[]{:S(2)}, u32[]{:S(2)}) collective-permute-start(bf16[256,512]{1,0:T(8,128)(2,1)S(1)} %bitcast.39), channel_id=1, source_target_pairs={{0,12},{8,4},{16,0},{24,8},{28,16},{20,24},{12,28},{4,20},{1,13},{... | collective-permute-start | bytes 786440 | tf_op jit(solution)/shard_map/ppermute | solution.py:539
  48.1 27.1 %collective-permute-start.15 = (bf16[256,512]{1,0:T(8,128)(2,1)S(1)}, bf16[256,512]{1,0:T(8,128)(2,1)}, u32[]{:S(2)}, u32[]{:S(2)}) collective-permute-start(bf16[256,512]{1,0:T(8,128)(2,1)S(1)} %bitcast.40), channel_id=1, source_target_pairs={{0,16},{8,24},{16,28},{24,20},{28,12},{20,4},{12,0},{4,8},{1,17},{... | collective-permute-start | bytes 786440 | tf_op jit(solution)/shard_map/ppermute | solution.py:539
  75.2 3.0 %collective-permute-start.16 = (bf16[128,4608]{1,0:T(8,128)(2,1)S(1)}, bf16[128,4608]{1,0:T(8,128)(2,1)S(1)}, u32[]{:S(2)}, u32[]{:S(2)}) collective-permute-start(bf16[128,4608]{1,0:T(8,128)(2,1)S(1)} %row_tree.1.refs_0_), channel_id=1, source_target_pairs={{0,1},{1,0},{2,3},{3,2},{4,5},{5,4},{6,7},{7,6},{8,9},{9,8},{10,11... | collective-permute-start | bytes 3538952 | tf_op jit(solution)/shard_map/ppermute | solution.py:595
  75.3 9.8 %collective-permute-start.17 = (bf16[256,512]{1,0:T(8,128)(2,1)}, bf16[256,512]{1,0:T(8,128)(2,1)S(1)}, u32[]{:S(2)}, u32[]{:S(2)}) collective-permute-start(bf16[256,512]{1,0:T(8,128)(2,1)} %collective-permute-done.15.refs_12_), channel_id=1, source_target_pairs={{0,8},{8,16},{16,24},{24,28},{28,20},{20,12},{12,4},{4,0},{1,9},{9... | collective-permute-start | bytes 786440 | tf_op jit(solution)/shard_map/ppermute | solution.py:539
  78.1 8.4 %collective-permute-start.18 = (bf16[256,512]{1,0:T(8,128)(2,1)S(1)}, bf16[256,512]{1,0:T(8,128)(2,1)S(1)}, u32[]{:S(2)}, u32[]{:S(2)}) collective-permute-start(bf16[256,512]{1,0:T(8,128)(2,1)S(1)} %collective-permute-done.14.refs_13_), channel_id=1, source_target_pairs={{0,4},{8,0},{16,8},{24,16},{28,24},{20,28},{12,20},{4,12},{1,5},{9... | collective-permute-start | bytes 786440 | tf_op jit(solution)/shard_map/ppermute | solution.py:539
  83.8 15.5 %collective-permute-start.23 = (bf16[128,2304]{1,0:T(8,128)(2,1)S(1)}, bf16[128,2304]{1,0:T(8,128)(2,1)S(1)}, u32[]{:S(2)}, u32[]{:S(2)}) collective-permute-start(bf16[128,2304]{1,0:T(8,128)(2,1)S(1)} %get-tuple-element.63), channel_id=1, source_target_pairs={{0,2},{1,3},{2,0},{3,1},{4,6},{5,7},{6,4},{7,5},{8,10},{9,11},{10,... | collective-permute-start | bytes 1769480 | tf_op jit(solution)/shard_map/ppermute | solution.py:595
  86.5 6.1 %collective-permute-start.19 = (bf16[128,512]{1,0:T(8,128)(2,1)S(1)}, bf16[128,512]{1,0:T(8,128)(2,1)S(1)}, u32[]{:S(2)}, u32[]{:S(2)}) collective-permute-start(bf16[128,512]{1,0:T(8,128)(2,1)S(1)} %slice.122), channel_id=1, source_target_pairs={{0,8},{8,16},{16,24},{24,28},{28,20},{20,12},{12,4},{4,0},{1,9},{9... | collective-permute-start | bytes 393224 | tf_op jit(solution)/shard_map/ppermute | solution.py:539
  87.9 5.0 %collective-permute-start.20 = (bf16[128,512]{1,0:T(8,128)(2,1)S(1)}, bf16[128,512]{1,0:T(8,128)(2,1)S(1)}, u32[]{:S(2)}, u32[]{:S(2)}) collective-permute-start(bf16[128,512]{1,0:T(8,128)(2,1)S(1)} %slice.123), channel_id=1, source_target_pairs={{0,4},{8,0},{16,8},{24,16},{28,24},{20,28},{12,20},{4,12},{1,5},{9... | collective-permute-start | bytes 393224 | tf_op jit(solution)/shard_map/ppermute | solution.py:539
  96.5 2.9 %collective-permute-start.21 = (bf16[2,9,64,128]{3,2,1,0:T(8,128)(2,1)S(1)}, bf16[2,9,64,128]{3,2,1,0:T(8,128)(2,1)}, u32[]{:S(2)}, u32[]{:S(2)}) collective-permute-start(bf16[2,9,64,128]{3,2,1,0:T(8,128)(2,1)S(1)} %get-tuple-element.74), channel_id=1, source_target_pairs={{0,1},{1,0},{2,3},{3,2},{4,5},{5,4},{6,7},{7,6},{8,9},{9,8},{10,11... | collective-permute-start | bytes 884744 | tf_op jit(solution)/shard_map/ppermute | solution.py:595
  100.4 6.3 %collective-permute-start.22 = (bf16[1,9,64,128]{3,2,1,0:T(8,128)(2,1)S(1)}, bf16[1,9,64,128]{3,2,1,0:T(8,128)(2,1)S(1)}, u32[]{:S(2)}, u32[]{:S(2)}) collective-permute-start(bf16[1,9,64,128]{3,2,1,0:T(8,128)(2,1)S(1)} %dynamic-slice_convert_fusion), channel_id=1, source_target_pairs={{0,2},{1,3},{2,0},{3,1},{4,6},{5,7},{6,4},{7,5},{8,10},{9,11},{10,... | collective-permute-start | bytes 442376 | tf_op jit(solution)/shard_map/ppermute | solution.py:595
  (24 other events, 248.9 us)

commit v5 on v4

--- a/solution.py
+++ b/solution.py
@@ -378,7 +378,7 @@
 
 
 def early_filter_kernel(rows, share, slots_ref, *refs):
-    *maps, lo, raw, hi, total, ends, grad, sems = refs
+    *maps, _, lo, raw, hi, total, ends, grad, sems = refs
     known = grad.shape[0]
     feats, grads = maps[:-known], maps[-known:]
     count = len(feats) - 1
@@ -409,11 +409,11 @@
         total[t] = functools.reduce(jnp.add, terms)
 
 
-def early_filter(slots, feats, grads, rows, share):
+def early_filter(slots, feats, grads, met, rows, share):
     pixels, chans = grads[0].shape
     count, lanes = len(feats) - 1, 128
     window = jax.ShapeDtypeStruct((count + 2, pixels, lanes), BF16)
-    inputs = feats + grads
+    inputs = feats + grads + [met]
     return pl.pallas_call(
         functools.partial(early_filter_kernel, rows, share),
         out_shape=[window] * 3 + [jax.ShapeDtypeStruct((9, lanes, chans), F32)],
@@ -570,7 +570,9 @@
     mid = size // 32 * 16
     feats[half_way] = [send(top[:mid], 1), send(bottom[mid:], -1)]
     grads = {0: own_grad}
-    late_grad = after(own_grad, top, bottom)
+    pairs = [(i, i ^ 1) for i in range(col_count)]
+    met = lax.ppermute(top[:16, :128], "cols", pairs)
+    late_grad, met, *_ = lax.optimization_barrier((own_grad, met, top, bottom))
     for d in (1, 2):
         grads[-d], grads[d] = send(late_grad, d), send(late_grad, -d)
 
@@ -609,7 +611,7 @@
     grads[half_way] = [send(top[:split], 1), send(bottom[split:], -1)]
     grads = listed(grads, True)
     share = chans // row_count
-    early = early_filter(after(slots, half), feats, grads[:known], rows, share)
+    early = early_filter(after(slots, half), feats, grads[:known], met, rows, share)
     terms, give = late_filter(where, slots, early, grads[known:], known, rows, share, col_count)
     filtered = give
     for level in range(levels):

time: 108 us -> 107 us (level)
  starting transfers between devices: 35.2 us -> 30.3 us
  waiting for transfers between devices: 17.3 us -> 20.8 us
    ppermute x16, starting transfers between devices: 23 us -> 19.9 us  [send(): return lax.ppermute(value, 'rows', hop)]
    ppermute x16, waiting for transfers between devices: 13.7 us -> 15.6 us  [send(): return lax.ppermute(value, 'rows', hop)]
    ppermute x5, starting transfers between devices: 2.72 us -> 0.94 us  [swap(): lax.ppermute(value, 'cols', [(i, i ^ 1 << level) for i in range(col_count)])]
    unnamed x47 -> x45, local copies, waits for them, and re-layouts: 2.66 us -> 2.66 us
  transfers between devices with their start and end apart: 25 -> 26, of which waited for: 10 -> 14; matrix products, arithmetic and copies ran while one was open for 4% -> 4% of each run, Pallas kernels for 41% -> 42%
where the time goes in v5:
time: 107 us; the launch traced here: 106 us
  Pallas kernels  46.5 us (43%)
  starting transfers between devices  30.3 us (28%)
  waiting for transfers between devices  20.8 us (19%)
  local copies, waits for them, and re-layouts  4.58 us (4%)
  other arithmetic  2.83 us (3%)
  between operations  1.33 us (1%)
    pallas_call x1, Pallas kernels, row_tree(): pl.pallas_call(functools.partial(row_tree_kernel, first, 1536, rows), out...  22.2 us
    ppermute x16, starting transfers between devices, send(): return lax.ppermute(value, 'rows', hop)  19.9 us
    ppermute x16, waiting for transfers between devices, send(): return lax.ppermute(value, 'rows', hop)  15.6 us
    pallas_call x2, Pallas kernels, merge(): pl.pallas_call(functools.partial(merge_kernel, 1152, len(others) == 2, sh...  10.4 us
    pallas_call x1, Pallas kernels, convolutions(): pl.pallas_call(functools.partial(conv_kernel, rows), out_shape=[block, bl...  5.22 us
    ppermute x2, starting transfers between devices, body(): beyond.append(lax.ppermute(parcel, 'rows', perm))  5.14 us
    ppermute x2, starting transfers between devices, body(): near = [lax.ppermute(last, 'cols', east), lax.ppermute(first, 'cols', west)]  4.32 us
    pallas_call x1, Pallas kernels, early_filter(): pl.pallas_call(functools.partial(early_filter_kernel, rows, share), out_s...  3.96 us
  transfers between devices with their start and end apart: 26, of which 14 were waited for; matrix products, arithmetic and copies ran while one was open for 4% of the time, Pallas kernels for 42%

profile of v5, /device:TPU:0, one launch (start us, length us, event | category | flops | bytes accessed | tf_op | source)
XLA Modules:
  0.0 106.3 jit_solution(7769537974147768641)
XLA Ops:
  0.6 1.7 %edges.1 = (bf16[16,512]{1,0:T(8,128)(2,1)}, bf16[16,512]{1,0:T(8,128)(2,1)}) custom-call(bf16[256,512]{1,0:T(8,128)(2,1)} %bitcast.31, bf16[256,512]{1,0:T(8,128)(2,1)} %bitcast.34), custom_call_target="tpu_custom_call" | custom-call | tf_op jit(solution)/shard_map/edges/pallas_call | solution.py:499
  2.3 1.3 %collective-permute-start.1 = (bf16[16,512]{1,0:T(8,128)(2,1)}, bf16[16,512]{1,0:T(8,128)(2,1)S(1)}, u32[]{:S(2)}, u32[]{:S(2)}) collective-permute-start(bf16[16,512]{1,0:T(8,128)(2,1)} %get-tuple-element.55), channel_id=1, source_target_pairs={{1,0},{2,1},{3,2},{5,4},{6,5},{7,6},{9,8},{10,9},{11,10},{13,12},{... | collective-permute-start | bytes 49160 | tf_op jit(solution)/shard_map/ppermute | solution.py:543
  3.6 3.0 %collective-permute-start = (bf16[16,512]{1,0:T(8,128)(2,1)}, bf16[16,512]{1,0:T(8,128)(2,1)S(1)}, u32[]{:S(2)}, u32[]{:S(2)}) collective-permute-start(bf16[16,512]{1,0:T(8,128)(2,1)} %get-tuple-element.54), channel_id=1, source_target_pairs={{0,1},{1,2},{2,3},{4,5},{5,6},{6,7},{8,9},{9,10},{10,11},{12,13},{... | collective-permute-start | bytes 49160 | tf_op jit(solution)/shard_map/ppermute | solution.py:543
  8.5 3.1 %collective-permute-start.2 = (bf16[336,512]{1,0:T(8,128)(2,1)S(1)}, bf16[336,512]{1,0:T(8,128)(2,1)S(1)}, u32[]{:S(2)}, u32[]{:S(2)}) collective-permute-start(bf16[336,512]{1,0:T(8,128)(2,1)S(1)} %maximum_dynamic-update-slice_fusion.refs_0_), channel_id=1, source_target_pairs={{0,8},{8,16},{16,24},{24,28},{28,20},{20,12},{12,4},{4,0},{1,9},{9... | collective-permute-start | bytes 1032200 | tf_op jit(solution)/shard_map/ppermute | solution.py:539
  12.4 7.5 %collective-permute-done.2.refs_1_ = bf16[336,512]{1,0:T(8,128)(2,1)S(1)} collective-permute-done((bf16[336,512]{1,0:T(8,128)(2,1)S(1)}, bf16[336,512]{1,0:T(8,128)(2,1)S(1)}, u32[]{:S(2)}, u32[]{:S(2)}) %collective-permute-start.2) | collective-permute-done | bytes 344096 | tf_op jit(solution)/shard_map/ppermute | solution.py:539
  19.9 2.5 %collective-permute-start.3 = (bf16[336,512]{1,0:T(8,128)(2,1)S(1)}, bf16[336,512]{1,0:T(8,128)(2,1)S(1)}, u32[]{:S(2)}, u32[]{:S(2)}) collective-permute-start(bf16[336,512]{1,0:T(8,128)(2,1)S(1)} %collective-permute-done.2.refs_1_), channel_id=1, source_target_pairs={{0,8},{8,16},{16,24},{24,28},{28,20},{20,12},{12,4},{4,0},{1,9},{9... | collective-permute-start | bytes 1032200 | tf_op jit(solution)/shard_map/ppermute | solution.py:539
  22.5 3.8 %collective-permute-start.8 = (bf16[80,512]{1,0:T(8,128)(2,1)S(1)}, bf16[80,512]{1,0:T(8,128)(2,1)S(1)}, u32[]{:S(2)}, u32[]{:S(2)}) collective-permute-start(bf16[80,512]{1,0:T(8,128)(2,1)S(1)} %pad.16), channel_id=1, source_target_pairs={{0,4},{4,8},{8,12},{12,16},{16,20},{20,24},{24,28},{1,5},{5,9},{9,... | collective-permute-start | bytes 245768 | tf_op jit(solution)/shard_map/ppermute | solution.py:561
  27.9 3.0 %collective-permute-done.3.refs_3_ = bf16[336,512]{1,0:T(8,128)(2,1)S(1)} collective-permute-done((bf16[336,512]{1,0:T(8,128)(2,1)S(1)}, bf16[336,512]{1,0:T(8,128)(2,1)S(1)}, u32[]{:S(2)}, u32[]{:S(2)}) %collective-permute-start.3) | collective-permute-done | bytes 344096 | tf_op jit(solution)/shard_map/ppermute | solution.py:539
  30.8 1.8 %collective-permute-start.4 = (bf16[336,512]{1,0:T(8,128)(2,1)S(1)}, bf16[336,512]{1,0:T(8,128)(2,1)S(1)}, u32[]{:S(2)}, u32[]{:S(2)}) collective-permute-start(bf16[336,512]{1,0:T(8,128)(2,1)S(1)} %collective-permute-done.3.refs_3_), channel_id=1, source_target_pairs={{0,8},{8,16},{16,24},{24,28},{28,20},{20,12},{12,4},{4,0},{1,9},{9... | collective-permute-start | bytes 1032200 | tf_op jit(solution)/shard_map/ppermute | solution.py:539
  35.4 5.2 %convolutions.1 = (bf16[256,512]{1,0:T(8,128)(2,1)}, bf16[256,512]{1,0:T(8,128)(2,1)}) custom-call(bf16[4608,512]{1,0:T(8,128)(2,1)} %kernel_ref.1, bf16[256,512]{1,0:T(8,128)(2,1)} %bitcast.33, bf16[256,512]{1,0:T(8,128)(2,1)} %bitcast.35, bf16[80,512]{1,0:T(8,128)(2,1)} %copy-done.19, bf16[80,512]{1,0:T(8,128)(2,1)} %copy-done.20, ...), custom_call_target="tpu_custom_call" | custom-call | flops 6000000000 | bytes 6291456 | tf_op jit(solution)/shard_map/convolutions/pallas_call | solution.py:349
  40.7 1.4 %collective-permute-done.7.refs_6_ = bf16[336,512]{1,0:T(8,128)(2,1)S(1)} collective-permute-done((bf16[336,512]{1,0:T(8,128)(2,1)}, bf16[336,512]{1,0:T(8,128)(2,1)S(1)}, u32[]{:S(2)}, u32[]{:S(2)}) %collective-permute-start.7) | collective-permute-done | bytes 344096 | tf_op jit(solution)/shard_map/ppermute | solution.py:539
  42.1 1.6 %collective-permute-start.10 = (bf16[160,512]{1,0:T(8,128)(2,1)S(1)}, bf16[160,512]{1,0:T(8,128)(2,1)S(1)}, u32[]{:S(2)}, u32[]{:S(2)}) collective-permute-start(bf16[160,512]{1,0:T(8,128)(2,1)S(1)} %slice.123), channel_id=1, source_target_pairs={{0,8},{8,16},{16,24},{24,28},{28,20},{20,12},{12,4},{4,0},{1,9},{9... | collective-permute-start | bytes 491528 | tf_op jit(solution)/shard_map/ppermute | solution.py:539
  45.5 1.5 %collective-permute-start.13 = (bf16[256,512]{1,0:T(8,128)(2,1)S(1)}, bf16[256,512]{1,0:T(8,128)(2,1)S(1)}, u32[]{:S(2)}, u32[]{:S(2)}) collective-permute-start(bf16[256,512]{1,0:T(8,128)(2,1)S(1)} %bitcast.37), channel_id=1, source_target_pairs={{0,4},{8,0},{16,8},{24,16},{28,24},{20,28},{12,20},{4,12},{1,5},{9... | collective-permute-start | bytes 786440 | tf_op jit(solution)/shard_map/ppermute | solution.py:539
  47.6 1.8 %collective-permute-start.15 = (bf16[256,512]{1,0:T(8,128)(2,1)S(1)}, bf16[256,512]{1,0:T(8,128)(2,1)}, u32[]{:S(2)}, u32[]{:S(2)}) collective-permute-start(bf16[256,512]{1,0:T(8,128)(2,1)S(1)} %bitcast.39), channel_id=1, source_target_pairs={{0,12},{8,4},{16,0},{24,8},{28,16},{20,24},{12,28},{4,20},{1,13},{... | collective-permute-start | bytes 786440 | tf_op jit(solution)/shard_map/ppermute | solution.py:539
  49.3 1.8 %collective-permute-start.16 = (bf16[256,512]{1,0:T(8,128)(2,1)S(1)}, bf16[256,512]{1,0:T(8,128)(2,1)}, u32[]{:S(2)}, u32[]{:S(2)}) collective-permute-start(bf16[256,512]{1,0:T(8,128)(2,1)S(1)} %bitcast.40), channel_id=1, source_target_pairs={{0,16},{8,24},{16,28},{24,20},{28,12},{20,4},{12,0},{4,8},{1,17},{... | collective-permute-start | bytes 786440 | tf_op jit(solution)/shard_map/ppermute | solution.py:539
  51.8 22.2 %row_tree.1.refs_0_ = bf16[128,4608]{1,0:T(8,128)(2,1)S(1)} custom-call(s32[8]{0:T(128)S(1)} %stack.52.rows_ref.slots_ref, bf16[128,256]{1,0:T(8,128)(2,1)S(1)} %get-tuple-element.84.mix_ref, bf16[336,512]{1,0:T(8,128)(2,1)} %copy-done.2, bf16[336,512]{1,0:T(8,128)(2,1)} %copy-done.10, bf16[336,512]{1,0:T(8,128)(2,1)} %copy-done.11, ...), custom_call_target="tpu_custom_call" | custom-call | flops 20000000000 | bytes 8388608 | tf_op jit(solution)/shard_map/row_tree/pallas_call | solution.py:185
  74.3 2.2 %collective-permute-start.18 = (bf16[256,512]{1,0:T(8,128)(2,1)}, bf16[256,512]{1,0:T(8,128)(2,1)S(1)}, u32[]{:S(2)}, u32[]{:S(2)}) collective-permute-start(bf16[256,512]{1,0:T(8,128)(2,1)} %collective-permute-done.16.refs_12_), channel_id=1, source_target_pairs={{0,8},{8,16},{16,24},{24,28},{28,20},{20,12},{12,4},{4,0},{1,9},{9... | collective-permute-start | bytes 786440 | tf_op jit(solution)/shard_map/ppermute | solution.py:539
  77.0 5.7 %merge.2 = (bf16[128,4608]{1,0:T(8,128)(2,1)}, bf16[128,2304]{1,0:T(8,128)(2,1)S(1)}) custom-call(s32[4]{0:T(128)S(1)} %constant_dynamic-update-slice_fusion.1.where_ref, bf16[128,256]{1,0:T(8,128)(2,1)S(1)} %get-tuple-element.85.mix_ref, bf16[128,4608]{1,0:T(8,128)(2,1)S(1)} %row_tree.1.refs_0_, bf16[128,4608]{1,0:T(8,128)(2,1)S(1)} %collective-permute-done.17.refs_1_), custom_call_target="tpu_custom_call" | custom-call | flops 4000000000 | bytes 4194304 | tf_op jit(solution)/shard_map/merge/pallas_call | solution.py:268
  83.2 2.1 %collective-permute-done.19.refs_1_ = bf16[256,512]{1,0:T(8,128)(2,1)S(1)} collective-permute-done((bf16[256,512]{1,0:T(8,128)(2,1)}, bf16[256,512]{1,0:T(8,128)(2,1)S(1)}, u32[]{:S(2)}, u32[]{:S(2)}) %collective-permute-start.19) | collective-permute-done | bytes 262176 | tf_op jit(solution)/shard_map/ppermute | solution.py:539
  85.3 1.8 %collective-permute-start.20 = (bf16[128,512]{1,0:T(8,128)(2,1)S(1)}, bf16[128,512]{1,0:T(8,128)(2,1)S(1)}, u32[]{:S(2)}, u32[]{:S(2)}) collective-permute-start(bf16[128,512]{1,0:T(8,128)(2,1)S(1)} %slice.126), channel_id=1, source_target_pairs={{0,8},{8,16},{16,24},{24,28},{28,20},{20,12},{12,4},{4,0},{1,9},{9... | collective-permute-start | bytes 393224 | tf_op jit(solution)/shard_map/ppermute | solution.py:539
  87.5 4.0 %early_filter.1 = (bf16[10,256,128]{2,1,0:T(8,128)(2,1)S(1)}, bf16[10,256,128]{2,1,0:T(8,128)(2,1)S(1)}, bf16[10,256,128]{2,1,0:T(8,128)(2,1)S(1)}, f32[9,128,512]{2,1,0:T(8,128)S(1)}) custom-call(s32[8]{0:T(128)S(1)} %stack.52.rows_ref.slots_ref, bf16[336,512]{1,0:T(8,128)(2,1)} %copy-done.2, bf16[336,512]{1,0:T(8,128)(2,1)} %copy-done.10, ...), custom_call_target="tpu_custom_call" | custom-call | flops 4000000000 | bytes 4194304 | tf_op jit(solution)/shard_map/early_filter/pallas_call | solution.py:417
  92.8 3.0 %late_filter.1 = (f32[2,9,64,128]{3,2,1,0:T(8,128)S(1)}, bf16[2,9,64,128]{3,2,1,0:T(8,128)(2,1)S(1)}) custom-call(s32[4]{0:T(128)S(1)} %pad_add_fusion.where_ref, s32[8]{0:T(128)S(1)} %stack.52.rows_ref.slots_ref, bf16[10,256,128]{2,1,0:T(8,128)(2,1)S(1)} %get-tuple-element.69.lo, bf16[10,256,128]{2,1,0:T(8,128)(2,1)S(1)} %get-tuple-element.70.raw, ...), custom_call_target="tpu_custom_call" | custom-call | flops 2000000000 | bytes 4194304 | tf_op jit(solution)/shard_map/late_filter/pallas_call | solution.py:462
  95.9 2.2 %collective-permute-done.24.refs_1_ = bf16[128,2304]{1,0:T(8,128)(2,1)S(1)} collective-permute-done((bf16[128,2304]{1,0:T(8,128)(2,1)S(1)}, bf16[128,2304]{1,0:T(8,128)(2,1)S(1)}, u32[]{:S(2)}, u32[]{:S(2)}) %collective-permute-start.24) | collective-permute-done | bytes 589856 | tf_op jit(solution)/shard_map/ppermute | solution.py:597
  100.1 4.7 %merge.3 = bf16[32,576]{1,0:T(8,128)(2,1)} custom-call(s32[4]{0:T(128)S(1)} %constant_dynamic-update-slice_fusion.where_ref, bf16[128,256]{1,0:T(8,128)(2,1)S(1)} %get-tuple-element.85.mix_ref, bf16[128,4608]{1,0:T(8,128)(2,1)S(1)} %copy-done, bf16[128,2304]{1,0:T(8,128)(2,1)S(1)} %collective-permute-done.24.refs_1_, ...), custom_call_target="tpu_custom_call" | custom-call | flops 4000000000 | bytes 4194304 | tf_op jit(solution)/shard_map/merge/pallas_call | solution.py:268
  (105 shorter events, 16.2 us)
Async XLA Ops:
  2.3 6.1 %collective-permute-start.1 = (bf16[16,512]{1,0:T(8,128)(2,1)}, bf16[16,512]{1,0:T(8,128)(2,1)S(1)}, u32[]{:S(2)}, u32[]{:S(2)}) collective-permute-start(bf16[16,512]{1,0:T(8,128)(2,1)} %get-tuple-element.55), channel_id=1, source_target_pairs={{1,0},{2,1},{3,2},{5,4},{6,5},{7,6},{9,8},{10,9},{11,10},{13,12},{... | collective-permute-start | bytes 49160 | tf_op jit(solution)/shard_map/ppermute | solution.py:543
  3.6 4.8 %collective-permute-start = (bf16[16,512]{1,0:T(8,128)(2,1)}, bf16[16,512]{1,0:T(8,128)(2,1)S(1)}, u32[]{:S(2)}, u32[]{:S(2)}) collective-permute-start(bf16[16,512]{1,0:T(8,128)(2,1)} %get-tuple-element.54), channel_id=1, source_target_pairs={{0,1},{1,2},{2,3},{4,5},{5,6},{6,7},{8,9},{9,10},{10,11},{12,13},{... | collective-permute-start | bytes 49160 | tf_op jit(solution)/shard_map/ppermute | solution.py:543
  8.5 11.4 %collective-permute-start.2 = (bf16[336,512]{1,0:T(8,128)(2,1)S(1)}, bf16[336,512]{1,0:T(8,128)(2,1)S(1)}, u32[]{:S(2)}, u32[]{:S(2)}) collective-permute-start(bf16[336,512]{1,0:T(8,128)(2,1)S(1)} %maximum_dynamic-update-slice_fusion.refs_0_), channel_id=1, source_target_pairs={{0,8},{8,16},{16,24},{24,28},{28,20},{20,12},{12,4},{4,0},{1,9},{9... | collective-permute-start | bytes 1032200 | tf_op jit(solution)/shard_map/ppermute | solution.py:539
  11.6 10.8 %collective-permute-start.5 = (bf16[336,512]{1,0:T(8,128)(2,1)S(1)}, bf16[336,512]{1,0:T(8,128)(2,1)S(1)}, u32[]{:S(2)}, u32[]{:S(2)}) collective-permute-start(bf16[336,512]{1,0:T(8,128)(2,1)S(1)} %maximum_dynamic-update-slice_fusion.refs_0_), channel_id=1, source_target_pairs={{0,4},{8,0},{16,8},{24,16},{28,24},{20,28},{12,20},{4,12},{1,5},{9... | collective-permute-start | bytes 1032200 | tf_op jit(solution)/shard_map/ppermute | solution.py:539
  19.9 10.9 %collective-permute-start.3 = (bf16[336,512]{1,0:T(8,128)(2,1)S(1)}, bf16[336,512]{1,0:T(8,128)(2,1)S(1)}, u32[]{:S(2)}, u32[]{:S(2)}) collective-permute-start(bf16[336,512]{1,0:T(8,128)(2,1)S(1)} %collective-permute-done.2.refs_1_), channel_id=1, source_target_pairs={{0,8},{8,16},{16,24},{24,28},{28,20},{20,12},{12,4},{4,0},{1,9},{9... | collective-permute-start | bytes 1032200 | tf_op jit(solution)/shard_map/ppermute | solution.py:539
  22.4 11.0 %collective-permute-start.6 = (bf16[336,512]{1,0:T(8,128)(2,1)S(1)}, bf16[336,512]{1,0:T(8,128)(2,1)}, u32[]{:S(2)}, u32[]{:S(2)}) collective-permute-start(bf16[336,512]{1,0:T(8,128)(2,1)S(1)} %collective-permute-done.5.refs_2_), channel_id=1, source_target_pairs={{0,4},{8,0},{16,8},{24,16},{28,24},{20,28},{12,20},{4,12},{1,5},{9... | collective-permute-start | bytes 1032200 | tf_op jit(solution)/shard_map/ppermute | solution.py:539
  22.5 11.6 %collective-permute-start.8 = (bf16[80,512]{1,0:T(8,128)(2,1)S(1)}, bf16[80,512]{1,0:T(8,128)(2,1)S(1)}, u32[]{:S(2)}, u32[]{:S(2)}) collective-permute-start(bf16[80,512]{1,0:T(8,128)(2,1)S(1)} %pad.16), channel_id=1, source_target_pairs={{0,4},{4,8},{8,12},{12,16},{16,20},{20,24},{24,28},{1,5},{5,9},{9,... | collective-permute-start | bytes 245768 | tf_op jit(solution)/shard_map/ppermute | solution.py:561
  26.4 7.7 %collective-permute-start.9 = (bf16[80,512]{1,0:T(8,128)(2,1)S(1)}, bf16[80,512]{1,0:T(8,128)(2,1)S(1)}, u32[]{:S(2)}, u32[]{:S(2)}) collective-permute-start(bf16[80,512]{1,0:T(8,128)(2,1)S(1)} %pad.17), channel_id=1, source_target_pairs={{4,0},{8,4},{12,8},{16,12},{20,16},{24,20},{28,24},{5,1},{9,5},{13... | collective-permute-start | bytes 245768 | tf_op jit(solution)/shard_map/ppermute | solution.py:561
  30.8 9.8 %collective-permute-start.4 = (bf16[336,512]{1,0:T(8,128)(2,1)S(1)}, bf16[336,512]{1,0:T(8,128)(2,1)S(1)}, u32[]{:S(2)}, u32[]{:S(2)}) collective-permute-start(bf16[336,512]{1,0:T(8,128)(2,1)S(1)} %collective-permute-done.3.refs_3_), channel_id=1, source_target_pairs={{0,8},{8,16},{16,24},{24,28},{28,20},{20,12},{12,4},{4,0},{1,9},{9... | collective-permute-start | bytes 1032200 | tf_op jit(solution)/shard_map/ppermute | solution.py:539
  33.4 8.7 %collective-permute-start.7 = (bf16[336,512]{1,0:T(8,128)(2,1)}, bf16[336,512]{1,0:T(8,128)(2,1)S(1)}, u32[]{:S(2)}, u32[]{:S(2)}) collective-permute-start(bf16[336,512]{1,0:T(8,128)(2,1)} %collective-permute-done.6.refs_4_), channel_id=1, source_target_pairs={{0,4},{8,0},{16,8},{24,16},{28,24},{20,28},{12,20},{4,12},{1,5},{9... | collective-permute-start | bytes 1032200 | tf_op jit(solution)/shard_map/ppermute | solution.py:539
  42.1 7.2 %collective-permute-start.10 = (bf16[160,512]{1,0:T(8,128)(2,1)S(1)}, bf16[160,512]{1,0:T(8,128)(2,1)S(1)}, u32[]{:S(2)}, u32[]{:S(2)}) collective-permute-start(bf16[160,512]{1,0:T(8,128)(2,1)S(1)} %slice.123), channel_id=1, source_target_pairs={{0,8},{8,16},{16,24},{24,28},{28,20},{20,12},{12,4},{4,0},{1,9},{9... | collective-permute-start | bytes 491528 | tf_op jit(solution)/shard_map/ppermute | solution.py:539
  43.8 7.3 %collective-permute-start.11 = (bf16[176,512]{1,0:T(8,128)(2,1)S(1)}, bf16[176,512]{1,0:T(8,128)(2,1)S(1)}, u32[]{:S(2)}, u32[]{:S(2)}) collective-permute-start(bf16[176,512]{1,0:T(8,128)(2,1)S(1)} %slice.124), channel_id=1, source_target_pairs={{0,4},{8,0},{16,8},{24,16},{28,24},{20,28},{12,20},{4,12},{1,5},{9... | collective-permute-start | bytes 540680 | tf_op jit(solution)/shard_map/ppermute | solution.py:539
  45.5 28.5 %collective-permute-start.13 = (bf16[256,512]{1,0:T(8,128)(2,1)S(1)}, bf16[256,512]{1,0:T(8,128)(2,1)S(1)}, u32[]{:S(2)}, u32[]{:S(2)}) collective-permute-start(bf16[256,512]{1,0:T(8,128)(2,1)S(1)} %bitcast.37), channel_id=1, source_target_pairs={{0,4},{8,0},{16,8},{24,16},{28,24},{20,28},{12,20},{4,12},{1,5},{9... | collective-permute-start | bytes 786440 | tf_op jit(solution)/shard_map/ppermute | solution.py:539
  47.0 27.0 %collective-permute-start.14 = (bf16[256,512]{1,0:T(8,128)(2,1)S(1)}, bf16[256,512]{1,0:T(8,128)(2,1)S(1)}, u32[]{:S(2)}, u32[]{:S(2)}) collective-permute-start(bf16[256,512]{1,0:T(8,128)(2,1)S(1)} %bitcast.38), channel_id=1, source_target_pairs={{0,8},{8,16},{16,24},{24,28},{28,20},{20,12},{12,4},{4,0},{1,9},{9... | collective-permute-start | bytes 786440 | tf_op jit(solution)/shard_map/ppermute | solution.py:539
  47.6 26.5 %collective-permute-start.15 = (bf16[256,512]{1,0:T(8,128)(2,1)S(1)}, bf16[256,512]{1,0:T(8,128)(2,1)}, u32[]{:S(2)}, u32[]{:S(2)}) collective-permute-start(bf16[256,512]{1,0:T(8,128)(2,1)S(1)} %bitcast.39), channel_id=1, source_target_pairs={{0,12},{8,4},{16,0},{24,8},{28,16},{20,24},{12,28},{4,20},{1,13},{... | collective-permute-start | bytes 786440 | tf_op jit(solution)/shard_map/ppermute | solution.py:539
  49.3 24.7 %collective-permute-start.16 = (bf16[256,512]{1,0:T(8,128)(2,1)S(1)}, bf16[256,512]{1,0:T(8,128)(2,1)}, u32[]{:S(2)}, u32[]{:S(2)}) collective-permute-start(bf16[256,512]{1,0:T(8,128)(2,1)S(1)} %bitcast.40), channel_id=1, source_target_pairs={{0,16},{8,24},{16,28},{24,20},{28,12},{20,4},{12,0},{4,8},{1,17},{... | collective-permute-start | bytes 786440 | tf_op jit(solution)/shard_map/ppermute | solution.py:539
  74.1 2.9 %collective-permute-start.17 = (bf16[128,4608]{1,0:T(8,128)(2,1)S(1)}, bf16[128,4608]{1,0:T(8,128)(2,1)S(1)}, u32[]{:S(2)}, u32[]{:S(2)}) collective-permute-start(bf16[128,4608]{1,0:T(8,128)(2,1)S(1)} %row_tree.1.refs_0_), channel_id=1, source_target_pairs={{0,1},{1,0},{2,3},{3,2},{4,5},{5,4},{6,7},{7,6},{8,9},{9,8},{10,11... | collective-permute-start | bytes 3538952 | tf_op jit(solution)/shard_map/ppermute | solution.py:597
  74.3 8.9 %collective-permute-start.18 = (bf16[256,512]{1,0:T(8,128)(2,1)}, bf16[256,512]{1,0:T(8,128)(2,1)S(1)}, u32[]{:S(2)}, u32[]{:S(2)}) collective-permute-start(bf16[256,512]{1,0:T(8,128)(2,1)} %collective-permute-done.16.refs_12_), channel_id=1, source_target_pairs={{0,8},{8,16},{16,24},{24,28},{28,20},{20,12},{12,4},{4,0},{1,9},{9... | collective-permute-start | bytes 786440 | tf_op jit(solution)/shard_map/ppermute | solution.py:539
  76.5 8.8 %collective-permute-start.19 = (bf16[256,512]{1,0:T(8,128)(2,1)}, bf16[256,512]{1,0:T(8,128)(2,1)S(1)}, u32[]{:S(2)}, u32[]{:S(2)}) collective-permute-start(bf16[256,512]{1,0:T(8,128)(2,1)} %collective-permute-done.15.refs_13_), channel_id=1, source_target_pairs={{0,4},{8,0},{16,8},{24,16},{28,24},{20,28},{12,20},{4,12},{1,5},{9... | collective-permute-start | bytes 786440 | tf_op jit(solution)/shard_map/ppermute | solution.py:539
  82.7 15.4 %collective-permute-start.24 = (bf16[128,2304]{1,0:T(8,128)(2,1)S(1)}, bf16[128,2304]{1,0:T(8,128)(2,1)S(1)}, u32[]{:S(2)}, u32[]{:S(2)}) collective-permute-start(bf16[128,2304]{1,0:T(8,128)(2,1)S(1)} %get-tuple-element.64), channel_id=1, source_target_pairs={{0,2},{1,3},{2,0},{3,1},{4,6},{5,7},{6,4},{7,5},{8,10},{9,11},{10,... | collective-permute-start | bytes 1769480 | tf_op jit(solution)/shard_map/ppermute | solution.py:597
  85.3 6.1 %collective-permute-start.20 = (bf16[128,512]{1,0:T(8,128)(2,1)S(1)}, bf16[128,512]{1,0:T(8,128)(2,1)S(1)}, u32[]{:S(2)}, u32[]{:S(2)}) collective-permute-start(bf16[128,512]{1,0:T(8,128)(2,1)S(1)} %slice.126), channel_id=1, source_target_pairs={{0,8},{8,16},{16,24},{24,28},{28,20},{20,12},{12,4},{4,0},{1,9},{9... | collective-permute-start | bytes 393224 | tf_op jit(solution)/shard_map/ppermute | solution.py:539
  87.1 5.0 %collective-permute-start.21 = (bf16[128,512]{1,0:T(8,128)(2,1)S(1)}, bf16[128,512]{1,0:T(8,128)(2,1)S(1)}, u32[]{:S(2)}, u32[]{:S(2)}) collective-permute-start(bf16[128,512]{1,0:T(8,128)(2,1)S(1)} %slice.127), channel_id=1, source_target_pairs={{0,4},{8,0},{16,8},{24,16},{28,24},{20,28},{12,20},{4,12},{1,5},{9... | collective-permute-start | bytes 393224 | tf_op jit(solution)/shard_map/ppermute | solution.py:539
  95.8 2.3 %collective-permute-start.22 = (bf16[2,9,64,128]{3,2,1,0:T(8,128)(2,1)S(1)}, bf16[2,9,64,128]{3,2,1,0:T(8,128)(2,1)}, u32[]{:S(2)}, u32[]{:S(2)}) collective-permute-start(bf16[2,9,64,128]{3,2,1,0:T(8,128)(2,1)S(1)} %get-tuple-element.76), channel_id=1, source_target_pairs={{0,1},{1,0},{2,3},{3,2},{4,5},{5,4},{6,7},{7,6},{8,9},{9,8},{10,11... | collective-permute-start | bytes 884744 | tf_op jit(solution)/shard_map/ppermute | solution.py:597
  99.2 6.3 %collective-permute-start.23 = (bf16[1,9,64,128]{3,2,1,0:T(8,128)(2,1)S(1)}, bf16[1,9,64,128]{3,2,1,0:T(8,128)(2,1)S(1)}, u32[]{:S(2)}, u32[]{:S(2)}) collective-permute-start(bf16[1,9,64,128]{3,2,1,0:T(8,128)(2,1)S(1)} %dynamic-slice_convert_fusion), channel_id=1, source_target_pairs={{0,2},{1,3},{2,0},{3,1},{4,6},{5,7},{6,4},{7,5},{8,10},{9,11},{10,... | collective-permute-start | bytes 442376 | tf_op jit(solution)/shard_map/ppermute | solution.py:597
  (24 other events, 258.6 us)

commit v6 on v5

--- a/solution.py
+++ b/solution.py
@@ -185,7 +185,7 @@
     return pl.pallas_call(
         functools.partial(row_tree_kernel, first, 1536, rows),
         out_shape=jax.ShapeDtypeStruct((rank, width), BF16),
-        in_specs=[SMEM, VMEM] + [ANY] * len(feats),
+        in_specs=[SMEM, VMEM] + [ANY] * (len(feats) - 2) + [pl.BlockSpec(memory_space=pl.ANY)] * 2,
         out_specs=VMEM,
         scratch_shapes=[
             maps,
@@ -199,7 +199,7 @@
         compiler_params=pltpu.CompilerParams(vmem_limit_bytes=48 << 20),
         cost_estimate=pl.CostEstimate(flops=2 * 10**10, bytes_accessed=8 << 20, transcendentals=0),
         name="row_tree",
-    )(slots, mix, *placed(feats))
+    )(slots, mix, *placed(feats[:-2]), *feats[-2:])
 
 
 def own_columns(where_ref, own, others, mixed, out_ref):

time: 107 us -> 107 us (level)
    unnamed x45 -> x47, local copies, waits for them, and re-layouts: 2.66 us -> 2.76 us
where the time goes in v6:
time: 107 us; the launch traced here: 106 us
  Pallas kernels  46.5 us (43%)
  starting transfers between devices  30 us (28%)
  waiting for transfers between devices  20.8 us (19%)
  local copies, waits for them, and re-layouts  4.68 us (4%)
  other arithmetic  2.82 us (3%)
  between operations  1.31 us (1%)
    pallas_call x1, Pallas kernels, row_tree(): pl.pallas_call(functools.partial(row_tree_kernel, first, 1536, rows), out...  22.2 us
    ppermute x16, starting transfers between devices, send(): return lax.ppermute(value, 'rows', hop)  20 us
    ppermute x16, waiting for transfers between devices, send(): return lax.ppermute(value, 'rows', hop)  15.6 us
    pallas_call x2, Pallas kernels, merge(): pl.pallas_call(functools.partial(merge_kernel, 1152, len(others) == 2, sh...  10.4 us
    pallas_call x1, Pallas kernels, convolutions(): pl.pallas_call(functools.partial(conv_kernel, rows), out_shape=[block, bl...  5.21 us
    ppermute x2, starting transfers between devices, body(): beyond.append(lax.ppermute(parcel, 'rows', perm))  5.14 us
    ppermute x2, starting transfers between devices, body(): near = [lax.ppermute(last, 'cols', east), lax.ppermute(first, 'cols', west)]  4.32 us
    pallas_call x1, Pallas kernels, early_filter(): pl.pallas_call(functools.partial(early_filter_kernel, rows, share), out_s...  3.96 us
  transfers between devices with their start and end apart: 26, of which 14 were waited for; matrix products, arithmetic and copies ran while one was open for 4% of the time, Pallas kernels for 42%

profile of v6, /device:TPU:0, one launch (start us, length us, event | category | flops | bytes accessed | tf_op | source)
XLA Modules:
  0.0 106.1 jit_solution(11501914987219499750)
XLA Ops:
  0.6 1.7 %edges.1 = (bf16[16,512]{1,0:T(8,128)(2,1)}, bf16[16,512]{1,0:T(8,128)(2,1)}) custom-call(bf16[256,512]{1,0:T(8,128)(2,1)} %bitcast.31, bf16[256,512]{1,0:T(8,128)(2,1)} %bitcast.34), custom_call_target="tpu_custom_call" | custom-call | tf_op jit(solution)/shard_map/edges/pallas_call | solution.py:499
  2.3 1.3 %collective-permute-start.1 = (bf16[16,512]{1,0:T(8,128)(2,1)}, bf16[16,512]{1,0:T(8,128)(2,1)S(1)}, u32[]{:S(2)}, u32[]{:S(2)}) collective-permute-start(bf16[16,512]{1,0:T(8,128)(2,1)} %get-tuple-element.55), channel_id=1, source_target_pairs={{1,0},{2,1},{3,2},{5,4},{6,5},{7,6},{9,8},{10,9},{11,10},{13,12},{... | collective-permute-start | bytes 49160 | tf_op jit(solution)/shard_map/ppermute | solution.py:543
  3.6 3.0 %collective-permute-start = (bf16[16,512]{1,0:T(8,128)(2,1)}, bf16[16,512]{1,0:T(8,128)(2,1)S(1)}, u32[]{:S(2)}, u32[]{:S(2)}) collective-permute-start(bf16[16,512]{1,0:T(8,128)(2,1)} %get-tuple-element.54), channel_id=1, source_target_pairs={{0,1},{1,2},{2,3},{4,5},{5,6},{6,7},{8,9},{9,10},{10,11},{12,13},{... | collective-permute-start | bytes 49160 | tf_op jit(solution)/shard_map/ppermute | solution.py:543
  8.5 3.1 %collective-permute-start.2 = (bf16[336,512]{1,0:T(8,128)(2,1)S(1)}, bf16[336,512]{1,0:T(8,128)(2,1)S(1)}, u32[]{:S(2)}, u32[]{:S(2)}) collective-permute-start(bf16[336,512]{1,0:T(8,128)(2,1)S(1)} %maximum_dynamic-update-slice_fusion.refs_0_), channel_id=1, source_target_pairs={{0,8},{8,16},{16,24},{24,28},{28,20},{20,12},{12,4},{4,0},{1,9},{9... | collective-permute-start | bytes 1032200 | tf_op jit(solution)/shard_map/ppermute | solution.py:539
  12.4 7.5 %collective-permute-done.2.refs_1_ = bf16[336,512]{1,0:T(8,128)(2,1)S(1)} collective-permute-done((bf16[336,512]{1,0:T(8,128)(2,1)S(1)}, bf16[336,512]{1,0:T(8,128)(2,1)S(1)}, u32[]{:S(2)}, u32[]{:S(2)}) %collective-permute-start.2) | collective-permute-done | bytes 344096 | tf_op jit(solution)/shard_map/ppermute | solution.py:539
  19.9 2.5 %collective-permute-start.3 = (bf16[336,512]{1,0:T(8,128)(2,1)S(1)}, bf16[336,512]{1,0:T(8,128)(2,1)S(1)}, u32[]{:S(2)}, u32[]{:S(2)}) collective-permute-start(bf16[336,512]{1,0:T(8,128)(2,1)S(1)} %collective-permute-done.2.refs_1_), channel_id=1, source_target_pairs={{0,8},{8,16},{16,24},{24,28},{28,20},{20,12},{12,4},{4,0},{1,9},{9... | collective-permute-start | bytes 1032200 | tf_op jit(solution)/shard_map/ppermute | solution.py:539
  22.5 3.8 %collective-permute-start.8 = (bf16[80,512]{1,0:T(8,128)(2,1)S(1)}, bf16[80,512]{1,0:T(8,128)(2,1)S(1)}, u32[]{:S(2)}, u32[]{:S(2)}) collective-permute-start(bf16[80,512]{1,0:T(8,128)(2,1)S(1)} %pad.16), channel_id=1, source_target_pairs={{0,4},{4,8},{8,12},{12,16},{16,20},{20,24},{24,28},{1,5},{5,9},{9,... | collective-permute-start | bytes 245768 | tf_op jit(solution)/shard_map/ppermute | solution.py:561
  26.4 1.3 %collective-permute-start.9 = (bf16[80,512]{1,0:T(8,128)(2,1)S(1)}, bf16[80,512]{1,0:T(8,128)(2,1)S(1)}, u32[]{:S(2)}, u32[]{:S(2)}) collective-permute-start(bf16[80,512]{1,0:T(8,128)(2,1)S(1)} %pad.17), channel_id=1, source_target_pairs={{4,0},{8,4},{12,8},{16,12},{20,16},{24,20},{28,24},{5,1},{9,5},{13... | collective-permute-start | bytes 245768 | tf_op jit(solution)/shard_map/ppermute | solution.py:561
  27.9 3.0 %collective-permute-done.3.refs_3_ = bf16[336,512]{1,0:T(8,128)(2,1)S(1)} collective-permute-done((bf16[336,512]{1,0:T(8,128)(2,1)S(1)}, bf16[336,512]{1,0:T(8,128)(2,1)S(1)}, u32[]{:S(2)}, u32[]{:S(2)}) %collective-permute-start.3) | collective-permute-done | bytes 344096 | tf_op jit(solution)/shard_map/ppermute | solution.py:539
  30.8 1.8 %collective-permute-start.4 = (bf16[336,512]{1,0:T(8,128)(2,1)S(1)}, bf16[336,512]{1,0:T(8,128)(2,1)S(1)}, u32[]{:S(2)}, u32[]{:S(2)}) collective-permute-start(bf16[336,512]{1,0:T(8,128)(2,1)S(1)} %collective-permute-done.3.refs_3_), channel_id=1, source_target_pairs={{0,8},{8,16},{16,24},{24,28},{28,20},{20,12},{12,4},{4,0},{1,9},{9... | collective-permute-start | bytes 1032200 | tf_op jit(solution)/shard_map/ppermute | solution.py:539
  35.5 5.2 %convolutions.1 = (bf16[256,512]{1,0:T(8,128)(2,1)}, bf16[256,512]{1,0:T(8,128)(2,1)}) custom-call(bf16[4608,512]{1,0:T(8,128)(2,1)} %kernel_ref.1, bf16[256,512]{1,0:T(8,128)(2,1)} %bitcast.33, bf16[256,512]{1,0:T(8,128)(2,1)} %bitcast.35, bf16[80,512]{1,0:T(8,128)(2,1)} %copy-done.20, bf16[80,512]{1,0:T(8,128)(2,1)} %copy-done.21, ...), custom_call_target="tpu_custom_call" | custom-call | flops 6000000000 | bytes 6291456 | tf_op jit(solution)/shard_map/convolutions/pallas_call | solution.py:349
  41.9 1.6 %collective-permute-start.10 = (bf16[160,512]{1,0:T(8,128)(2,1)S(1)}, bf16[160,512]{1,0:T(8,128)(2,1)S(1)}, u32[]{:S(2)}, u32[]{:S(2)}) collective-permute-start(bf16[160,512]{1,0:T(8,128)(2,1)S(1)} %slice.123), channel_id=1, source_target_pairs={{0,8},{8,16},{16,24},{24,28},{28,20},{20,12},{12,4},{4,0},{1,9},{9... | collective-permute-start | bytes 491528 | tf_op jit(solution)/shard_map/ppermute | solution.py:539
  45.3 1.7 %collective-permute-start.13 = (bf16[256,512]{1,0:T(8,128)(2,1)S(1)}, bf16[256,512]{1,0:T(8,128)(2,1)S(1)}, u32[]{:S(2)}, u32[]{:S(2)}) collective-permute-start(bf16[256,512]{1,0:T(8,128)(2,1)S(1)} %bitcast.37), channel_id=1, source_target_pairs={{0,4},{8,0},{16,8},{24,16},{28,24},{20,28},{12,20},{4,12},{1,5},{9... | collective-permute-start | bytes 786440 | tf_op jit(solution)/shard_map/ppermute | solution.py:539
  47.3 1.9 %collective-permute-start.15 = (bf16[256,512]{1,0:T(8,128)(2,1)S(1)}, bf16[256,512]{1,0:T(8,128)(2,1)}, u32[]{:S(2)}, u32[]{:S(2)}) collective-permute-start(bf16[256,512]{1,0:T(8,128)(2,1)S(1)} %bitcast.39), channel_id=1, source_target_pairs={{0,12},{8,4},{16,0},{24,8},{28,16},{20,24},{12,28},{4,20},{1,13},{... | collective-permute-start | bytes 786440 | tf_op jit(solution)/shard_map/ppermute | solution.py:539
  49.2 1.7 %collective-permute-start.16 = (bf16[256,512]{1,0:T(8,128)(2,1)S(1)}, bf16[256,512]{1,0:T(8,128)(2,1)}, u32[]{:S(2)}, u32[]{:S(2)}) collective-permute-start(bf16[256,512]{1,0:T(8,128)(2,1)S(1)} %bitcast.40), channel_id=1, source_target_pairs={{0,16},{8,24},{16,28},{24,20},{28,12},{20,4},{12,0},{4,8},{1,17},{... | collective-permute-start | bytes 786440 | tf_op jit(solution)/shard_map/ppermute | solution.py:539
  50.9 22.2 %row_tree.1.refs_0_ = bf16[128,4608]{1,0:T(8,128)(2,1)S(1)} custom-call(s32[8]{0:T(128)S(1)} %stack.52.rows_ref.slots_ref, bf16[128,256]{1,0:T(8,128)(2,1)S(1)} %get-tuple-element.84.mix_ref, bf16[336,512]{1,0:T(8,128)(2,1)} %copy-done.4, bf16[336,512]{1,0:T(8,128)(2,1)} %copy-done.12, bf16[336,512]{1,0:T(8,128)(2,1)} %copy-done.13, ...), custom_call_target="tpu_custom_call" | custom-call | flops 20000000000 | bytes 8388608 | tf_op jit(solution)/shard_map/row_tree/pallas_call | solution.py:185
  74.1 2.2 %collective-permute-start.18 = (bf16[256,512]{1,0:T(8,128)(2,1)}, bf16[256,512]{1,0:T(8,128)(2,1)S(1)}, u32[]{:S(2)}, u32[]{:S(2)}) collective-permute-start(bf16[256,512]{1,0:T(8,128)(2,1)} %collective-permute-done.16.refs_12_), channel_id=1, source_target_pairs={{0,8},{8,16},{16,24},{24,28},{28,20},{20,12},{12,4},{4,0},{1,9},{9... | collective-permute-start | bytes 786440 | tf_op jit(solution)/shard_map/ppermute | solution.py:539
  76.8 5.7 %merge.2 = (bf16[128,4608]{1,0:T(8,128)(2,1)}, bf16[128,2304]{1,0:T(8,128)(2,1)S(1)}) custom-call(s32[4]{0:T(128)S(1)} %constant_dynamic-update-slice_fusion.1.where_ref, bf16[128,256]{1,0:T(8,128)(2,1)S(1)} %get-tuple-element.85.mix_ref, bf16[128,4608]{1,0:T(8,128)(2,1)S(1)} %row_tree.1.refs_0_, bf16[128,4608]{1,0:T(8,128)(2,1)S(1)} %collective-permute-done.17.refs_1_), custom_call_target="tpu_custom_call" | custom-call | flops 4000000000 | bytes 4194304 | tf_op jit(solution)/shard_map/merge/pallas_call | solution.py:268
  83.1 2.3 %collective-permute-done.19.refs_1_ = bf16[256,512]{1,0:T(8,128)(2,1)S(1)} collective-permute-done((bf16[256,512]{1,0:T(8,128)(2,1)}, bf16[256,512]{1,0:T(8,128)(2,1)S(1)}, u32[]{:S(2)}, u32[]{:S(2)}) %collective-permute-start.19) | collective-permute-done | bytes 262176 | tf_op jit(solution)/shard_map/ppermute | solution.py:539
  85.4 1.8 %collective-permute-start.20 = (bf16[128,512]{1,0:T(8,128)(2,1)S(1)}, bf16[128,512]{1,0:T(8,128)(2,1)S(1)}, u32[]{:S(2)}, u32[]{:S(2)}) collective-permute-start(bf16[128,512]{1,0:T(8,128)(2,1)S(1)} %slice.126), channel_id=1, source_target_pairs={{0,8},{8,16},{16,24},{24,28},{28,20},{20,12},{12,4},{4,0},{1,9},{9... | collective-permute-start | bytes 393224 | tf_op jit(solution)/shard_map/ppermute | solution.py:539
  87.5 4.0 %early_filter.1 = (bf16[10,256,128]{2,1,0:T(8,128)(2,1)S(1)}, bf16[10,256,128]{2,1,0:T(8,128)(2,1)S(1)}, bf16[10,256,128]{2,1,0:T(8,128)(2,1)S(1)}, f32[9,128,512]{2,1,0:T(8,128)S(1)}) custom-call(s32[8]{0:T(128)S(1)} %stack.52.rows_ref.slots_ref, bf16[336,512]{1,0:T(8,128)(2,1)} %copy-done.4, bf16[336,512]{1,0:T(8,128)(2,1)} %copy-done.12, ...), custom_call_target="tpu_custom_call" | custom-call | flops 4000000000 | bytes 4194304 | tf_op jit(solution)/shard_map/early_filter/pallas_call | solution.py:417
  92.9 3.0 %late_filter.1 = (f32[2,9,64,128]{3,2,1,0:T(8,128)S(1)}, bf16[2,9,64,128]{3,2,1,0:T(8,128)(2,1)S(1)}) custom-call(s32[4]{0:T(128)S(1)} %pad_add_fusion.where_ref, s32[8]{0:T(128)S(1)} %stack.52.rows_ref.slots_ref, bf16[10,256,128]{2,1,0:T(8,128)(2,1)S(1)} %get-tuple-element.69.lo, bf16[10,256,128]{2,1,0:T(8,128)(2,1)S(1)} %get-tuple-element.70.raw, ...), custom_call_target="tpu_custom_call" | custom-call | flops 2000000000 | bytes 4194304 | tf_op jit(solution)/shard_map/late_filter/pallas_call | solution.py:462
  95.9 2.0 %collective-permute-done.24.refs_1_ = bf16[128,2304]{1,0:T(8,128)(2,1)S(1)} collective-permute-done((bf16[128,2304]{1,0:T(8,128)(2,1)S(1)}, bf16[128,2304]{1,0:T(8,128)(2,1)S(1)}, u32[]{:S(2)}, u32[]{:S(2)}) %collective-permute-start.24) | collective-permute-done | bytes 589856 | tf_op jit(solution)/shard_map/ppermute | solution.py:597
  100.0 4.7 %merge.3 = bf16[32,576]{1,0:T(8,128)(2,1)} custom-call(s32[4]{0:T(128)S(1)} %constant_dynamic-update-slice_fusion.where_ref, bf16[128,256]{1,0:T(8,128)(2,1)S(1)} %get-tuple-element.85.mix_ref, bf16[128,4608]{1,0:T(8,128)(2,1)S(1)} %copy-done.2, bf16[128,2304]{1,0:T(8,128)(2,1)S(1)} %collective-permute-done.24.refs_1_, ...), custom_call_target="tpu_custom_call" | custom-call | flops 4000000000 | bytes 4194304 | tf_op jit(solution)/shard_map/merge/pallas_call | solution.py:268
  (107 shorter events, 15.8 us)
Async XLA Ops:
  2.3 6.1 %collective-permute-start.1 = (bf16[16,512]{1,0:T(8,128)(2,1)}, bf16[16,512]{1,0:T(8,128)(2,1)S(1)}, u32[]{:S(2)}, u32[]{:S(2)}) collective-permute-start(bf16[16,512]{1,0:T(8,128)(2,1)} %get-tuple-element.55), channel_id=1, source_target_pairs={{1,0},{2,1},{3,2},{5,4},{6,5},{7,6},{9,8},{10,9},{11,10},{13,12},{... | collective-permute-start | bytes 49160 | tf_op jit(solution)/shard_map/ppermute | solution.py:543
  3.6 4.8 %collective-permute-start = (bf16[16,512]{1,0:T(8,128)(2,1)}, bf16[16,512]{1,0:T(8,128)(2,1)S(1)}, u32[]{:S(2)}, u32[]{:S(2)}) collective-permute-start(bf16[16,512]{1,0:T(8,128)(2,1)} %get-tuple-element.54), channel_id=1, source_target_pairs={{0,1},{1,2},{2,3},{4,5},{5,6},{6,7},{8,9},{9,10},{10,11},{12,13},{... | collective-permute-start | bytes 49160 | tf_op jit(solution)/shard_map/ppermute | solution.py:543
  8.5 11.4 %collective-permute-start.2 = (bf16[336,512]{1,0:T(8,128)(2,1)S(1)}, bf16[336,512]{1,0:T(8,128)(2,1)S(1)}, u32[]{:S(2)}, u32[]{:S(2)}) collective-permute-start(bf16[336,512]{1,0:T(8,128)(2,1)S(1)} %maximum_dynamic-update-slice_fusion.refs_0_), channel_id=1, source_target_pairs={{0,8},{8,16},{16,24},{24,28},{28,20},{20,12},{12,4},{4,0},{1,9},{9... | collective-permute-start | bytes 1032200 | tf_op jit(solution)/shard_map/ppermute | solution.py:539
  11.6 10.8 %collective-permute-start.5 = (bf16[336,512]{1,0:T(8,128)(2,1)S(1)}, bf16[336,512]{1,0:T(8,128)(2,1)S(1)}, u32[]{:S(2)}, u32[]{:S(2)}) collective-permute-start(bf16[336,512]{1,0:T(8,128)(2,1)S(1)} %maximum_dynamic-update-slice_fusion.refs_0_), channel_id=1, source_target_pairs={{0,4},{8,0},{16,8},{24,16},{28,24},{20,28},{12,20},{4,12},{1,5},{9... | collective-permute-start | bytes 1032200 | tf_op jit(solution)/shard_map/ppermute | solution.py:539
  19.9 10.9 %collective-permute-start.3 = (bf16[336,512]{1,0:T(8,128)(2,1)S(1)}, bf16[336,512]{1,0:T(8,128)(2,1)S(1)}, u32[]{:S(2)}, u32[]{:S(2)}) collective-permute-start(bf16[336,512]{1,0:T(8,128)(2,1)S(1)} %collective-permute-done.2.refs_1_), channel_id=1, source_target_pairs={{0,8},{8,16},{16,24},{24,28},{28,20},{20,12},{12,4},{4,0},{1,9},{9... | collective-permute-start | bytes 1032200 | tf_op jit(solution)/shard_map/ppermute | solution.py:539
  22.4 10.8 %collective-permute-start.6 = (bf16[336,512]{1,0:T(8,128)(2,1)S(1)}, bf16[336,512]{1,0:T(8,128)(2,1)S(1)}, u32[]{:S(2)}, u32[]{:S(2)}) collective-permute-start(bf16[336,512]{1,0:T(8,128)(2,1)S(1)} %collective-permute-done.5.refs_2_), channel_id=1, source_target_pairs={{0,4},{8,0},{16,8},{24,16},{28,24},{20,28},{12,20},{4,12},{1,5},{9... | collective-permute-start | bytes 1032200 | tf_op jit(solution)/shard_map/ppermute | solution.py:539
  22.5 11.7 %collective-permute-start.8 = (bf16[80,512]{1,0:T(8,128)(2,1)S(1)}, bf16[80,512]{1,0:T(8,128)(2,1)S(1)}, u32[]{:S(2)}, u32[]{:S(2)}) collective-permute-start(bf16[80,512]{1,0:T(8,128)(2,1)S(1)} %pad.16), channel_id=1, source_target_pairs={{0,4},{4,8},{8,12},{12,16},{16,20},{20,24},{24,28},{1,5},{5,9},{9,... | collective-permute-start | bytes 245768 | tf_op jit(solution)/shard_map/ppermute | solution.py:561
  26.4 7.8 %collective-permute-start.9 = (bf16[80,512]{1,0:T(8,128)(2,1)S(1)}, bf16[80,512]{1,0:T(8,128)(2,1)S(1)}, u32[]{:S(2)}, u32[]{:S(2)}) collective-permute-start(bf16[80,512]{1,0:T(8,128)(2,1)S(1)} %pad.17), channel_id=1, source_target_pairs={{4,0},{8,4},{12,8},{16,12},{20,16},{24,20},{28,24},{5,1},{9,5},{13... | collective-permute-start | bytes 245768 | tf_op jit(solution)/shard_map/ppermute | solution.py:561
  30.8 9.9 %collective-permute-start.4 = (bf16[336,512]{1,0:T(8,128)(2,1)S(1)}, bf16[336,512]{1,0:T(8,128)(2,1)S(1)}, u32[]{:S(2)}, u32[]{:S(2)}) collective-permute-start(bf16[336,512]{1,0:T(8,128)(2,1)S(1)} %collective-permute-done.3.refs_3_), channel_id=1, source_target_pairs={{0,8},{8,16},{16,24},{24,28},{28,20},{20,12},{12,4},{4,0},{1,9},{9... | collective-permute-start | bytes 1032200 | tf_op jit(solution)/shard_map/ppermute | solution.py:539
  33.3 8.6 %collective-permute-start.7 = (bf16[336,512]{1,0:T(8,128)(2,1)S(1)}, bf16[336,512]{1,0:T(8,128)(2,1)S(1)}, u32[]{:S(2)}, u32[]{:S(2)}) collective-permute-start(bf16[336,512]{1,0:T(8,128)(2,1)S(1)} %collective-permute-done.6.refs_4_), channel_id=1, source_target_pairs={{0,4},{8,0},{16,8},{24,16},{28,24},{20,28},{12,20},{4,12},{1,5},{9... | collective-permute-start | bytes 1032200 | tf_op jit(solution)/shard_map/ppermute | solution.py:539
  41.9 7.4 %collective-permute-start.10 = (bf16[160,512]{1,0:T(8,128)(2,1)S(1)}, bf16[160,512]{1,0:T(8,128)(2,1)S(1)}, u32[]{:S(2)}, u32[]{:S(2)}) collective-permute-start(bf16[160,512]{1,0:T(8,128)(2,1)S(1)} %slice.123), channel_id=1, source_target_pairs={{0,8},{8,16},{16,24},{24,28},{28,20},{20,12},{12,4},{4,0},{1,9},{9... | collective-permute-start | bytes 491528 | tf_op jit(solution)/shard_map/ppermute | solution.py:539
  43.5 7.4 %collective-permute-start.11 = (bf16[176,512]{1,0:T(8,128)(2,1)S(1)}, bf16[176,512]{1,0:T(8,128)(2,1)S(1)}, u32[]{:S(2)}, u32[]{:S(2)}) collective-permute-start(bf16[176,512]{1,0:T(8,128)(2,1)S(1)} %slice.124), channel_id=1, source_target_pairs={{0,4},{8,0},{16,8},{24,16},{28,24},{20,28},{12,20},{4,12},{1,5},{9... | collective-permute-start | bytes 540680 | tf_op jit(solution)/shard_map/ppermute | solution.py:539
  45.3 27.9 %collective-permute-start.13 = (bf16[256,512]{1,0:T(8,128)(2,1)S(1)}, bf16[256,512]{1,0:T(8,128)(2,1)S(1)}, u32[]{:S(2)}, u32[]{:S(2)}) collective-permute-start(bf16[256,512]{1,0:T(8,128)(2,1)S(1)} %bitcast.37), channel_id=1, source_target_pairs={{0,4},{8,0},{16,8},{24,16},{28,24},{20,28},{12,20},{4,12},{1,5},{9... | collective-permute-start | bytes 786440 | tf_op jit(solution)/shard_map/ppermute | solution.py:539
  47.0 26.2 %collective-permute-start.14 = (bf16[256,512]{1,0:T(8,128)(2,1)S(1)}, bf16[256,512]{1,0:T(8,128)(2,1)S(1)}, u32[]{:S(2)}, u32[]{:S(2)}) collective-permute-start(bf16[256,512]{1,0:T(8,128)(2,1)S(1)} %bitcast.38), channel_id=1, source_target_pairs={{0,8},{8,16},{16,24},{24,28},{28,20},{20,12},{12,4},{4,0},{1,9},{9... | collective-permute-start | bytes 786440 | tf_op jit(solution)/shard_map/ppermute | solution.py:539
  47.3 25.9 %collective-permute-start.15 = (bf16[256,512]{1,0:T(8,128)(2,1)S(1)}, bf16[256,512]{1,0:T(8,128)(2,1)}, u32[]{:S(2)}, u32[]{:S(2)}) collective-permute-start(bf16[256,512]{1,0:T(8,128)(2,1)S(1)} %bitcast.39), channel_id=1, source_target_pairs={{0,12},{8,4},{16,0},{24,8},{28,16},{20,24},{12,28},{4,20},{1,13},{... | collective-permute-start | bytes 786440 | tf_op jit(solution)/shard_map/ppermute | solution.py:539
  49.2 24.8 %collective-permute-start.16 = (bf16[256,512]{1,0:T(8,128)(2,1)S(1)}, bf16[256,512]{1,0:T(8,128)(2,1)}, u32[]{:S(2)}, u32[]{:S(2)}) collective-permute-start(bf16[256,512]{1,0:T(8,128)(2,1)S(1)} %bitcast.40), channel_id=1, source_target_pairs={{0,16},{8,24},{16,28},{24,20},{28,12},{20,4},{12,0},{4,8},{1,17},{... | collective-permute-start | bytes 786440 | tf_op jit(solution)/shard_map/ppermute | solution.py:539
  74.0 2.8 %collective-permute-start.17 = (bf16[128,4608]{1,0:T(8,128)(2,1)S(1)}, bf16[128,4608]{1,0:T(8,128)(2,1)S(1)}, u32[]{:S(2)}, u32[]{:S(2)}) collective-permute-start(bf16[128,4608]{1,0:T(8,128)(2,1)S(1)} %row_tree.1.refs_0_), channel_id=1, source_target_pairs={{0,1},{1,0},{2,3},{3,2},{4,5},{5,4},{6,7},{7,6},{8,9},{9,8},{10,11... | collective-permute-start | bytes 3538952 | tf_op jit(solution)/shard_map/ppermute | solution.py:597
  74.1 9.0 %collective-permute-start.18 = (bf16[256,512]{1,0:T(8,128)(2,1)}, bf16[256,512]{1,0:T(8,128)(2,1)S(1)}, u32[]{:S(2)}, u32[]{:S(2)}) collective-permute-start(bf16[256,512]{1,0:T(8,128)(2,1)} %collective-permute-done.16.refs_12_), channel_id=1, source_target_pairs={{0,8},{8,16},{16,24},{24,28},{28,20},{20,12},{12,4},{4,0},{1,9},{9... | collective-permute-start | bytes 786440 | tf_op jit(solution)/shard_map/ppermute | solution.py:539
  76.3 9.0 %collective-permute-start.19 = (bf16[256,512]{1,0:T(8,128)(2,1)}, bf16[256,512]{1,0:T(8,128)(2,1)S(1)}, u32[]{:S(2)}, u32[]{:S(2)}) collective-permute-start(bf16[256,512]{1,0:T(8,128)(2,1)} %collective-permute-done.15.refs_13_), channel_id=1, source_target_pairs={{0,4},{8,0},{16,8},{24,16},{28,24},{20,28},{12,20},{4,12},{1,5},{9... | collective-permute-start | bytes 786440 | tf_op jit(solution)/shard_map/ppermute | solution.py:539
  82.5 15.4 %collective-permute-start.24 = (bf16[128,2304]{1,0:T(8,128)(2,1)S(1)}, bf16[128,2304]{1,0:T(8,128)(2,1)S(1)}, u32[]{:S(2)}, u32[]{:S(2)}) collective-permute-start(bf16[128,2304]{1,0:T(8,128)(2,1)S(1)} %get-tuple-element.64), channel_id=1, source_target_pairs={{0,2},{1,3},{2,0},{3,1},{4,6},{5,7},{6,4},{7,5},{8,10},{9,11},{10,... | collective-permute-start | bytes 1769480 | tf_op jit(solution)/shard_map/ppermute | solution.py:597
  85.4 6.1 %collective-permute-start.20 = (bf16[128,512]{1,0:T(8,128)(2,1)S(1)}, bf16[128,512]{1,0:T(8,128)(2,1)S(1)}, u32[]{:S(2)}, u32[]{:S(2)}) collective-permute-start(bf16[128,512]{1,0:T(8,128)(2,1)S(1)} %slice.126), channel_id=1, source_target_pairs={{0,8},{8,16},{16,24},{24,28},{28,20},{20,12},{12,4},{4,0},{1,9},{9... | collective-permute-start | bytes 393224 | tf_op jit(solution)/shard_map/ppermute | solution.py:539
  87.2 5.0 %collective-permute-start.21 = (bf16[128,512]{1,0:T(8,128)(2,1)S(1)}, bf16[128,512]{1,0:T(8,128)(2,1)S(1)}, u32[]{:S(2)}, u32[]{:S(2)}) collective-permute-start(bf16[128,512]{1,0:T(8,128)(2,1)S(1)} %slice.127), channel_id=1, source_target_pairs={{0,4},{8,0},{16,8},{24,16},{28,24},{20,28},{12,20},{4,12},{1,5},{9... | collective-permute-start | bytes 393224 | tf_op jit(solution)/shard_map/ppermute | solution.py:539
  95.9 2.1 %collective-permute-start.22 = (bf16[2,9,64,128]{3,2,1,0:T(8,128)(2,1)S(1)}, bf16[2,9,64,128]{3,2,1,0:T(8,128)(2,1)}, u32[]{:S(2)}, u32[]{:S(2)}) collective-permute-start(bf16[2,9,64,128]{3,2,1,0:T(8,128)(2,1)S(1)} %get-tuple-element.76), channel_id=1, source_target_pairs={{0,1},{1,0},{2,3},{3,2},{4,5},{5,4},{6,7},{7,6},{8,9},{9,8},{10,11... | collective-permute-start | bytes 884744 | tf_op jit(solution)/shard_map/ppermute | solution.py:597
  99.1 6.3 %collective-permute-start.23 = (bf16[1,9,64,128]{3,2,1,0:T(8,128)(2,1)S(1)}, bf16[1,9,64,128]{3,2,1,0:T(8,128)(2,1)S(1)}, u32[]{:S(2)}, u32[]{:S(2)}) collective-permute-start(bf16[1,9,64,128]{3,2,1,0:T(8,128)(2,1)S(1)} %dynamic-slice_convert_fusion), channel_id=1, source_target_pairs={{0,2},{1,3},{2,0},{3,1},{4,6},{5,7},{6,4},{7,5},{8,10},{9,11},{10,... | collective-permute-start | bytes 442376 | tf_op jit(solution)/shard_map/ppermute | solution.py:597
  (25 other events, 293.8 us)
